TPU v7x, 32 devices: a whole 2x2x4 slice. The times are simulated.
32 devices in a mesh: img: 16 (over z, y, core), ori: 2 (over x).
Axes of the slice: x: 2, y: 2, z: 4, core: 2. Of those that a mesh axis runs over, the one named last changes fastest.
Arguments:
- images: float32 [4096, 2048], P(('img', 'ori')), may hold values from -40 to 40
- precision: float32 [4096], P('img'), may hold values from 0.5 to 2
- projections: bfloat16 [8192, 2048], P('ori'), may hold values from -1 to 1
- tile_mask: int32 [32, 64], P('img', 'ori'), may hold values from 0 to 1, as said below
Outputs:
- posteriors: bfloat16 [4096, 8192], P('img', 'ori')
- references: float32 [8192, 2048], P(('ori', 'img'))
Inputs may be any that keep to these rules, and one draw needn't show every extreme that they name: `tile_mask`: every image block has at least one live tile.
All inputs are finite; a program needn't handle non-finite values.
Results may differ from a plain program's by a relative error of at most 0.0095.
Values may be sent and summed in bfloat16 or wider, within the bound.
No kernel may reach another device: no remote copies, remote signals or barrier semaphores. Data moves between devices by JAX's collectives and lax.ppermute only.
A program may use at most 128 MiB of HBM per device.

v0:
```python
import jax
import jax.numpy as jnp
from jax import lax
from jax.sharding import PartitionSpec as P

prior_weight = 1.0
very_low = -1e30


def weighted_sums(weights, rows_block):
    return lax.dot_general(
        weights, rows_block, (((0,), (0,)), ((), ())), preferred_element_type=jnp.float32
    )


def body(images, precision, projections, tile_mask):
    lowered = images.astype(jnp.bfloat16)
    grouped = lax.all_gather(lowered, "ori", axis=0, tiled=True)
    proj_float = projections.astype(jnp.float32)
    squared = jnp.sum(proj_float * proj_float, axis=1)
    blocks, tiles_here = tile_mask.shape
    per_block = grouped.shape[0] // blocks
    tile_width = projections.shape[0] // tiles_here
    columns = grouped.shape[1]
    products = lax.dot_general(
        grouped, projections, (((1,), (1,)), ((), ())), preferred_element_type=jnp.float32
    )
    scores = precision[:, None] * (products - 0.5 * squared[None, :])
    shaped = scores.reshape(blocks, per_block, tiles_here, tile_width)
    alive = jnp.broadcast_to((tile_mask > 0)[:, None, :, None], shaped.shape)
    masked = jnp.where(alive, shaped, very_low)
    local_high = jnp.max(masked, axis=(2, 3))
    row_high = lax.pmax(local_high, "ori")
    local_total = jnp.sum(
        jnp.where(alive, jnp.exp(masked - row_high[:, :, None, None]), 0.0), axis=(2, 3)
    )
    row_total = lax.psum(local_total, "ori")
    probable = (
        jnp.where(alive, jnp.exp(masked - row_high[:, :, None, None]), 0.0)
        / row_total[:, :, None, None]
    )
    posteriors = probable.reshape(scores.shape).astype(jnp.bfloat16)
    counts = jnp.sum(posteriors.astype(jnp.float32), axis=0)
    half_width = columns // 2
    left_sums, totals = (
        lax.psum_scatter(
            weighted_sums(posteriors, grouped[:, :half_width]).astype(jnp.bfloat16),
            "img",
            scatter_dimension=0,
            tiled=True,
        ).astype(jnp.float32),
        lax.psum_scatter(
            counts.astype(jnp.bfloat16), "img", scatter_dimension=0, tiled=True
        ).astype(jnp.float32),
    )
    right_sums = lax.psum_scatter(
        weighted_sums(posteriors, grouped[:, half_width:]).astype(jnp.bfloat16),
        "img",
        scatter_dimension=0,
        tiled=True,
    ).astype(jnp.float32)
    summed = jnp.concatenate([left_sums, right_sums], axis=1)
    rows_here = summed.shape[0]
    first_row = lax.axis_index("img") * rows_here
    prior_rows = lax.dynamic_slice_in_dim(proj_float, first_row, rows_here, 0)
    refined = (summed + prior_weight * prior_rows) / (totals[:, None] + prior_weight)
    return (posteriors, refined)


def solution(mesh):
    return jax.shard_map(
        body,
        mesh=mesh,
        in_specs=(P(("img", "ori"), None), P("img"), P("ori", None), P("img", "ori")),
        out_specs=(P("img", "ori"), P(("ori", "img"), None)),
        check_vma=False,
    )
```

profile of v0, /device:TPU:0, one launch (start us, length us, event | category | flops | bytes accessed | tf_op | source)
XLA Modules:
  0.0 294.3 jit_solution(2245869548018482485)
XLA Ops:
  7.2 0.0 all-gather.2.cloned.1.call-start
  7.2 2.1 convert_element_type.22
  9.3 0.0 all-gather.2.cloned.1.call-update
  9.3 0.0 reduce-scatter.5.cloned.1.call-start
  9.4 0.7 broadcast_compare_fusion
  10.1 0.0 copy-start.3
  10.1 7.2 %multiply_reduce_fusion = f32[4096]{0:T(1024)S(1)} fusion(bf16[4096,2048]{1,0:T(8,128)(2,1)} %param.6), kind=kLoop, calls=%fused_computation | loop fusion | flops 25161728 | bytes 16793600 | tf_op jit(solution)/shard_map/reduce_sum | solution.py:20
  17.3 16.9 %all-gather.2.cloned.1.call-done = bf16[256,2048]{1,0:T(8,128)(2,1)} async-done(((bf16[128,2048]{1,0:T(8,128)(2,1)}), bf16[256,2048]{1,0:T(8,128)(2,1)}) %all-gather.2.cloned.1.call-update) | async-done | bytes 1048592 | tf_op jit(solution)/shard_map/all_gather | solution.py:18
  34.2 0.3 broadcast_in_dim.22
  34.5 0.0 copy-done.3
  34.5 13.1 %fusion.6 = (f32[256]{0:T(256)S(1)}, f32[256,4096]{1,0:T(8,128)}) fusion(f32[4096]{0:T(1024)S(1)} %broadcast_multiply_fusion, bf16[256,2048]{1,0:T(8,128)(2,1)} %all-gather.2.cloned.1.call-done, bf16[4096,2048]{1,0:T(8,128)(2,1)} %param.6, f32[256]{0:T(256)S(1)} %copy-done.3, pred[32,8,32,128]{3,2,1,0:T(32,128)(4,1)S(1)} %bitcast.15), kind=kOutput, calls=%fused_computation.16 | convolution fusion | flops 4299161600 | bytes 23087104 | tf_op jit(solution)/shard_map/dot_general | solution.py:25
  47.6 4.9 %pmax.7 = f32[256]{0:T(256)S(1)} all-reduce(f32[256]{0:T(256)S(1)} %get-tuple-element.4), channel_id=1, replica_groups=mesh['img'=16,'ori'=2] {'ori'}, use_global_device_ids=true, to_apply=%region_2.3 | all-reduce | flops 256 | bytes 2048 | tf_op jit(solution)/shard_map/pmax | solution.py:33
  52.6 3.4 %fusion.2 = f32[256]{0:T(256)S(1)} fusion(f32[256,4096]{1,0:T(8,128)} %get-tuple-element.5, pred[32,8,32,128]{3,2,1,0:T(32,128)(4,1)S(1)} %bitcast.16, f32[256]{0:T(256)S(1)} %pmax.7), kind=kLoop, calls=%fused_computation.8 | loop fusion | flops 3145472 | bytes 5244928 | tf_op jit(solution)/shard_map/reduce_sum | solution.py:34
  55.9 5.1 %psum.7 = f32[256]{0:T(256)S(1)} all-reduce(f32[256]{0:T(256)S(1)} %fusion.2), channel_id=1, replica_groups=mesh['img'=16,'ori'=2] {'ori'}, use_global_device_ids=true, to_apply=%region_4.5 | all-reduce | flops 256 | bytes 2048 | tf_op jit(solution)/shard_map/psum | solution.py:37
  61.0 0.0 copy-start.1
  61.0 3.9 %fusion.5 = (bf16[4096]{0:T(1024)(128)(2,1)S(1)}, bf16[256,4096]{1,0:T(8,128)(2,1)S(1)}) fusion(f32[256]{0:T(256)S(1)} %psum.7, f32[256,4096]{1,0:T(8,128)} %get-tuple-element.5, f32[256]{0:T(256)S(1)} %pmax.7, pred[32,8,32,128]{3,2,1,0:T(32,128)(4,1)S(1)} %bitcast.17), kind=kLoop, calls=%fused_computation.15 | loop fusion | flops 5238784 | bytes 7350272 | tf_op jit(solution)/shard_map/reduce_sum | solution.py:43
  64.9 0.0 copy-start
  64.9 0.0 copy-done.1
  65.0 5.6 %convolution_convert_fusion = bf16[4096,1024]{1,0:T(8,128)(2,1)} fusion(bf16[256,4096]{1,0:T(8,128)(2,1)S(1)} %get-tuple-element.3, bf16[256,2048]{1,0:T(8,128)(2,1)S(1)} %copy-done.1), kind=kOutput, calls=%fused_computation.1 | convolution fusion | flops 2151677952 | bytes 11010048 | tf_op jit(solution)/shard_map/dot_general | solution.py:11
  70.5 0.0 copy-start.2
  70.5 0.0 reduce-scatter.5.cloned.1.call-update
  70.6 0.0 reduce-scatter.3.cloned.1.call-start
  70.6 0.0 copy-done
  70.6 1.1 copy-done.2
  71.8 5.6 %convolution_convert_fusion.1 = bf16[4096,1024]{1,0:T(8,128)(2,1)} fusion(bf16[256,4096]{1,0:T(8,128)(2,1)S(1)} %get-tuple-element.3, bf16[256,2048]{1,0:T(8,128)(2,1)S(1)} %copy-done.2), kind=kOutput, calls=%fused_computation.2 | convolution fusion | flops 2151677952 | bytes 11010048 | tf_op jit(solution)/shard_map/dot_general | solution.py:11
  77.4 0.0 reduce-scatter.3.cloned.1.call-update
  77.4 0.0 copy-start.4
  77.4 20.0 %convert_element_type.23 = f32[4096,2048]{1,0:T(8,128)} convert(bf16[4096,2048]{1,0:T(8,128)(2,1)} %param.6) | non-fusion elementwise | flops 8388608 | bytes 50331648 | tf_op jit(solution)/shard_map/convert_element_type | solution.py:19
  97.4 0.0 copy-done.4
  97.4 0.6 dynamic-slice
  98.6 34.0 %all-reduce = bf16[4096]{0:T(1024)(128)(2,1)S(1)} all-reduce(bf16[4096]{0:T(1024)(128)(2,1)S(1)} %get-tuple-element.2), channel_id=4, replica_groups=mesh['img'=16,'ori'=2] {'img'}, use_global_device_ids=true, to_apply=%region_8.9.clone | all-reduce | flops 4096 | bytes 16384
  132.6 0.1 convert_add_fusion
  132.7 43.0 %reduce-scatter.5.cloned.1.call-done = bf16[256,1024]{1,0:T(8,128)(2,1)} async-done(((bf16[4096,1024]{1,0:T(8,128)(2,1)}), bf16[256,1024]{1,0:T(8,128)(2,1)}) %reduce-scatter.5.cloned.1.call-update) | async-done | bytes 524304 | tf_op jit(solution)/shard_map/reduce_scatter | solution.py:56
  175.8 108.5 %reduce-scatter.3.cloned.1.call-done = bf16[256,1024]{1,0:T(8,128)(2,1)} async-done(((bf16[4096,1024]{1,0:T(8,128)(2,1)}), bf16[256,1024]{1,0:T(8,128)(2,1)}) %reduce-scatter.3.cloned.1.call-update) | async-done | bytes 524304 | tf_op jit(solution)/shard_map/reduce_scatter | solution.py:46
  284.2 3.5 %add_divide_fusion = f32[256,2048]{1,0:T(8,128)} fusion(f32[4096,2048]{1,0:T(8,128)} %convert_element_type.23, s32[]{:T(128)S(6)} %select_n.18, bf16[256,1024]{1,0:T(8,128)(2,1)} %reduce-scatter.5.cloned.1.call-done, bf16[256,1024]{1,0:T(8,128)(2,1)} %reduce-scatter.3.cloned.1.call-done, f32[256]{0:T(256)S(1)} %convert_add_fusion), kind=kLoop, calls=%fused_computation.9 | loop fusion | flops 3145728 | bytes 5243908 | tf_op jit(solution)/shard_map/div | solution.py:66
  (1 shorter events, 0.0 us)
Async XLA Ops:
  7.2 27.0 %all-gather.2.cloned.1.call-start = ((), (), s32[]{:S(2)}) async-start(), calls=%async_computation.2 | async-start | bytes 1572864 | tf_op jit(solution)/shard_map/all_gather | solution.py:18
  9.3 166.4 %reduce-scatter.5.cloned.1.call-start = ((), (), s32[]{:S(2)}) async-start(), calls=%async_computation.4 | async-start | bytes 8912896 | tf_op jit(solution)/shard_map/reduce_scatter | solution.py:56
  10.1 24.4 %copy-start.3 = (f32[256]{0:T(256)S(1)}, f32[256]{0:T(256)}, u32[]{:S(2)}) copy-start(f32[256]{0:T(256)} %param.5) | copy-start | bytes 3076
  61.0 3.9 %copy-start.1 = (bf16[256,2048]{1,0:T(8,128)(2,1)S(1)}, bf16[256,2048]{1,0:T(8,128)(2,1)}, u32[]{:S(2)}) copy-start(bf16[256,2048]{1,0:T(8,128)(2,1)} %all-gather.2.cloned.1.call-done) | copy-start | bytes 3145732
  64.9 5.7 %copy-start = (bf16[256,4096]{1,0:T(8,128)(2,1)}, bf16[256,4096]{1,0:T(8,128)(2,1)S(1)}, u32[]{:S(2)}) copy-start(bf16[256,4096]{1,0:T(8,128)(2,1)S(1)} %get-tuple-element.3) | copy-start | bytes 6291460
  70.5 1.2 copy-start.2
  70.6 213.6 %reduce-scatter.3.cloned.1.call-start = ((), (), s32[]{:S(2)}) async-start(), calls=%async_computation.3 | async-start | bytes 8912896 | tf_op jit(solution)/shard_map/reduce_scatter | solution.py:46
  77.4 20.0 %copy-start.4 = (u32[32]{0:T(128)S(1)}, u32[32]{0:T(128)}, u32[]{:S(2)}) copy-start(u32[32]{0:T(128)} %constant.28) | copy-start | bytes 388
Sparse Core Ops, SparseCore 0:
  10.1 23.9 all-gather.1
  70.7 105.0 reduce-scatter.4
  179.8 104.3 reduce-scatter.2
where the time goes:
time: 295 us; the launch traced here: 294 us
  waiting for transfers between devices  168 us (57%)
  blocking collectives  44 us (15%)
  other arithmetic  40.8 us (14%)
  matrix products  24.3 us (8%)
  between operations  14.5 us (5%)
    reduce_scatter x1, waiting for transfers between devices, body(): lax.psum_scatter(weighted_sums(posteriors, grouped[:, :half_width]).astyp...  108 us
    reduce_scatter x1, waiting for transfers between devices, body(): lax.psum_scatter(weighted_sums(posteriors, grouped[:, half_width:]).astyp...  43 us
    unnamed x1, blocking collectives  34 us
    convert_element_type x1, other arithmetic, body(): proj_float = projections.astype(jnp.float32)  20 us
    all_gather x1, waiting for transfers between devices, body(): grouped = lax.all_gather(lowered, 'ori', axis=0, tiled=True)  16.9 us
    dot_general x1, matrix products, body(): lax.dot_general(grouped, projections, (((1,), (1,)), ((), ())), preferred...  13.1 us
    dot_general x2, matrix products, weighted_sums(): lax.dot_general(weights, rows_block, (((0,), (0,)), ((), ())), preferred_...  11.2 us
    reduce_sum x1, other arithmetic, body(): squared = jnp.sum(proj_float * proj_float, axis=1)  7.19 us
  transfers between devices with their start and end apart: 3, of which 3 were waited for; matrix products, arithmetic and copies ran while one was open for 12% of the time, Pallas kernels for 0%

commit v1 on v0

v1 whole, which is shorter than its diff:
```python
import functools

import jax
import jax.numpy as jnp
from jax import lax
from jax.experimental import pallas as pl
from jax.experimental.pallas import tpu as pltpu
from jax.sharding import PartitionSpec as P

prior_weight = 1.0
very_low = -1e30
both = ("img", "ori")
lanes = 128
cores = 2
vmem = pl.BlockSpec(memory_space=pltpu.VMEM)
smem = pl.BlockSpec(memory_space=pltpu.SMEM)
anywhere = pl.BlockSpec(memory_space=pl.ANY)
contract_last = (((1,), (1,)), ((), ()))


def weighted_sums(weights, rows_block):
    return lax.dot_general(
        weights, rows_block, (((0,), (0,)), ((), ())), preferred_element_type=jnp.float32
    )


def reduced_body(images, precision, projections, tile_mask):
    lowered = images.astype(jnp.bfloat16)
    grouped = lax.all_gather(lowered, "ori", axis=0, tiled=True)
    proj_float = projections.astype(jnp.float32)
    squared = jnp.sum(proj_float * proj_float, axis=1)
    blocks, tiles_here = tile_mask.shape
    per_block = grouped.shape[0] // blocks
    tile_width = projections.shape[0] // tiles_here
    columns = grouped.shape[1]
    products = lax.dot_general(
        grouped, projections, contract_last, preferred_element_type=jnp.float32
    )
    scores = precision[:, None] * (products - 0.5 * squared[None, :])
    shaped = scores.reshape(blocks, per_block, tiles_here, tile_width)
    alive = jnp.broadcast_to((tile_mask > 0)[:, None, :, None], shaped.shape)
    masked = jnp.where(alive, shaped, very_low)
    local_high = jnp.max(masked, axis=(2, 3))
    row_high = lax.pmax(local_high, "ori")
    lifted = jnp.where(alive, jnp.exp(masked - row_high[:, :, None, None]), 0.0)
    row_total = lax.psum(jnp.sum(lifted, axis=(2, 3)), "ori")
    probable = lifted / row_total[:, :, None, None]
    posteriors = probable.reshape(scores.shape).astype(jnp.bfloat16)
    counts = jnp.sum(posteriors.astype(jnp.float32), axis=0)
    half_width = columns // 2
    halves = [
        lax.psum_scatter(
            weighted_sums(posteriors, part).astype(jnp.bfloat16),
            "img",
            scatter_dimension=0,
            tiled=True,
        ).astype(jnp.float32)
        for part in (grouped[:, :half_width], grouped[:, half_width:])
    ]
    totals = lax.psum_scatter(
        counts.astype(jnp.bfloat16), "img", scatter_dimension=0, tiled=True
    ).astype(jnp.float32)
    summed = jnp.concatenate(halves, axis=1)
    rows_here = summed.shape[0]
    first_row = lax.axis_index("img") * rows_here
    prior_rows = lax.dynamic_slice_in_dim(proj_float, first_row, rows_here, 0)
    refined = (summed + prior_weight * prior_rows) / (totals[:, None] + prior_weight)
    return (posteriors, refined)


def as_row(column):
    return jnp.transpose(jnp.broadcast_to(column, (column.shape[0], lanes)))[0:1, :]


def as_column(row):
    return jnp.transpose(jnp.broadcast_to(row, (lanes, row.shape[1])))[:, 0:1]


def scores_kernel(
    mask_s, prec_ref, own_ref, other_ref, proj_ref, scores_ref, stats_ref, half_ref,
    rows_buf, high, total, prec_col, sems,
):
    step = pl.program_id(0)
    here = lax.axis_index("ori")
    chip = lax.axis_index("img") // cores
    shard = own_ref.shape[0]
    blocks, tiles = mask_s.shape
    width = proj_ref.shape[0]
    tiles_here = tiles // pl.num_programs(0)
    tile = width // tiles_here

    @pl.when(step == 0)
    def _():
        copies = [
            pltpu.make_async_copy(
                ref, rows_buf.at[pl.ds(pl.multiple_of(at * shard, shard), shard)], sems.at[i]
            )
            for i, (ref, at) in enumerate(((own_ref, here), (other_ref, 1 - here)))
        ]
        for copy in copies:
            copy.start()
        prec_col[...] = jnp.transpose(
            jnp.broadcast_to(prec_ref[...], (lanes, prec_ref.shape[1]))
        )
        high[...] = jnp.full(high.shape, very_low, jnp.float32)
        total[...] = jnp.zeros(total.shape, jnp.float32)
        for copy in copies:
            copy.wait()

    wide = proj_ref[...].astype(jnp.float32)
    half = 0.5 * jnp.sum(wide * wide, axis=1, keepdims=True)
    half_wide = jnp.broadcast_to(half, (width, lanes))

    @pl.when(step == chip)
    def _():
        half_ref[...] = half_wide

    half_row = jnp.transpose(half_wide)[0:1, :]
    products = lax.dot_general(
        rows_buf[...], proj_ref[...], contract_last, preferred_element_type=jnp.float32
    )
    scores = prec_col[:, 0:1] * (products - half_row)
    for b in range(blocks):
        rows = slice(b * shard, (b + 1) * shard)
        parts = []
        for t in range(tiles_here):
            alive = mask_s[b, step * tiles_here + t] > 0
            kept = jnp.where(alive, scores[rows, t * tile : (t + 1) * tile], very_low)
            scores_ref[rows, t * tile : (t + 1) * tile] = kept
            parts += [kept[:, c : c + lanes] for c in range(0, tile, lanes)]
        before = high[rows, :]
        now = functools.reduce(jnp.maximum, parts, before)
        added = functools.reduce(jnp.add, [jnp.exp(part - now) for part in parts])
        total[rows, :] = total[rows, :] * jnp.exp(before - now) + added
        high[rows, :] = now

    @pl.when(step == pl.num_programs(0) - 1)
    def _():
        top = jnp.max(high[...], axis=1, keepdims=True)
        mass = jnp.sum(total[...] * jnp.exp(high[...] - top), axis=1, keepdims=True)
        stats_ref[0:1, :] = as_row(top)
        stats_ref[1:2, :] = as_row(mass)
        stats_ref[2:3, :] = prec_ref[...]
        stats_ref[3:8, :] = jnp.zeros((5, stats_ref.shape[1]), jnp.float32)


def posterior_kernel(scores_ref, mine_ref, theirs_ref, post_ref, meta_ref):
    top = jnp.maximum(mine_ref[0:1, :], theirs_ref[0:1, :])
    mass = mine_ref[1:2, :] * jnp.exp(mine_ref[0:1, :] - top) + theirs_ref[
        1:2, :
    ] * jnp.exp(theirs_ref[0:1, :] - top)
    share = 1.0 / mass

    @pl.when(pl.program_id(0) == 0)
    def _():
        parts, _, shard = meta_ref.shape
        for b in range(parts):
            columns = slice(b * shard, (b + 1) * shard)
            meta_ref[b, 0:1, :] = top[:, columns]
            meta_ref[b, 1:2, :] = share[:, columns]
            meta_ref[b, 2:8, :] = mine_ref[2:8, columns]

    post_ref[...] = (
        jnp.exp(scores_ref[...] - as_column(top)) * as_column(share)
    ).astype(post_ref.dtype)


def sums_kernel(steps, counts_of, first, last, *refs):
    mask_s, meta_ref, half_ref, proj_ref = refs[:4]
    refs = refs[4:]
    pieces = refs[: len(counts_of)]
    refs = refs[len(counts_of) :]
    if not first:
        acc_ref, cnt_ref = refs[:2]
        refs = refs[2:]
    outs, refs = refs[: 3 if last else 2], refs[3 if last else 2 :]
    proj_buf, rows_buf, weights_buf, seen_buf, sems = refs
    img, ori = lax.axis_index("img"), lax.axis_index("ori")
    chip, core = img // cores, lax.rem(img, cores)
    width, columns = proj_buf.shape
    shard = rows_buf.shape[0] // len(steps)
    copies = [
        pltpu.make_async_copy(
            proj_ref.at[pl.ds(pl.multiple_of(chip * width, width), width)],
            proj_buf,
            sems.at[len(pieces)],
        )
    ]
    at = 0
    for i, (piece, n) in enumerate(zip(pieces, counts_of, strict=True)):
        copies.append(pltpu.make_async_copy(piece, rows_buf.at[at : at + n], sems.at[i]))
        at += n
    for copy in copies:
        copy.start()
    for copy in copies:
        copy.wait()
    tiles = mask_s.shape[1]
    tiles_here = tiles * width // proj_ref.shape[0]
    tile = width // tiles_here
    products = lax.dot_general(
        proj_buf[...], rows_buf[...], contract_last, preferred_element_type=jnp.float32
    )
    weights, seen = [], jnp.zeros((width, shard), jnp.float32)
    for b, (d_img, d_ori) in enumerate(steps):
        source_img, source_ori = img ^ d_img, ori ^ d_ori
        parts = lax.div(mask_s.shape[0] * 1, lax.axis_size("img"))
        meta = meta_ref[lax.div(source_img, cores) * parts + source_ori]
        top, share, prec = meta[0:1, :], meta[1:2, :], meta[2:3, :]
        mine = prec * (products[:, b * shard : (b + 1) * shard] - half_ref[...])
        down = []
        for t in range(tiles_here):
            alive = mask_s[source_img * parts + source_ori, chip * tiles_here + t] > 0
            floor = jnp.where(alive, -top, very_low)
            down.append(
                (jnp.exp(mine[t * tile : (t + 1) * tile, :] + floor) * share).astype(
                    jnp.bfloat16
                )
            )
        weight = jnp.concatenate(down, axis=0)
        seen += weight.astype(jnp.float32)
        weights.append(weight)
    for b, weight in enumerate(weights):
        weights_buf[:, b * shard : (b + 1) * shard] = weight
    if not first:
        seen += cnt_ref[...]
    everything = pl.ds(0, width)
    if last:
        kept_ref, kept_cnt_ref, sent_ref = outs
        half_width = width // 2
        keep = pl.ds(pl.multiple_of(core * half_width, half_width), half_width)
        send = pl.ds(pl.multiple_of((1 - core) * half_width, half_width), half_width)
        seen_buf[...] = jnp.broadcast_to(jnp.sum(seen, axis=1, keepdims=True), seen.shape)
        kept_cnt_ref[...] = seen_buf[keep, :]
        sent_ref[:, columns:] = seen_buf[send, :].astype(jnp.bfloat16)
        targets = ((send, sent_ref), (keep, kept_ref))
    else:
        outs[1][...] = seen
        targets = ((everything, outs[0]),)
    chunk = min(columns, 512)
    for where, out in targets:
        for c in range(0, columns, chunk):
            part = slice(c, c + chunk)
            sums = lax.dot_general(
                weights_buf[where, :],
                rows_buf[:, part],
                (((1,), (0,)), ((), ())),
                preferred_element_type=jnp.float32,
            )
            if not first:
                sums += acc_ref[where, part]
            out[:, part] = sums.astype(out.dtype)


def final_kernel(kept_ref, kept_cnt_ref, got_ref, proj_ref, out_ref):
    columns = out_ref.shape[1]
    counts = kept_cnt_ref[:, 0:1] + got_ref[:, columns : columns + 1].astype(jnp.float32)
    sums = kept_ref[...] + got_ref[:, :columns].astype(jnp.float32)
    prior = prior_weight * proj_ref[...].astype(jnp.float32)
    out_ref[...] = (sums + prior) / (counts + prior_weight)


def gathered_body(n_img, n_ori, images, precision, projections, tile_mask):
    n = n_img * n_ori
    shard, columns = images.shape
    orient = projections.shape[0]
    chips = n_img // cores
    width = orient // chips
    blocks, tiles = tile_mask.shape

    def swap(a, d_img, d_ori):
        mask = d_img * n_ori + d_ori
        return lax.ppermute(a, both, [(i, i ^ mask) for i in range(n)])

    x, y, core = (0, 1), (cores, 0), (1, 0)
    lowered = images.astype(jnp.bfloat16)

    def plane(a):
        from_x, from_y = swap(a, *x), swap(a, *y)
        h = a.shape[0] // 2
        far = [swap(from_x[:h], *y), swap(from_y[h:], *x)]
        return [(x, [from_x]), (y, [from_y]), ((y[0], x[1]), far)]

    slabs = [(0, lowered)]
    bit = n_img // 2
    while bit > cores:
        slabs += [(d | bit, swap(a, bit, 0)) for d, a in slabs]
        bit //= 2
    order = sorted(slabs, key=lambda slab: slab[0].bit_count() * n_img + slab[0])
    groups = []
    for d, a in order:
        groups.append(
            [((d, 0), [a])] + [((d ^ p[0], p[1]), pieces) for p, pieces in plane(a)]
        )
    from_x = groups[0][1][1][0]

    all_masks = lax.all_gather(tile_mask, "img", axis=0, tiled=True)
    prec_row = precision.reshape(1, -1)
    rows = prec_row.shape[1]
    f32 = jnp.float32
    scores, stats, half = pl.pallas_call(
        scores_kernel,
        grid=(chips,),
        in_specs=[
            smem,
            vmem,
            anywhere,
            anywhere,
            pl.BlockSpec((width, columns), lambda i: (i, 0)),
        ],
        out_specs=[
            pl.BlockSpec((rows, width), lambda i: (0, i)),
            pl.BlockSpec((8, rows), lambda i: (0, 0)),
            pl.BlockSpec((width, lanes), lambda i: (0, 0)),
        ],
        out_shape=[
            jax.ShapeDtypeStruct((rows, orient), f32),
            jax.ShapeDtypeStruct((8, rows), f32),
            jax.ShapeDtypeStruct((width, lanes), f32),
        ],
        scratch_shapes=[
            pltpu.VMEM((rows, columns), jnp.bfloat16),
            pltpu.VMEM((rows, lanes), f32),
            pltpu.VMEM((rows, lanes), f32),
            pltpu.VMEM((rows, lanes), f32),
            pltpu.SemaphoreType.DMA((2,)),
        ],
        compiler_params=pltpu.CompilerParams(vmem_limit_bytes=32 * 2**20),
        cost_estimate=pl.CostEstimate(
            flops=2 * rows * orient * columns,
            bytes_accessed=2 * orient * columns + 4 * rows * orient,
            transcendentals=rows * orient,
        ),
        name="scores",
    )(tile_mask, prec_row, lowered, from_x, projections)
    theirs = swap(stats, *x)
    cut = 4
    posteriors, meta = pl.pallas_call(
        posterior_kernel,
        grid=(cut,),
        in_specs=[
            pl.BlockSpec((rows, orient // cut), lambda i: (0, i)),
            pl.BlockSpec((8, rows), lambda i: (0, 0)),
            pl.BlockSpec((8, rows), lambda i: (0, 0)),
        ],
        out_specs=[
            pl.BlockSpec((rows, orient // cut), lambda i: (0, i)),
            pl.BlockSpec((n_ori, 8, shard), lambda i: (0, 0, 0)),
        ],
        out_shape=[
            jax.ShapeDtypeStruct((rows, orient), jnp.bfloat16),
            jax.ShapeDtypeStruct((n_ori, 8, shard), f32),
        ],
        compiler_params=pltpu.CompilerParams(vmem_limit_bytes=32 * 2**20),
        cost_estimate=pl.CostEstimate(
            flops=3 * rows * orient,
            bytes_accessed=6 * rows * orient,
            transcendentals=rows * orient,
        ),
        name="posterior",
    )(scores, stats, theirs)
    same_core = [[i * cores + c for i in range(chips)] for c in range(cores)]
    all_meta = lax.all_gather(meta, "img", axis=0, tiled=True, axis_index_groups=same_core)

    def add(group, state, last):
        steps = tuple(d for d, _ in group)
        pieces = [p for _, ps in group for p in ps]
        counts_of = tuple(p.shape[0] for p in pieces)
        first = state is None
        images_here = sum(counts_of)
        if last:
            out_shape = [
                jax.ShapeDtypeStruct((width // 2, columns), f32),
                jax.ShapeDtypeStruct((width // 2, lanes), f32),
                jax.ShapeDtypeStruct((width // 2, columns + lanes), jnp.bfloat16),
            ]
            aliases = {}
        else:
            out_shape = [
                jax.ShapeDtypeStruct((width, columns), f32),
                jax.ShapeDtypeStruct((width, lanes), f32),
            ]
            aliases = {} if first else {4 + len(pieces): 0, 5 + len(pieces): 1}
        return pl.pallas_call(
            functools.partial(sums_kernel, steps, counts_of, first, last),
            in_specs=[smem, vmem, vmem, anywhere]
            + [anywhere] * len(pieces)
            + ([] if first else [vmem, vmem]),
            out_specs=[vmem] * len(out_shape),
            out_shape=out_shape,
            input_output_aliases=aliases,
            scratch_shapes=[
                pltpu.VMEM((width, columns), jnp.bfloat16),
                pltpu.VMEM((images_here, columns), jnp.bfloat16),
                pltpu.VMEM((width, images_here), jnp.bfloat16),
                pltpu.VMEM((width, lanes), f32),
                pltpu.SemaphoreType.DMA((len(pieces) + 1,)),
            ],
            compiler_params=pltpu.CompilerParams(vmem_limit_bytes=32 * 2**20),
            cost_estimate=pl.CostEstimate(
                flops=4 * width * images_here * columns,
                bytes_accessed=2 * (width + images_here) * columns + 8 * width * columns,
                transcendentals=width * images_here,
            ),
            name="sums",
        )(all_masks, all_meta, half, projections, *pieces, *(state or ()))

    state = None
    for i, group in enumerate(groups):
        state = add(group, state, i == len(groups) - 1)
    kept, kept_cnt, sent = state
    got = swap(sent, *core)
    out_rows = width // 2
    cut = 4
    first_row = lax.axis_index("img").astype(jnp.int32).reshape(1)
    refined = pl.pallas_call(
        lambda at, *refs: final_kernel(*refs),
        grid_spec=pltpu.PrefetchScalarGridSpec(
            num_scalar_prefetch=1,
            grid=(cut,),
            in_specs=[
                pl.BlockSpec((out_rows // cut, columns), lambda i, at: (i, 0)),
                pl.BlockSpec((out_rows // cut, lanes), lambda i, at: (i, 0)),
                pl.BlockSpec((out_rows // cut, columns + lanes), lambda i, at: (i, 0)),
                pl.BlockSpec((out_rows // cut, columns), lambda i, at: (at[0] * cut + i, 0)),
            ],
            out_specs=pl.BlockSpec((out_rows // cut, columns), lambda i, at: (i, 0)),
        ),
        out_shape=jax.ShapeDtypeStruct((out_rows, columns), f32),
        compiler_params=pltpu.CompilerParams(vmem_limit_bytes=32 * 2**20),
        name="final",
    )(first_row, kept, kept_cnt, got, projections)
    return posteriors, refined


def solution(mesh):
    n_img, n_ori = mesh.shape["img"], mesh.shape["ori"]

    def body(images, precision, projections, tile_mask):
        shard, columns = images.shape
        orient = projections.shape[0]
        blocks, tiles = tile_mask.shape
        gathered_bytes = 2 * images.size * n_img * n_ori // cores
        fits = (
            n_ori == 2
            and n_img >= 2 * cores
            and n_img & (n_img - 1) == 0
            and blocks == n_ori
            and shard % lanes == 0
            and tiles * cores % n_img == 0
            and orient % (tiles * lanes) == 0
            and gathered_bytes <= 16 * 2**20
        )
        if fits:
            return gathered_body(n_img, n_ori, images, precision, projections, tile_mask)
        return reduced_body(images, precision, projections, tile_mask)

    return jax.shard_map(
        body,
        mesh=mesh,
        in_specs=(P(("img", "ori"), None), P("img"), P("ori", None), P("img", "ori")),
        out_specs=(P("img", "ori"), P(("ori", "img"), None)),
        check_vma=False,
    )
```

time: 295 us -> 170 us (0.58)
  waiting for transfers between devices: 168 us -> 34.4 us
  other arithmetic: 40.8 us -> 1.29 us
  Pallas kernels: 0 us -> 38.4 us
  starting transfers between devices: 0.12 us -> 25 us
  matrix products: 24.3 us -> 0 us
  between operations: 14.5 us -> 0.84 us
  blocking collectives: 44 us -> 56.9 us
  local copies, waits for them, and re-layouts: 2.08 us -> 13 us
    reduce_scatter x2 -> x0, waiting for transfers between devices: 151 us -> none  [the longest x1 108 us: body(): lax.psum_scatter(weighted_sums(posteriors, grouped[:, :half_width]).astyp...]
    all_gather x0 -> x2, blocking collectives: none -> 56.9 us  [the longest x1 30.8 us: gathered_body(): lax.all_gather(meta, 'img', axis=0, tiled=True, axis_index_groups=same_core)]
    pallas_call x0 -> x7, Pallas kernels: none -> 38.4 us  [the longest x4 21.5 us: add(): pl.pallas_call(functools.partial(sums_kernel, steps, counts_of, first, la...]
    ppermute x0 -> x21, waiting for transfers between devices: none -> 34.4 us  [swap(): return lax.ppermute(a, both, [(i, i ^ mask) for i in range(n)])]
    unnamed x1 -> x0, blocking collectives: 34 us -> none
    ppermute x0 -> x21, starting transfers between devices: none -> 25 us  [swap(): return lax.ppermute(a, both, [(i, i ^ mask) for i in range(n)])]
    dot_general x3 -> x0, matrix products: 24.3 us -> none  [the longest x1 13.1 us: body(): lax.dot_general(grouped, projections, (((1,), (1,)), ((), ())), preferred...]
    convert_element_type x2 -> x1, other arithmetic: 22.1 us -> 1.29 us  [gathered_body(): lowered = images.astype(jnp.bfloat16)]
  transfers between devices with their start and end apart: 3 -> 21, of which waited for: 3 -> 4; matrix products, arithmetic and copies ran while one was open for 12% -> 0% of each run, Pallas kernels for 0% -> 18%
where the time goes in v1:
time: 170 us
  blocking collectives  56.9 us (33%)
  Pallas kernels  38.4 us (23%)
  waiting for transfers between devices  34.4 us (20%)
  starting transfers between devices  25 us (15%)
  local copies, waits for them, and re-layouts  13 us (8%)
    ppermute x21, waiting for transfers between devices, swap(): return lax.ppermute(a, both, [(i, i ^ mask) for i in range(n)])  34.4 us
    all_gather x1, blocking collectives, gathered_body(): lax.all_gather(meta, 'img', axis=0, tiled=True, axis_index_groups=same_core)  30.8 us
    all_gather x1, blocking collectives, gathered_body(): all_masks = lax.all_gather(tile_mask, 'img', axis=0, tiled=True)  26.1 us
    ppermute x21, starting transfers between devices, swap(): return lax.ppermute(a, both, [(i, i ^ mask) for i in range(n)])  25 us
    pallas_call x4, Pallas kernels, add(): pl.pallas_call(functools.partial(sums_kernel, steps, counts_of, first, la...  21.5 us
    unnamed x8, local copies, waits for them, and re-layouts  12.9 us
    pallas_call x1, Pallas kernels, gathered_body(): pl.pallas_call(scores_kernel, grid=(chips,), in_specs=[smem, vmem, anywhe...  12.1 us
  transfers between devices with their start and end apart: 21, of which 4 were waited for; matrix products, arithmetic and copies ran while one was open for 0% of the time, Pallas kernels for 18%

profile of v1, /device:TPU:0, one launch (start us, length us, event | category | flops | bytes accessed | tf_op | source)
XLA Modules:
  0.0 169.9 jit_solution(14417625113683745169)
XLA Ops:
  0.6 1.3 convert_element_type.3.own_ref.refs_4_
  1.9 4.1 %collective-permute-start.2 = (bf16[128,2048]{1,0:T(8,128)(2,1)S(1)}, bf16[128,2048]{1,0:T(8,128)(2,1)S(1)}, u32[]{:S(2)}, u32[]{:S(2)}) collective-permute-start(bf16[128,2048]{1,0:T(8,128)(2,1)S(1)} %convert_element_type.3.own_ref.refs_4_), channel_id=1, source_target_pairs={{0,16},{1,17},{2,18},{3,19},{4,20},{5,21},{6,22},{7,23},{8,24},{9,... | collective-permute-start | bytes 1572872 | tf_op jit(solution)/shard_map/ppermute | solution.py:272
  6.0 1.5 collective-permute-start
  7.5 1.6 collective-permute-start.12
  9.1 1.5 collective-permute-start.17
  10.6 18.7 %collective-permute-done.2.refs_4_ = bf16[128,2048]{1,0:T(8,128)(2,1)S(1)} collective-permute-done((bf16[128,2048]{1,0:T(8,128)(2,1)S(1)}, bf16[128,2048]{1,0:T(8,128)(2,1)S(1)}, u32[]{:S(2)}, u32[]{:S(2)}) %collective-permute-start.2) | collective-permute-done | bytes 524320 | tf_op jit(solution)/shard_map/ppermute | solution.py:272
  29.3 0.7 collective-permute-start.3
  29.9 0.0 collective-permute-done.other_ref.refs_5_
  30.0 1.6 collective-permute-start.18
  31.6 0.0 collective-permute-done.12.refs_4_
  31.6 1.4 collective-permute-start.13
  33.0 0.5 collective-permute-start.14
  33.5 0.0 copy-start
  33.5 5.8 %copy-done = bf16[4096,2048]{1,0:T(8,128)(2,1)S(1)} copy-done((bf16[4096,2048]{1,0:T(8,128)(2,1)S(1)}, bf16[4096,2048]{1,0:T(8,128)(2,1)}, u32[]{:S(2)}) %copy-start) | copy-done | bytes 16777240
  39.3 0.0 copy-start.2
  39.3 0.7 copy-done.2
  40.0 0.0 copy-start.3
  40.0 0.7 copy-done.3
  40.6 12.1 %scores.1 = (f32[256,4096]{1,0:T(8,128)S(1)}, f32[8,256]{1,0:T(8,128)S(1)}, f32[512,128]{1,0:T(8,128)S(1)}) custom-call(s32[2,32]{1,0:T(2,128)S(1)} %copy-done.2, f32[1,256]{1,0:T(1,128)S(1)} %bitcast.9, bf16[128,2048]{1,0:T(8,128)(2,1)S(1)} %convert_element_type.3.own_ref.refs_4_, bf16[128,2048]{1,0:T(8,128)(2,1)S(1)} %collective-permute-done.other_ref.refs_5_, ...), custom_call_target="tpu_custom_call" | custom-call | flops 4294967296 | bytes 20971520 | tf_op jit(solution)/shard_map/scores/pallas_call | solution.py:300
  52.8 0.0 collective-permute-done.17.refs_6_
  52.8 0.8 collective-permute-start.1
  53.6 2.9 %collective-permute-done.1.theirs_ref = f32[8,256]{1,0:T(8,128)S(1)} collective-permute-done((f32[8,256]{1,0:T(8,128)S(1)}, f32[8,256]{1,0:T(8,128)S(1)}, u32[]{:S(2)}, u32[]{:S(2)}) %collective-permute-start.1) | collective-permute-done | bytes 8224 | tf_op jit(solution)/shard_map/ppermute | solution.py:272
  56.5 0.8 collective-permute-start.8
  57.3 0.0 collective-permute-done.18.refs_7_
  57.3 1.3 collective-permute-start.9
  58.6 0.0 collective-permute-done.3.refs_4_
  58.6 1.4 collective-permute-start.4
  60.1 0.0 collective-permute-done.13.refs_5_
  60.1 0.5 collective-permute-start.5
  60.6 0.0 collective-permute-done.14.refs_6_
  60.6 0.8 collective-permute-start.19
  61.5 9.9 %collective-permute-done.8.refs_5_ = bf16[128,2048]{1,0:T(8,128)(2,1)S(1)} collective-permute-done((bf16[128,2048]{1,0:T(8,128)(2,1)S(1)}, bf16[128,2048]{1,0:T(8,128)(2,1)S(1)}, u32[]{:S(2)}, u32[]{:S(2)}) %collective-permute-start.8) | collective-permute-done | bytes 524320 | tf_op jit(solution)/shard_map/ppermute | solution.py:272
  71.4 1.5 collective-permute-start.15
  72.9 0.0 collective-permute-done.9.refs_6_
  72.9 0.6 collective-permute-start.16
  73.5 26.1 %all-gather = s32[16,2,32]{2,1,0:T(2,128)S(1)} all-gather(s32[1,2,32]{2,1,0:T(2,128)S(1)} %bitcast.8), channel_id=1, replica_groups=mesh['img'=16,'ori'=2] {'img'}, dimensions={0}, use_global_device_ids=true | all-gather | bytes 4352 | tf_op jit(solution)/shard_map/all_gather | solution.py:296
  99.6 2.8 %posterior.1 = (bf16[256,4096]{1,0:T(8,128)(2,1)}, f32[2,8,128]{2,1,0:T(8,128)S(1)}) custom-call(f32[256,4096]{1,0:T(8,128)S(1)} %get-tuple-element.16.scores_ref, f32[8,256]{1,0:T(8,128)S(1)} %get-tuple-element.17.mine_ref, f32[8,256]{1,0:T(8,128)S(1)} %collective-permute-done.1.theirs_ref), custom_call_target="tpu_custom_call" | custom-call | flops 3145728 | bytes 6291456 | tf_op jit(solution)/shard_map/posterior/pallas_call | solution.py:337
  102.4 30.8 %all_gather.7.refs_1_ = f32[16,8,128]{2,1,0:T(8,128)S(1)} all-gather(f32[2,8,128]{2,1,0:T(8,128)S(1)} %get-tuple-element.19), channel_id=1, replica_groups={{0,4,8,12,16,20,24,28},{2,6,10,14,18,22,26,30},{1,5,9,13,17,21,25,29},{..., dimensions={0}, use_global_device_ids=true | all-gather | bytes 73728 | tf_op jit(solution)/shard_map/all_gather | solution.py:362
  133.2 0.0 collective-permute-done.19.refs_8_
  133.2 0.1 collective-permute-start.10
  133.3 0.0 collective-permute-done.4.refs_5_
  133.3 1.5 collective-permute-start.11
  134.8 5.1 %sums.4 = (f32[512,2048]{1,0:T(8,128)S(1)}, f32[512,128]{1,0:T(8,128)S(1)}) custom-call(s32[32,32]{1,0:T(8,128)S(1)} %bitcast.4, f32[16,8,128]{2,1,0:T(8,128)S(1)} %all_gather.7.refs_1_, f32[512,128]{1,0:T(8,128)S(1)} %get-tuple-element.20.refs_2_, bf16[4096,2048]{1,0:T(8,128)(2,1)} %refs_3_.9, bf16[128,2048]{1,0:T(8,128)(2,1)S(1)} %convert_element_type.3.own_ref.refs_4_, ...), custom_call_target="tpu_custom_call" | custom-call | flops 2147483648 | bytes 12582912 | tf_op jit(solution)/shard_map/sums/pallas_call | solution.py:383
  140.0 0.0 collective-permute-done.5.refs_6_
  140.0 2.0 %collective-permute-start.6 = (bf16[64,2048]{1,0:T(8,128)(2,1)S(1)}, bf16[64,2048]{1,0:T(8,128)(2,1)S(1)}, u32[]{:S(2)}, u32[]{:S(2)}) collective-permute-start(bf16[64,2048]{1,0:T(8,128)(2,1)S(1)} %slice.32), channel_id=1, source_target_pairs={{0,4},{1,5},{2,6},{3,7},{4,0},{5,1},{6,2},{7,3},{8,12},{9,13},{10,... | collective-permute-start | bytes 786440 | tf_op jit(solution)/shard_map/ppermute | solution.py:272
  142.0 0.0 collective-permute-done.15.refs_7_
  142.0 0.6 collective-permute-start.7
  142.7 0.0 collective-permute-done.16.refs_8_
  142.7 5.2 %sums.5 = (f32[512,2048]{1,0:T(8,128)S(1)}, f32[512,128]{1,0:T(8,128)S(1)}) custom-call(s32[32,32]{1,0:T(8,128)S(1)} %bitcast.5, f32[16,8,128]{2,1,0:T(8,128)S(1)} %all_gather.7.refs_1_, f32[512,128]{1,0:T(8,128)S(1)} %get-tuple-element.20.refs_2_, bf16[4096,2048]{1,0:T(8,128)(2,1)} %refs_3_.9, ...), custom_call_target="tpu_custom_call", output_to_operand_aliasing={{0}: (9, {}), {1}: (10, {})} | custom-call | flops 2147483648 | bytes 12582912 | tf_op jit(solution)/shard_map/sums/pallas_call | solution.py:383
  147.9 0.0 collective-permute-done.10.refs_7_
  147.9 0.0 collective-permute-done.11.refs_8_
  147.9 5.2 %sums.6 = (f32[512,2048]{1,0:T(8,128)S(1)}, f32[512,128]{1,0:T(8,128)S(1)}) custom-call(s32[32,32]{1,0:T(8,128)S(1)} %bitcast.6, f32[16,8,128]{2,1,0:T(8,128)S(1)} %all_gather.7.refs_1_, f32[512,128]{1,0:T(8,128)S(1)} %get-tuple-element.20.refs_2_, bf16[4096,2048]{1,0:T(8,128)(2,1)} %refs_3_.9, ...), custom_call_target="tpu_custom_call", output_to_operand_aliasing={{0}: (9, {}), {1}: (10, {})} | custom-call | flops 2147483648 | bytes 12582912 | tf_op jit(solution)/shard_map/sums/pallas_call | solution.py:383
  153.1 0.0 collective-permute-done.6.refs_7_
  153.1 0.0 collective-permute-done.7.refs_8_
  153.1 6.0 %sums.7 = (f32[256,2048]{1,0:T(8,128)S(1)}, f32[256,128]{1,0:T(8,128)S(1)}, bf16[256,2176]{1,0:T(8,128)(2,1)}) custom-call(s32[32,32]{1,0:T(8,128)S(1)} %bitcast.7, f32[16,8,128]{2,1,0:T(8,128)S(1)} %all_gather.7.refs_1_, f32[512,128]{1,0:T(8,128)S(1)} %get-tuple-element.20.refs_2_, bf16[4096,2048]{1,0:T(8,128)(2,1)} %refs_3_.9, ...), custom_call_target="tpu_custom_call" | custom-call | flops 2147483648 | bytes 12582912 | tf_op jit(solution)/shard_map/sums/pallas_call | solution.py:383
  159.1 0.1 collective-permute-start.20
  159.2 2.9 %collective-permute-done.20.refs_2_ = bf16[256,2176]{1,0:T(8,128)(2,1)S(1)} collective-permute-done((bf16[256,2176]{1,0:T(8,128)(2,1)}, bf16[256,2176]{1,0:T(8,128)(2,1)S(1)}, u32[]{:S(2)}, u32[]{:S(2)}) %collective-permute-start.20) | collective-permute-done | bytes 1114144 | tf_op jit(solution)/shard_map/ppermute | solution.py:272
  162.1 0.0 copy-start.1
  162.1 5.8 %copy-done.1 = bf16[4096,2048]{1,0:T(8,128)(2,1)S(1)} copy-done((bf16[4096,2048]{1,0:T(8,128)(2,1)S(1)}, bf16[4096,2048]{1,0:T(8,128)(2,1)}, u32[]{:S(2)}) %copy-start.1) | copy-done | bytes 16777240
  167.9 2.0 %final.1 = f32[256,2048]{1,0:T(8,128)} custom-call(s32[1]{0:T(128)} %bitcast.1.at, f32[256,2048]{1,0:T(8,128)S(1)} %get-tuple-element.27.refs_0_, f32[256,128]{1,0:T(8,128)S(1)} %get-tuple-element.28.refs_1_, bf16[256,2176]{1,0:T(8,128)(2,1)S(1)} %collective-permute-done.20.refs_2_, bf16[4096,2048]{1,0:T(8,128)(2,1)S(1)} %copy-done.1), custom_call_target="tpu_custom_call" | custom-call | tf_op jit(solution)/shard_map/final/pallas_call | solution.py:415
  (8 shorter events, 0.1 us)
Async XLA Ops:
  1.9 27.4 %collective-permute-start.2 = (bf16[128,2048]{1,0:T(8,128)(2,1)S(1)}, bf16[128,2048]{1,0:T(8,128)(2,1)S(1)}, u32[]{:S(2)}, u32[]{:S(2)}) collective-permute-start(bf16[128,2048]{1,0:T(8,128)(2,1)S(1)} %convert_element_type.3.own_ref.refs_4_), channel_id=1, source_target_pairs={{0,16},{1,17},{2,18},{3,19},{4,20},{5,21},{6,22},{7,23},{8,24},{9,... | collective-permute-start | bytes 1572872 | tf_op jit(solution)/shard_map/ppermute | solution.py:272
  6.0 23.9 %collective-permute-start = (bf16[128,2048]{1,0:T(8,128)(2,1)S(1)}, bf16[128,2048]{1,0:T(8,128)(2,1)S(1)}, u32[]{:S(2)}, u32[]{:S(2)}) collective-permute-start(bf16[128,2048]{1,0:T(8,128)(2,1)S(1)} %convert_element_type.3.own_ref.refs_4_), channel_id=1, source_target_pairs={{0,1},{1,0},{2,3},{3,2},{4,5},{5,4},{6,7},{7,6},{8,9},{9,8},{10,11... | collective-permute-start | bytes 1572872 | tf_op jit(solution)/shard_map/ppermute | solution.py:272
  7.5 24.0 %collective-permute-start.12 = (bf16[128,2048]{1,0:T(8,128)(2,1)S(1)}, bf16[128,2048]{1,0:T(8,128)(2,1)S(1)}, u32[]{:S(2)}, u32[]{:S(2)}) collective-permute-start(bf16[128,2048]{1,0:T(8,128)(2,1)S(1)} %convert_element_type.3.own_ref.refs_4_), channel_id=1, source_target_pairs={{0,8},{1,9},{2,10},{3,11},{4,12},{5,13},{6,14},{7,15},{8,0},{9,1},... | collective-permute-start | bytes 1572872 | tf_op jit(solution)/shard_map/ppermute | solution.py:272
  9.1 43.7 %collective-permute-start.17 = (bf16[128,2048]{1,0:T(8,128)(2,1)S(1)}, bf16[128,2048]{1,0:T(8,128)(2,1)S(1)}, u32[]{:S(2)}, u32[]{:S(2)}) collective-permute-start(bf16[128,2048]{1,0:T(8,128)(2,1)S(1)} %convert_element_type.3.own_ref.refs_4_), channel_id=1, source_target_pairs={{0,4},{1,5},{2,6},{3,7},{4,0},{5,1},{6,2},{7,3},{8,12},{9,13},{10,... | collective-permute-start | bytes 1572872 | tf_op jit(solution)/shard_map/ppermute | solution.py:272
  29.3 29.3 %collective-permute-start.3 = (bf16[128,2048]{1,0:T(8,128)(2,1)S(1)}, bf16[128,2048]{1,0:T(8,128)(2,1)S(1)}, u32[]{:S(2)}, u32[]{:S(2)}) collective-permute-start(bf16[128,2048]{1,0:T(8,128)(2,1)S(1)} %collective-permute-done.2.refs_4_), channel_id=1, source_target_pairs={{0,8},{1,9},{2,10},{3,11},{4,12},{5,13},{6,14},{7,15},{8,0},{9,1},... | collective-permute-start | bytes 1572872 | tf_op jit(solution)/shard_map/ppermute | solution.py:272
  30.0 27.3 %collective-permute-start.18 = (bf16[64,2048]{1,0:T(8,128)(2,1)S(1)}, bf16[64,2048]{1,0:T(8,128)(2,1)S(1)}, u32[]{:S(2)}, u32[]{:S(2)}) collective-permute-start(bf16[64,2048]{1,0:T(8,128)(2,1)S(1)} %slice.38), channel_id=1, source_target_pairs={{0,4},{1,5},{2,6},{3,7},{4,0},{5,1},{6,2},{7,3},{8,12},{9,13},{10,... | collective-permute-start | bytes 786440 | tf_op jit(solution)/shard_map/ppermute | solution.py:272
  31.6 28.5 %collective-permute-start.13 = (bf16[128,2048]{1,0:T(8,128)(2,1)S(1)}, bf16[128,2048]{1,0:T(8,128)(2,1)S(1)}, u32[]{:S(2)}, u32[]{:S(2)}) collective-permute-start(bf16[128,2048]{1,0:T(8,128)(2,1)S(1)} %collective-permute-done.12.refs_4_), channel_id=1, source_target_pairs={{0,1},{1,0},{2,3},{3,2},{4,5},{5,4},{6,7},{7,6},{8,9},{9,8},{10,11... | collective-permute-start | bytes 1572872 | tf_op jit(solution)/shard_map/ppermute | solution.py:272
  33.0 27.6 %collective-permute-start.14 = (bf16[128,2048]{1,0:T(8,128)(2,1)S(1)}, bf16[128,2048]{1,0:T(8,128)(2,1)S(1)}, u32[]{:S(2)}, u32[]{:S(2)}) collective-permute-start(bf16[128,2048]{1,0:T(8,128)(2,1)S(1)} %collective-permute-done.12.refs_4_), channel_id=1, source_target_pairs={{0,4},{1,5},{2,6},{3,7},{4,0},{5,1},{6,2},{7,3},{8,12},{9,13},{10,... | collective-permute-start | bytes 1572872 | tf_op jit(solution)/shard_map/ppermute | solution.py:272
  33.5 5.8 %copy-start = (bf16[4096,2048]{1,0:T(8,128)(2,1)S(1)}, bf16[4096,2048]{1,0:T(8,128)(2,1)}, u32[]{:S(2)}) copy-start(bf16[4096,2048]{1,0:T(8,128)(2,1)} %refs_3_.9) | copy-start | bytes 50331652
  39.3 0.7 copy-start.2
  40.0 0.7 copy-start.3
  52.8 3.7 %collective-permute-start.1 = (f32[8,256]{1,0:T(8,128)S(1)}, f32[8,256]{1,0:T(8,128)S(1)}, u32[]{:S(2)}, u32[]{:S(2)}) collective-permute-start(f32[8,256]{1,0:T(8,128)S(1)} %get-tuple-element.17.mine_ref), channel_id=1, source_target_pairs={{0,1},{1,0},{2,3},{3,2},{4,5},{5,4},{6,7},{7,6},{8,9},{9,8},{10,11... | collective-permute-start | bytes 24584 | tf_op jit(solution)/shard_map/ppermute | solution.py:272
  56.5 14.9 %collective-permute-start.8 = (bf16[128,2048]{1,0:T(8,128)(2,1)S(1)}, bf16[128,2048]{1,0:T(8,128)(2,1)S(1)}, u32[]{:S(2)}, u32[]{:S(2)}) collective-permute-start(bf16[128,2048]{1,0:T(8,128)(2,1)S(1)} %collective-permute-done.2.refs_4_), channel_id=1, source_target_pairs={{0,1},{1,0},{2,3},{3,2},{4,5},{5,4},{6,7},{7,6},{8,9},{9,8},{10,11... | collective-permute-start | bytes 1572872 | tf_op jit(solution)/shard_map/ppermute | solution.py:272
  57.3 15.6 %collective-permute-start.9 = (bf16[128,2048]{1,0:T(8,128)(2,1)S(1)}, bf16[128,2048]{1,0:T(8,128)(2,1)S(1)}, u32[]{:S(2)}, u32[]{:S(2)}) collective-permute-start(bf16[128,2048]{1,0:T(8,128)(2,1)S(1)} %collective-permute-done.2.refs_4_), channel_id=1, source_target_pairs={{0,4},{1,5},{2,6},{3,7},{4,0},{5,1},{6,2},{7,3},{8,12},{9,13},{10,... | collective-permute-start | bytes 1572872 | tf_op jit(solution)/shard_map/ppermute | solution.py:272
  58.6 74.7 %collective-permute-start.4 = (bf16[128,2048]{1,0:T(8,128)(2,1)S(1)}, bf16[128,2048]{1,0:T(8,128)(2,1)S(1)}, u32[]{:S(2)}, u32[]{:S(2)}) collective-permute-start(bf16[128,2048]{1,0:T(8,128)(2,1)S(1)} %collective-permute-done.3.refs_4_), channel_id=1, source_target_pairs={{0,1},{1,0},{2,3},{3,2},{4,5},{5,4},{6,7},{7,6},{8,9},{9,8},{10,11... | collective-permute-start | bytes 1572872 | tf_op jit(solution)/shard_map/ppermute | solution.py:272
  60.1 79.9 %collective-permute-start.5 = (bf16[128,2048]{1,0:T(8,128)(2,1)S(1)}, bf16[128,2048]{1,0:T(8,128)(2,1)S(1)}, u32[]{:S(2)}, u32[]{:S(2)}) collective-permute-start(bf16[128,2048]{1,0:T(8,128)(2,1)S(1)} %collective-permute-done.3.refs_4_), channel_id=1, source_target_pairs={{0,4},{1,5},{2,6},{3,7},{4,0},{5,1},{6,2},{7,3},{8,12},{9,13},{10,... | collective-permute-start | bytes 1572872 | tf_op jit(solution)/shard_map/ppermute | solution.py:272
  60.6 72.6 %collective-permute-start.19 = (bf16[64,2048]{1,0:T(8,128)(2,1)S(1)}, bf16[64,2048]{1,0:T(8,128)(2,1)S(1)}, u32[]{:S(2)}, u32[]{:S(2)}) collective-permute-start(bf16[64,2048]{1,0:T(8,128)(2,1)S(1)} %slice.39), channel_id=1, source_target_pairs={{0,1},{1,0},{2,3},{3,2},{4,5},{5,4},{6,7},{7,6},{8,9},{9,8},{10,11... | collective-permute-start | bytes 786440 | tf_op jit(solution)/shard_map/ppermute | solution.py:272
  71.4 70.6 %collective-permute-start.15 = (bf16[64,2048]{1,0:T(8,128)(2,1)S(1)}, bf16[64,2048]{1,0:T(8,128)(2,1)S(1)}, u32[]{:S(2)}, u32[]{:S(2)}) collective-permute-start(bf16[64,2048]{1,0:T(8,128)(2,1)S(1)} %slice.36), channel_id=1, source_target_pairs={{0,4},{1,5},{2,6},{3,7},{4,0},{5,1},{6,2},{7,3},{8,12},{9,13},{10,... | collective-permute-start | bytes 786440 | tf_op jit(solution)/shard_map/ppermute | solution.py:272
  72.9 69.8 %collective-permute-start.16 = (bf16[64,2048]{1,0:T(8,128)(2,1)S(1)}, bf16[64,2048]{1,0:T(8,128)(2,1)S(1)}, u32[]{:S(2)}, u32[]{:S(2)}) collective-permute-start(bf16[64,2048]{1,0:T(8,128)(2,1)S(1)} %slice.37), channel_id=1, source_target_pairs={{0,1},{1,0},{2,3},{3,2},{4,5},{5,4},{6,7},{7,6},{8,9},{9,8},{10,11... | collective-permute-start | bytes 786440 | tf_op jit(solution)/shard_map/ppermute | solution.py:272
  133.2 14.6 %collective-permute-start.10 = (bf16[64,2048]{1,0:T(8,128)(2,1)S(1)}, bf16[64,2048]{1,0:T(8,128)(2,1)S(1)}, u32[]{:S(2)}, u32[]{:S(2)}) collective-permute-start(bf16[64,2048]{1,0:T(8,128)(2,1)S(1)} %slice.34), channel_id=1, source_target_pairs={{0,4},{1,5},{2,6},{3,7},{4,0},{5,1},{6,2},{7,3},{8,12},{9,13},{10,... | collective-permute-start | bytes 786440 | tf_op jit(solution)/shard_map/ppermute | solution.py:272
  133.3 14.6 %collective-permute-start.11 = (bf16[64,2048]{1,0:T(8,128)(2,1)S(1)}, bf16[64,2048]{1,0:T(8,128)(2,1)S(1)}, u32[]{:S(2)}, u32[]{:S(2)}) collective-permute-start(bf16[64,2048]{1,0:T(8,128)(2,1)S(1)} %slice.35), channel_id=1, source_target_pairs={{0,1},{1,0},{2,3},{3,2},{4,5},{5,4},{6,7},{7,6},{8,9},{9,8},{10,11... | collective-permute-start | bytes 786440 | tf_op jit(solution)/shard_map/ppermute | solution.py:272
  140.0 13.1 %collective-permute-start.6 = (bf16[64,2048]{1,0:T(8,128)(2,1)S(1)}, bf16[64,2048]{1,0:T(8,128)(2,1)S(1)}, u32[]{:S(2)}, u32[]{:S(2)}) collective-permute-start(bf16[64,2048]{1,0:T(8,128)(2,1)S(1)} %slice.32), channel_id=1, source_target_pairs={{0,4},{1,5},{2,6},{3,7},{4,0},{5,1},{6,2},{7,3},{8,12},{9,13},{10,... | collective-permute-start | bytes 786440 | tf_op jit(solution)/shard_map/ppermute | solution.py:272
  142.0 11.1 %collective-permute-start.7 = (bf16[64,2048]{1,0:T(8,128)(2,1)S(1)}, bf16[64,2048]{1,0:T(8,128)(2,1)S(1)}, u32[]{:S(2)}, u32[]{:S(2)}) collective-permute-start(bf16[64,2048]{1,0:T(8,128)(2,1)S(1)} %slice.33), channel_id=1, source_target_pairs={{0,1},{1,0},{2,3},{3,2},{4,5},{5,4},{6,7},{7,6},{8,9},{9,8},{10,11... | collective-permute-start | bytes 786440 | tf_op jit(solution)/shard_map/ppermute | solution.py:272
  159.1 3.0 %collective-permute-start.20 = (bf16[256,2176]{1,0:T(8,128)(2,1)}, bf16[256,2176]{1,0:T(8,128)(2,1)S(1)}, u32[]{:S(2)}, u32[]{:S(2)}) collective-permute-start(bf16[256,2176]{1,0:T(8,128)(2,1)} %get-tuple-element.29), channel_id=1, source_target_pairs={{0,2},{1,3},{2,0},{3,1},{4,6},{5,7},{6,4},{7,5},{8,10},{9,11},{10,... | collective-permute-start | bytes 3342344 | tf_op jit(solution)/shard_map/ppermute | solution.py:272
  162.1 5.8 %copy-start.1 = (bf16[4096,2048]{1,0:T(8,128)(2,1)S(1)}, bf16[4096,2048]{1,0:T(8,128)(2,1)}, u32[]{:S(2)}) copy-start(bf16[4096,2048]{1,0:T(8,128)(2,1)} %refs_3_.9) | copy-start | bytes 50331652

commit v2 on v0

v2 whole, which is shorter than its diff:
```python
import functools

import jax
import jax.numpy as jnp
from jax import lax
from jax.experimental import pallas as pl
from jax.experimental.pallas import tpu as pltpu
from jax.sharding import PartitionSpec as P

prior_weight = 1.0
very_low = -1e30
both = ("img", "ori")
lanes = 128
cores = 2
vmem = pl.BlockSpec(memory_space=pltpu.VMEM)
smem = pl.BlockSpec(memory_space=pltpu.SMEM)
contract_last = (((1,), (1,)), ((), ()))


def weighted_sums(weights, rows_block):
    return lax.dot_general(
        weights, rows_block, (((0,), (0,)), ((), ())), preferred_element_type=jnp.float32
    )


def reduced_body(images, precision, projections, tile_mask):
    lowered = images.astype(jnp.bfloat16)
    grouped = lax.all_gather(lowered, "ori", axis=0, tiled=True)
    proj_float = projections.astype(jnp.float32)
    squared = jnp.sum(proj_float * proj_float, axis=1)
    blocks, tiles_here = tile_mask.shape
    per_block = grouped.shape[0] // blocks
    tile_width = projections.shape[0] // tiles_here
    columns = grouped.shape[1]
    products = lax.dot_general(
        grouped, projections, contract_last, preferred_element_type=jnp.float32
    )
    scores = precision[:, None] * (products - 0.5 * squared[None, :])
    shaped = scores.reshape(blocks, per_block, tiles_here, tile_width)
    alive = jnp.broadcast_to((tile_mask > 0)[:, None, :, None], shaped.shape)
    masked = jnp.where(alive, shaped, very_low)
    local_high = jnp.max(masked, axis=(2, 3))
    row_high = lax.pmax(local_high, "ori")
    lifted = jnp.where(alive, jnp.exp(masked - row_high[:, :, None, None]), 0.0)
    row_total = lax.psum(jnp.sum(lifted, axis=(2, 3)), "ori")
    probable = lifted / row_total[:, :, None, None]
    posteriors = probable.reshape(scores.shape).astype(jnp.bfloat16)
    counts = jnp.sum(posteriors.astype(jnp.float32), axis=0)
    half_width = columns // 2
    halves = [
        lax.psum_scatter(
            weighted_sums(posteriors, part).astype(jnp.bfloat16),
            "img",
            scatter_dimension=0,
            tiled=True,
        ).astype(jnp.float32)
        for part in (grouped[:, :half_width], grouped[:, half_width:])
    ]
    totals = lax.psum_scatter(
        counts.astype(jnp.bfloat16), "img", scatter_dimension=0, tiled=True
    ).astype(jnp.float32)
    summed = jnp.concatenate(halves, axis=1)
    rows_here = summed.shape[0]
    first_row = lax.axis_index("img") * rows_here
    prior_rows = lax.dynamic_slice_in_dim(proj_float, first_row, rows_here, 0)
    refined = (summed + prior_weight * prior_rows) / (totals[:, None] + prior_weight)
    return (posteriors, refined)


def as_row(column):
    return jnp.transpose(jnp.broadcast_to(column, (column.shape[0], lanes)))[0:1, :]


def as_column(row):
    return jnp.transpose(jnp.broadcast_to(row, (lanes, row.shape[1])))[:, 0:1]


def load_kernel(chips, away_ref, proj_ref, mine_ref, row_ref, col_ref, sems):
    width = proj_ref.shape[0] // chips
    chip = lax.axis_index("img") // cores

    def copy(i):
        rows = pl.ds(pl.multiple_of(i * width, width), width)
        return pltpu.make_async_copy(away_ref.at[rows], proj_ref.at[rows], sems.at[i])

    for i in range(chips):
        copy(i).start()
    mine = pltpu.make_async_copy(
        away_ref.at[pl.ds(pl.multiple_of(chip * width, width), width)], mine_ref, sems.at[chips]
    )
    mine.start()

    @pl.loop(0, chips)
    def _(i):
        copy(i).wait()
        here = pl.ds(pl.multiple_of(i * width, width), width)
        wide = proj_ref[here, :].astype(jnp.float32)
        half = 0.5 * jnp.sum(wide * wide, axis=1, keepdims=True)
        half_wide = jnp.broadcast_to(half, (width, lanes))
        row_ref[:, here] = jnp.transpose(half_wide)[0:8, :]

        @pl.when(i == chip)
        def _():
            col_ref[...] = half_wide

    mine.wait()


def scores_kernel(
    chips, mask_s, prec_ref, half_ref, own_ref, first_ref, second_ref, proj_ref, scores_ref, stats_ref,
    rows_buf,
):
    here = lax.axis_index("ori")
    core = lax.rem(lax.axis_index("img"), cores)
    shard = own_ref.shape[0]
    blocks, tiles = mask_s.shape
    width = proj_ref.shape[0] // chips
    tiles_here = tiles // chips
    tile = width // tiles_here
    rows_buf[pl.ds(pl.multiple_of(here * shard, shard), shard), :] = own_ref[...]
    there = pl.ds(pl.multiple_of((1 - here) * shard, shard), shard)

    @pl.when(core == 0)
    def _():
        rows_buf[there, :] = first_ref[...]

    @pl.when(core != 0)
    def _():
        rows_buf[there, :] = second_ref[...]

    prec_col = as_column(prec_ref[...])
    high = [jnp.full((shard, lanes), very_low, jnp.float32)] * blocks
    total = [jnp.zeros((shard, lanes), jnp.float32)] * blocks
    for step in range(chips):
        where = slice(step * width, (step + 1) * width)
        products = lax.dot_general(
            rows_buf[...], proj_ref[where, :], contract_last, preferred_element_type=jnp.float32
        )
        scores = prec_col * (products - half_ref[0:1, where])
        for b in range(blocks):
            rows = slice(b * shard, (b + 1) * shard)
            parts = []
            for t in range(tiles_here):
                at = step * width + t * tile
                alive = mask_s[b, step * tiles_here + t] > 0
                kept = jnp.where(alive, scores[rows, t * tile : (t + 1) * tile], very_low)
                scores_ref[rows, at : at + tile] = kept
                parts += [kept[:, c : c + lanes] for c in range(0, tile, lanes)]
            now = functools.reduce(jnp.maximum, parts, high[b])
            added = functools.reduce(jnp.add, [jnp.exp(part - now) for part in parts])
            total[b] = total[b] * jnp.exp(high[b] - now) + added
            high[b] = now
    for b in range(blocks):
        rows = slice(b * shard, (b + 1) * shard)
        top = jnp.max(high[b], axis=1, keepdims=True)
        mass = jnp.sum(total[b] * jnp.exp(high[b] - top), axis=1, keepdims=True)
        stats_ref[0:1, rows] = as_row(top)
        stats_ref[1:2, rows] = as_row(mass)
    stats_ref[2:8, :] = jnp.zeros((6, stats_ref.shape[1]), jnp.float32)


def joined(mine_ref, theirs_ref):
    top = jnp.maximum(mine_ref[0:1, :], theirs_ref[0:1, :])
    mass = mine_ref[1:2, :] * jnp.exp(mine_ref[0:1, :] - top) + theirs_ref[
        1:2, :
    ] * jnp.exp(theirs_ref[0:1, :] - top)
    return top, 1.0 / mass


def meta_kernel(mask_s, prec_ref, mine_ref, theirs_ref, meta_ref):
    top, share = joined(mine_ref, theirs_ref)
    parts, _, shard = meta_ref.shape
    tiles = mask_s.shape[1]
    for b in range(parts):
        columns = slice(b * shard, (b + 1) * shard)
        floor = -top[:, columns]
        for t in range(tiles):
            meta_ref[b, t : t + 1, :] = jnp.where(mask_s[b, t] > 0, floor, very_low)
        meta_ref[b, tiles : tiles + 1, :] = share[:, columns]
        meta_ref[b, tiles + 1 : tiles + 2, :] = prec_ref[:, columns]
        meta_ref[b, tiles + 2 : tiles + 8, :] = jnp.zeros((6, shard), jnp.float32)


def posterior_kernel(scores_ref, mine_ref, theirs_ref, post_ref):
    top, share = joined(mine_ref, theirs_ref)
    n = post_ref.shape[1]
    here = pl.ds(pl.multiple_of(pl.program_id(0) * n, n), n)
    post_ref[...] = (
        jnp.exp(scores_ref[:, here] - as_column(top)) * as_column(share)
    ).astype(post_ref.dtype)


def sums_kernel(n_metas, shapes, first, last, *refs):
    half_ref, proj_ref = refs[:2]
    metas, refs = refs[2 : 2 + n_metas], refs[2 + n_metas :]
    pieces, refs = refs[: len(shapes)], refs[len(shapes) :]
    if not first:
        acc_ref, cnt_ref = refs[:2]
        refs = refs[2:]
    n_outs = 3 if last else 2
    outs, (rows_buf, weights_buf, seen_buf) = refs[:n_outs], refs[n_outs:]
    img, ori = lax.axis_index("img"), lax.axis_index("ori")
    chip, core = img // cores, lax.rem(img, cores)
    width, columns = proj_ref.shape
    n_ori = lax.axis_size("ori")
    per_meta, tiles, shard = metas[0].shape
    tiles -= 8
    tiles_here = tiles * cores // lax.axis_size("img")
    tile = width // tiles_here
    seen = jnp.zeros((width, shard), jnp.float32)

    def meta_row(at, row):
        def read(d):
            which, inner = divmod(d[0] * n_ori, per_meta)
            return metas[which][inner + (ori ^ d[1]), pl.ds(row, 1), :]

        if at[0] == at[1]:
            return read(at[0])
        return jnp.where(core == 0, read(at[0]), read(at[1]))

    done = 0
    for piece, shards in zip(pieces, shapes, strict=True):
        n = piece.shape[0]
        rows_buf[done : done + n, :] = piece[...]
        done += n
    products = lax.dot_general(
        proj_ref[...], rows_buf[...], contract_last, preferred_element_type=jnp.float32
    )
    for b, at in enumerate(sum(shapes, ())):
        here = slice(b * shard, (b + 1) * shard)
        mine = meta_row(at, tiles + 1) * (products[:, here] - half_ref[...])
        share = meta_row(at, tiles)
        for t in range(tiles_here):
            down = slice(t * tile, (t + 1) * tile)
            floor = meta_row(at, chip * tiles_here + t)
            weights_buf[down, here] = (jnp.exp(mine[down, :] + floor) * share).astype(
                jnp.bfloat16
            )
        seen += weights_buf[:, here].astype(jnp.float32)
    if not first:
        seen += cnt_ref[...]
    if last:
        kept_ref, kept_cnt_ref, sent_ref = outs
        half_width = width // 2
        keep = pl.ds(pl.multiple_of(core * half_width, half_width), half_width)
        send = pl.ds(pl.multiple_of((1 - core) * half_width, half_width), half_width)
        seen_buf[...] = jnp.broadcast_to(jnp.sum(seen, axis=1, keepdims=True), seen.shape)
        kept_cnt_ref[...] = seen_buf[keep, :]
        sent_ref[:, columns:] = seen_buf[send, :].astype(jnp.bfloat16)
        targets = ((send, sent_ref), (keep, kept_ref))
    else:
        outs[1][...] = seen
        targets = ((pl.ds(0, width), outs[0]),)
    chunk = min(columns, 512)
    for where, out in targets:
        for c in range(0, columns, chunk):
            part = slice(c, c + chunk)
            sums = lax.dot_general(
                weights_buf[where, :],
                rows_buf[:, part],
                (((1,), (0,)), ((), ())),
                preferred_element_type=jnp.float32,
            )
            if not first:
                sums += acc_ref[where, part]
            out[:, part] = sums.astype(out.dtype)


def final_kernel(kept_ref, kept_cnt_ref, got_ref, proj_ref, out_ref):
    rows, columns = out_ref.shape
    core = lax.rem(lax.axis_index("img"), cores)
    first_row = (core * pl.num_programs(0) + pl.program_id(0)) * rows
    counts = kept_cnt_ref[:, 0:1] + got_ref[:, columns : columns + 1].astype(jnp.float32)
    sums = kept_ref[...] + got_ref[:, :columns].astype(jnp.float32)
    prior = prior_weight * proj_ref[pl.ds(pl.multiple_of(first_row, rows), rows), :].astype(
        jnp.float32
    )
    out_ref[...] = (sums + prior) * (1.0 / (counts + prior_weight))


def gathered_body(n_img, n_ori, images, precision, projections, tile_mask):
    n = n_img * n_ori
    shard, columns = images.shape
    orient = projections.shape[0]
    chips = n_img // cores
    width = orient // chips
    blocks, tiles = tile_mask.shape
    f32 = jnp.float32
    limit = pltpu.CompilerParams(vmem_limit_bytes=14 * 2**20)

    def swap(a, even, odd=None):
        masks = [d[0] * cores * n_ori + d[1] for d in (even, odd or even)]
        return lax.ppermute(a, both, [(i, i ^ masks[i // n_ori % cores]) for i in range(n)])

    def moved(shards, even, odd=None):
        odd = odd or even
        return tuple(
            ((e[0] ^ even[0], e[1] ^ even[1]), (o[0] ^ odd[0], o[1] ^ odd[1])) for e, o in shards
        )

    x, y = (0, 1), (1, 0)
    near, far = (x, y), (y, x)

    def sent(piece, even, odd=None):
        return moved(piece[0], even, odd), swap(piece[1], even, odd)

    def together(values):
        leaves, tree = jax.tree.flatten(values)
        arrays = iter(lax.optimization_barrier([a for a in leaves if not isinstance(a, int)]))
        return tree.unflatten([a if isinstance(a, int) else next(arrays) for a in leaves])

    lowered = images.astype(jnp.bfloat16)
    own = ((((0, 0), (0, 0)),), lowered)
    near_slab, far_slab = sent(own, (2, 0)), sent(own, (4, 0))
    own_a, own_b = sent(own, *near), sent(own, *far)

    prec_row = precision.reshape(1, -1)
    rows = prec_row.shape[1]
    held, held_chip, half_row, half_col = pl.pallas_call(
        functools.partial(load_kernel, chips),
        in_specs=[pl.BlockSpec(memory_space=pltpu.HBM)],
        out_specs=[vmem] * 4,
        out_shape=[
            pltpu.VMEM(projections.shape, projections.dtype),
            jax.ShapeDtypeStruct((width, columns), projections.dtype),
            jax.ShapeDtypeStruct((8, orient), f32),
            jax.ShapeDtypeStruct((width, lanes), f32),
        ],
        scratch_shapes=[pltpu.SemaphoreType.DMA((chips + 1,))],
        compiler_params=limit,
        cost_estimate=pl.CostEstimate(flops=0, bytes_accessed=0, transcendentals=0),
        name="load",
    )(pltpu.with_memory_space_constraint(projections, pltpu.HBM))
    held = pltpu.with_memory_space_constraint(held, pltpu.VMEM)
    own_a, own_b, held_chip, half_row, half_col = together(
        (own_a, own_b, held_chip, half_row, half_col)
    )
    own_c = sent(own_a, *far)
    whole = lambda i: (0, 0)
    scores, stats = pl.pallas_call(
        functools.partial(scores_kernel, chips),
        in_specs=[smem] + [vmem] * 6,
        out_specs=[vmem] * 2,
        out_shape=[
            pltpu.VMEM((rows, orient), f32),
            jax.ShapeDtypeStruct((8, rows), f32),
        ],
        scratch_shapes=[pltpu.VMEM((rows, columns), jnp.bfloat16)],
        compiler_params=limit,
        cost_estimate=pl.CostEstimate(flops=0, bytes_accessed=0, transcendentals=0),
        name="scores",
    )(tile_mask, prec_row, half_row, lowered, own_a[1], own_b[1], held)
    theirs = swap(stats, x)
    meta = pl.pallas_call(
        meta_kernel,
        in_specs=[smem, vmem, vmem, vmem],
        out_specs=vmem,
        out_shape=jax.ShapeDtypeStruct((n_ori, tiles + 8, shard), f32),
        compiler_params=limit,
        cost_estimate=pl.CostEstimate(flops=0, bytes_accessed=0, transcendentals=0),
        name="meta",
    )(tile_mask, prec_row, stats, theirs)
    close = [swap(meta, (d, 0)) for d in (1, 2, 3)]
    far_slab, near_slab, own_c, meta, scores = together(
        (far_slab, near_slab, own_c, meta, scores)
    )
    last_slab = sent(far_slab, (2, 0))
    far_a = sent(far_slab, *near)
    cut = 4
    posteriors = pl.pallas_call(
        posterior_kernel,
        grid=(cut,),
        in_specs=[
            vmem,
            pl.BlockSpec((8, rows), whole),
            pl.BlockSpec((8, rows), whole),
        ],
        out_specs=pl.BlockSpec((rows, orient // cut), lambda i: (0, i)),
        out_shape=jax.ShapeDtypeStruct((rows, orient), jnp.bfloat16),
        compiler_params=limit,
        cost_estimate=pl.CostEstimate(flops=0, bytes_accessed=0, transcendentals=0),
        name="posterior",
    )(scores, stats, theirs)

    close, posteriors, far_slab, near_slab = together(
        (close, posteriors, far_slab, near_slab)
    )
    far_b = sent(far_slab, *far)
    near_a = sent(near_slab, *near)
    metas = jnp.concatenate([meta, *close], axis=0)
    metas = [metas, swap(metas, (4, 0))]
    near_b = sent(own_b, (2, 0))
    far_a, far_b, last_slab = together((far_a, far_b, last_slab))
    far_c = sent(far_a, *far)
    last_a, last_b = sent(last_slab, *near), sent(last_slab, *far)

    def add(group, state, last):
        shapes = tuple(shards for shards, _ in group)
        pieces = [a for _, a in group]
        images_here = sum(a.shape[0] for a in pieces)
        first = state is None
        if last:
            out_shape = [
                jax.ShapeDtypeStruct((width // 2, columns), f32),
                jax.ShapeDtypeStruct((width // 2, lanes), f32),
                jax.ShapeDtypeStruct((width // 2, columns + lanes), jnp.bfloat16),
            ]
        else:
            out_shape = [
                jax.ShapeDtypeStruct((width, columns), f32),
                jax.ShapeDtypeStruct((width, lanes), f32),
            ]
        n_ins = 2 + len(metas) + len(pieces) + (0 if first else 2)
        return pl.pallas_call(
            functools.partial(sums_kernel, len(metas), shapes, first, last),
            in_specs=[vmem] * n_ins,
            out_specs=[vmem] * len(out_shape),
            out_shape=out_shape,
            input_output_aliases={} if first or last else {n_ins - 2: 0, n_ins - 1: 1},
            scratch_shapes=[
                pltpu.VMEM((images_here, columns), jnp.bfloat16),
                pltpu.VMEM((width, images_here), jnp.bfloat16),
                pltpu.VMEM((width, lanes), f32),
            ],
            compiler_params=limit,
        cost_estimate=pl.CostEstimate(flops=0, bytes_accessed=0, transcendentals=0),
            name="sums",
        )(half_col, held_chip, *metas, *pieces, *(state or ()))

    state = add([own, own_a, own_b, own_c], None, False)
    state = add([near_slab, far_slab, far_a, far_b], state, False)
    state, far_c, own_c = together((state, far_c, own_c))
    near_c = sent(own_c, (2, 0))
    state = add([near_a, far_c, last_slab], state, False)
    state, last_a = together((state, last_a))
    last_c = sent(last_a, *far)
    state = add([last_a, last_b, near_b], state, False)
    kept, kept_cnt, sent_away = add([near_c, last_c], state, True)
    got = lax.ppermute(sent_away, both, [(i, i ^ n_ori) for i in range(n)])
    out_rows = width // 2
    cut = 4
    refined = pl.pallas_call(
        final_kernel,
        grid=(cut,),
        in_specs=[
            pl.BlockSpec((out_rows // cut, columns), lambda i: (i, 0)),
            pl.BlockSpec((out_rows // cut, lanes), lambda i: (i, 0)),
            pl.BlockSpec((out_rows // cut, columns + lanes), lambda i: (i, 0)),
            vmem,
        ],
        out_specs=pl.BlockSpec((out_rows // cut, columns), lambda i: (i, 0)),
        out_shape=jax.ShapeDtypeStruct((out_rows, columns), f32),
        compiler_params=limit,
        cost_estimate=pl.CostEstimate(flops=0, bytes_accessed=0, transcendentals=0),
        name="final",
    )(kept, kept_cnt, got, held_chip)
    return posteriors, refined


def solution(mesh):
    n_img, n_ori = mesh.shape["img"], mesh.shape["ori"]

    def body(images, precision, projections, tile_mask):
        shard, columns = images.shape
        orient = projections.shape[0]
        blocks, tiles = tile_mask.shape
        gathered_bytes = 2 * images.size * n_img * n_ori // cores
        fits = (
            n_ori == 2
            and n_img == 8 * cores
            and blocks == n_ori
            and shard % lanes == 0
            and tiles * cores % n_img == 0
            and orient % (tiles * lanes) == 0
            and gathered_bytes <= 16 * 2**20
        )
        if fits:
            return gathered_body(n_img, n_ori, images, precision, projections, tile_mask)
        return reduced_body(images, precision, projections, tile_mask)

    return jax.shard_map(
        body,
        mesh=mesh,
        in_specs=(P(("img", "ori"), None), P("img"), P("ori", None), P("img", "ori")),
        out_specs=(P("img", "ori"), P(("ori", "img"), None)),
        check_vma=False,
    )
```

time: 295 us -> 89 us (0.30)
  waiting for transfers between devices: 168 us -> 28.9 us
  blocking collectives: 44 us -> 0 us
  other arithmetic: 40.8 us -> 1.29 us
  Pallas kernels: 0 us -> 30.9 us
  starting transfers between devices: 0.12 us -> 26.9 us
  matrix products: 24.3 us -> 0 us
  between operations: 14.5 us -> 0.78 us
    reduce_scatter x2 -> x0, waiting for transfers between devices: 151 us -> none  [the longest x1 108 us: body(): lax.psum_scatter(weighted_sums(posteriors, grouped[:, :half_width]).astyp...]
    unnamed x1 -> x0, blocking collectives: 34 us -> none
    pallas_call x0 -> x10, Pallas kernels: none -> 30.9 us  [the longest x5 13.3 us: add(): pl.pallas_call(functools.partial(sums_kernel, len(metas), shapes, first,...]
    ppermute x0 -> x21, waiting for transfers between devices: none -> 28.9 us  [the longest x20 26.2 us: swap(): lax.ppermute(a, both, [(i, i ^ masks[i // n_ori % cores]) for i in range(...]
    ppermute x0 -> x21, starting transfers between devices: none -> 26.9 us  [the longest x20 26.8 us: swap(): lax.ppermute(a, both, [(i, i ^ masks[i // n_ori % cores]) for i in range(...]
    dot_general x3 -> x0, matrix products: 24.3 us -> none  [the longest x1 13.1 us: body(): lax.dot_general(grouped, projections, (((1,), (1,)), ((), ())), preferred...]
    convert_element_type x2 -> x1, other arithmetic: 22.1 us -> 1.29 us  [gathered_body(): lowered = images.astype(jnp.bfloat16)]
    all_gather x1 -> x0, waiting for transfers between devices: 16.9 us -> none  [body(): grouped = lax.all_gather(lowered, 'ori', axis=0, tiled=True)]
  transfers between devices with their start and end apart: 3 -> 21, of which waited for: 3 -> 8; matrix products, arithmetic and copies ran while one was open for 12% -> 0% of each run, Pallas kernels for 0% -> 30%
where the time goes in v2:
time: 89 us; the launch traced here: 88.8 us
  Pallas kernels  30.9 us (35%)
  waiting for transfers between devices  28.9 us (32%)
  starting transfers between devices  26.9 us (30%)
  other arithmetic  1.29 us (1%)
    ppermute x20, starting transfers between devices, swap(): lax.ppermute(a, both, [(i, i ^ masks[i // n_ori % cores]) for i in range(...  26.8 us
    ppermute x20, waiting for transfers between devices, swap(): lax.ppermute(a, both, [(i, i ^ masks[i // n_ori % cores]) for i in range(...  26.2 us
    pallas_call x5, Pallas kernels, add(): pl.pallas_call(functools.partial(sums_kernel, len(metas), shapes, first,...  13.3 us
    pallas_call x1, Pallas kernels, gathered_body(): pl.pallas_call(functools.partial(load_kernel, chips), in_specs=[pl.BlockS...  6.53 us
    pallas_call x1, Pallas kernels, gathered_body(): pl.pallas_call(functools.partial(scores_kernel, chips), in_specs=[smem] +...  5.83 us
    ppermute x1, waiting for transfers between devices, gathered_body(): got = lax.ppermute(sent_away, both, [(i, i ^ n_ori) for i in range(n)])  2.74 us
    pallas_call x1, Pallas kernels, gathered_body(): pl.pallas_call(posterior_kernel, grid=(cut,), in_specs=[vmem, pl.BlockSpe...  2.62 us
    pallas_call x1, Pallas kernels, gathered_body(): pl.pallas_call(final_kernel, grid=(cut,), in_specs=[pl.BlockSpec((out_row...  1.98 us
  transfers between devices with their start and end apart: 21, of which 8 were waited for; matrix products, arithmetic and copies ran while one was open for 0% of the time, Pallas kernels for 30%

profile of v2, /device:TPU:0, one launch (start us, length us, event | category | flops | bytes accessed | tf_op | source)
XLA Modules:
  0.0 88.8 jit_solution(8600628131372432679)
XLA Ops:
  0.6 1.3 %convert_element_type.3.own_ref.refs_4_ = bf16[128,2048]{1,0:T(8,128)(2,1)S(1)} convert(f32[128,2048]{1,0:T(8,128)} %param.4) | non-fusion elementwise | flops 262144 | bytes 1572864 | tf_op jit(solution)/shard_map/convert_element_type | solution.py:312
  1.9 0.0 copy-start
  1.9 0.0 copy-start.1
  1.9 3.0 %collective-permute-start = (bf16[128,2048]{1,0:T(8,128)(2,1)S(1)}, bf16[128,2048]{1,0:T(8,128)(2,1)S(1)}, u32[]{:S(2)}, u32[]{:S(2)}) collective-permute-start(bf16[128,2048]{1,0:T(8,128)(2,1)S(1)} %convert_element_type.3.own_ref.refs_4_), channel_id=1, source_target_pairs={{0,1},{1,0},{2,6},{3,7},{4,5},{5,4},{6,2},{7,3},{8,9},{9,8},{10,14... | collective-permute-start | bytes 1572872 | tf_op jit(solution)/shard_map/ppermute | solution.py:293
  5.0 1.5 %collective-permute-start.1 = (bf16[128,2048]{1,0:T(8,128)(2,1)S(1)}, bf16[128,2048]{1,0:T(8,128)(2,1)S(1)}, u32[]{:S(2)}, u32[]{:S(2)}) collective-permute-start(bf16[128,2048]{1,0:T(8,128)(2,1)S(1)} %convert_element_type.3.own_ref.refs_4_), channel_id=1, source_target_pairs={{0,4},{1,5},{2,3},{3,2},{4,0},{5,1},{6,7},{7,6},{8,12},{9,13},{10,... | collective-permute-start | bytes 1572872 | tf_op jit(solution)/shard_map/ppermute | solution.py:293
  6.5 2.6 %collective-permute-start.6 = (bf16[128,2048]{1,0:T(8,128)(2,1)S(1)}, bf16[128,2048]{1,0:T(8,128)(2,1)S(1)}, u32[]{:S(2)}, u32[]{:S(2)}) collective-permute-start(bf16[128,2048]{1,0:T(8,128)(2,1)S(1)} %convert_element_type.3.own_ref.refs_4_), channel_id=1, source_target_pairs={{0,16},{1,17},{2,18},{3,19},{4,20},{5,21},{6,22},{7,23},{8,24},{9,... | collective-permute-start | bytes 1572872 | tf_op jit(solution)/shard_map/ppermute | solution.py:293
  9.1 1.6 %collective-permute-start.7 = (bf16[128,2048]{1,0:T(8,128)(2,1)S(1)}, bf16[128,2048]{1,0:T(8,128)(2,1)S(1)}, u32[]{:S(2)}, u32[]{:S(2)}) collective-permute-start(bf16[128,2048]{1,0:T(8,128)(2,1)S(1)} %convert_element_type.3.own_ref.refs_4_), channel_id=1, source_target_pairs={{0,8},{1,9},{2,10},{3,11},{4,12},{5,13},{6,14},{7,15},{8,0},{9,1},... | collective-permute-start | bytes 1572872 | tf_op jit(solution)/shard_map/ppermute | solution.py:293
  10.6 6.5 %load.1 = (bf16[4096,2048]{1,0:T(8,128)(2,1)S(1)}, bf16[512,2048]{1,0:T(8,128)(2,1)S(1)}, f32[8,4096]{1,0:T(8,128)S(1)}, f32[512,128]{1,0:T(8,128)S(1)}) custom-call(bf16[4096,2048]{1,0:T(8,128)(2,1)} %away_ref.1), custom_call_target="tpu_custom_call" | custom-call | tf_op jit(solution)/shard_map/load/pallas_call | solution.py:319
  17.2 0.0 collective-permute-done.first_ref.refs_5_
  17.2 0.0 collective-permute-done.1.second_ref.refs_6_
  17.2 1.5 %collective-permute-start.8 = (bf16[128,2048]{1,0:T(8,128)(2,1)S(1)}, bf16[128,2048]{1,0:T(8,128)(2,1)S(1)}, u32[]{:S(2)}, u32[]{:S(2)}) collective-permute-start(bf16[128,2048]{1,0:T(8,128)(2,1)S(1)} %collective-permute-done.first_ref.refs_5_), channel_id=1, source_target_pairs={{0,4},{1,5},{2,3},{3,2},{4,0},{5,1},{6,7},{7,6},{8,12},{9,13},{10,... | collective-permute-start | bytes 1572872 | tf_op jit(solution)/shard_map/ppermute | solution.py:293
  18.7 0.0 copy-done
  18.7 0.0 copy-done.1
  18.7 5.8 %scores.1 = (f32[256,4096]{1,0:T(8,128)S(1)}, f32[8,256]{1,0:T(8,128)S(1)}) custom-call(s32[2,32]{1,0:T(2,128)S(1)} %copy-done, f32[1,256]{1,0:T(1,128)S(1)} %bitcast.1, f32[8,4096]{1,0:T(8,128)S(1)} %get-tuple-element.48.half_ref, bf16[128,2048]{1,0:T(8,128)(2,1)S(1)} %convert_element_type.3.own_ref.refs_4_, ...), custom_call_target="tpu_custom_call" | custom-call | tf_op jit(solution)/shard_map/scores/pallas_call | solution.py:340
  24.6 1.7 %collective-permute-start.2 = (f32[8,256]{1,0:T(8,128)S(1)}, f32[8,256]{1,0:T(8,128)S(1)}, u32[]{:S(2)}, u32[]{:S(2)}) collective-permute-start(f32[8,256]{1,0:T(8,128)S(1)} %get-tuple-element.52.mine_ref), channel_id=1, source_target_pairs={{0,1},{1,0},{2,3},{3,2},{4,5},{5,4},{6,7},{7,6},{8,9},{9,8},{10,11... | collective-permute-start | bytes 24584 | tf_op jit(solution)/shard_map/ppermute | solution.py:293
  26.2 2.0 %collective-permute-done.2.theirs_ref = f32[8,256]{1,0:T(8,128)S(1)} collective-permute-done((f32[8,256]{1,0:T(8,128)S(1)}, f32[8,256]{1,0:T(8,128)S(1)}, u32[]{:S(2)}, u32[]{:S(2)}) %collective-permute-start.2) | collective-permute-done | bytes 8224 | tf_op jit(solution)/shard_map/ppermute | solution.py:293
  28.3 0.6 meta.1
  28.9 1.0 %collective-permute-start.3 = (f32[2,40,128]{2,1,0:T(8,128)S(1)}, f32[2,40,128]{2,1,0:T(8,128)S(1)}, u32[]{:S(2)}, u32[]{:S(2)}) collective-permute-start(f32[2,40,128]{2,1,0:T(8,128)S(1)} %meta.1), channel_id=1, source_target_pairs={{0,4},{1,5},{2,6},{3,7},{4,0},{5,1},{6,2},{7,3},{8,12},{9,13},{10,... | collective-permute-start | bytes 122888 | tf_op jit(solution)/shard_map/ppermute | solution.py:293
  29.9 2.1 %collective-permute-start.4 = (f32[2,40,128]{2,1,0:T(8,128)S(1)}, f32[2,40,128]{2,1,0:T(8,128)S(1)}, u32[]{:S(2)}, u32[]{:S(2)}) collective-permute-start(f32[2,40,128]{2,1,0:T(8,128)S(1)} %meta.1), channel_id=1, source_target_pairs={{0,8},{1,9},{2,10},{3,11},{4,12},{5,13},{6,14},{7,15},{8,0},{9,1},... | collective-permute-start | bytes 122888 | tf_op jit(solution)/shard_map/ppermute | solution.py:293
  32.0 0.0 collective-permute-done.6.refs_5_
  32.0 0.5 collective-permute-start.5
  32.4 0.0 collective-permute-done.7.refs_4_
  32.5 0.0 collective-permute-done.8.refs_7_
  32.5 2.6 %posterior.1 = bf16[256,4096]{1,0:T(8,128)(2,1)} custom-call(f32[256,4096]{1,0:T(8,128)S(1)} %get-tuple-element.54.scores_ref, f32[8,256]{1,0:T(8,128)S(1)} %get-tuple-element.52.mine_ref, f32[8,256]{1,0:T(8,128)S(1)} %collective-permute-done.2.theirs_ref), custom_call_target="tpu_custom_call" | custom-call | tf_op jit(solution)/shard_map/posterior/pallas_call | solution.py:370
  35.1 0.0 collective-permute-done.3
  35.1 0.0 collective-permute-done.4
  35.1 1.8 %collective-permute-done.5 = f32[2,40,128]{2,1,0:T(8,128)S(1)} collective-permute-done((f32[2,40,128]{2,1,0:T(8,128)S(1)}, f32[2,40,128]{2,1,0:T(8,128)S(1)}, u32[]{:S(2)}, u32[]{:S(2)}) %collective-permute-start.5) | collective-permute-done | bytes 40992 | tf_op jit(solution)/shard_map/ppermute | solution.py:293
  36.9 0.7 collective-permute-start.11
  37.6 1.5 %collective-permute-start.10 = (bf16[128,2048]{1,0:T(8,128)(2,1)S(1)}, bf16[128,2048]{1,0:T(8,128)(2,1)S(1)}, u32[]{:S(2)}, u32[]{:S(2)}) collective-permute-start(bf16[128,2048]{1,0:T(8,128)(2,1)S(1)} %collective-permute-done.6.refs_5_), channel_id=1, source_target_pairs={{0,1},{1,0},{2,6},{3,7},{4,5},{5,4},{6,2},{7,3},{8,9},{9,8},{10,14... | collective-permute-start | bytes 1572872 | tf_op jit(solution)/shard_map/ppermute | solution.py:293
  39.1 0.5 collective-permute-start.12
  39.6 0.5 collective-permute-start.15
  40.2 11.6 %collective-permute-done.11.refs_7_ = bf16[128,2048]{1,0:T(8,128)(2,1)S(1)} collective-permute-done((bf16[128,2048]{1,0:T(8,128)(2,1)S(1)}, bf16[128,2048]{1,0:T(8,128)(2,1)S(1)}, u32[]{:S(2)}, u32[]{:S(2)}) %collective-permute-start.11) | collective-permute-done | bytes 524320 | tf_op jit(solution)/shard_map/ppermute | solution.py:293
  51.7 0.0 collective-permute-done.10.refs_6_
  51.7 0.0 collective-permute-done.12.refs_6_
  51.7 0.7 collective-permute-start.13
  52.5 1.5 %collective-permute-start.16 = (bf16[128,2048]{1,0:T(8,128)(2,1)S(1)}, bf16[128,2048]{1,0:T(8,128)(2,1)S(1)}, u32[]{:S(2)}, u32[]{:S(2)}) collective-permute-start(bf16[128,2048]{1,0:T(8,128)(2,1)S(1)} %collective-permute-done.12.refs_6_), channel_id=1, source_target_pairs={{0,1},{1,0},{2,6},{3,7},{4,5},{5,4},{6,2},{7,3},{8,9},{9,8},{10,14... | collective-permute-start | bytes 1572872 | tf_op jit(solution)/shard_map/ppermute | solution.py:293
  54.0 2.6 %collective-permute-start.9 = (f32[8,40,128]{2,1,0:T(8,128)S(1)}, f32[8,40,128]{2,1,0:T(8,128)S(1)}, u32[]{:S(2)}, u32[]{:S(2)}) collective-permute-start(f32[8,40,128]{2,1,0:T(8,128)S(1)} %constant_dynamic-update-slice_fusion.refs_2_), channel_id=1, source_target_pairs={{0,16},{1,17},{2,18},{3,19},{4,20},{5,21},{6,22},{7,23},{8,24},{9,... | collective-permute-start | bytes 491528 | tf_op jit(solution)/shard_map/ppermute | solution.py:293
  56.6 0.5 collective-permute-start.19
  57.1 4.9 %collective-permute-done.9.refs_3_ = f32[8,40,128]{2,1,0:T(8,128)S(1)} collective-permute-done((f32[8,40,128]{2,1,0:T(8,128)S(1)}, f32[8,40,128]{2,1,0:T(8,128)S(1)}, u32[]{:S(2)}, u32[]{:S(2)}) %collective-permute-start.9) | collective-permute-done | bytes 163872 | tf_op jit(solution)/shard_map/ppermute | solution.py:293
  62.0 2.7 %sums.5 = (f32[512,2048]{1,0:T(8,128)S(1)}, f32[512,128]{1,0:T(8,128)S(1)}) custom-call(f32[512,128]{1,0:T(8,128)S(1)} %get-tuple-element.58.refs_0_, bf16[512,2048]{1,0:T(8,128)(2,1)S(1)} %get-tuple-element.59.refs_1_.proj_ref, f32[8,40,128]{2,1,0:T(8,128)S(1)} %constant_dynamic-update-slice_fusion.refs_2_, ...), custom_call_target="tpu_custom_call" | custom-call | tf_op jit(solution)/shard_map/sums/pallas_call | solution.py:414
  64.7 1.5 %collective-permute-start.18 = (bf16[128,2048]{1,0:T(8,128)(2,1)S(1)}, bf16[128,2048]{1,0:T(8,128)(2,1)S(1)}, u32[]{:S(2)}, u32[]{:S(2)}) collective-permute-start(bf16[128,2048]{1,0:T(8,128)(2,1)S(1)} %collective-permute-done.12.refs_6_), channel_id=1, source_target_pairs={{0,4},{1,5},{2,3},{3,2},{4,0},{5,1},{6,7},{7,6},{8,12},{9,13},{10,... | collective-permute-start | bytes 1572872 | tf_op jit(solution)/shard_map/ppermute | solution.py:293
  66.1 2.7 %sums.6 = (f32[512,2048]{1,0:T(8,128)S(1)}, f32[512,128]{1,0:T(8,128)S(1)}) custom-call(f32[512,128]{1,0:T(8,128)S(1)} %get-tuple-element.58.refs_0_, bf16[512,2048]{1,0:T(8,128)(2,1)S(1)} %get-tuple-element.59.refs_1_.proj_ref, f32[8,40,128]{2,1,0:T(8,128)S(1)} %constant_dynamic-update-slice_fusion.refs_2_, ...), custom_call_target="tpu_custom_call", output_to_operand_aliasing={{0}: (8, {}), {1}: (9, {})} | custom-call | tf_op jit(solution)/shard_map/sums/pallas_call | solution.py:414
  68.9 0.0 collective-permute-done.13.refs_5_
  68.9 0.0 collective-permute-done.15.refs_4_
  68.9 2.7 %sums.7 = (f32[512,2048]{1,0:T(8,128)S(1)}, f32[512,128]{1,0:T(8,128)S(1)}) custom-call(f32[512,128]{1,0:T(8,128)S(1)} %get-tuple-element.58.refs_0_, bf16[512,2048]{1,0:T(8,128)(2,1)S(1)} %get-tuple-element.59.refs_1_.proj_ref, f32[8,40,128]{2,1,0:T(8,128)S(1)} %constant_dynamic-update-slice_fusion.refs_2_, ...), custom_call_target="tpu_custom_call", output_to_operand_aliasing={{0}: (7, {}), {1}: (8, {})} | custom-call | tf_op jit(solution)/shard_map/sums/pallas_call | solution.py:414
  71.6 0.0 collective-permute-done.16.refs_4_
  71.6 0.7 collective-permute-start.17
  72.3 0.6 collective-permute-start.14
  72.9 0.0 collective-permute-done.19.refs_6_
  72.9 1.0 %collective-permute-done.18.refs_5_ = bf16[128,2048]{1,0:T(8,128)(2,1)S(1)} collective-permute-done((bf16[128,2048]{1,0:T(8,128)(2,1)S(1)}, bf16[128,2048]{1,0:T(8,128)(2,1)S(1)}, u32[]{:S(2)}, u32[]{:S(2)}) %collective-permute-start.18) | collective-permute-done | bytes 524320 | tf_op jit(solution)/shard_map/ppermute | solution.py:293
  73.9 2.7 %sums.8 = (f32[512,2048]{1,0:T(8,128)S(1)}, f32[512,128]{1,0:T(8,128)S(1)}) custom-call(f32[512,128]{1,0:T(8,128)S(1)} %get-tuple-element.58.refs_0_, bf16[512,2048]{1,0:T(8,128)(2,1)S(1)} %get-tuple-element.59.refs_1_.proj_ref, f32[8,40,128]{2,1,0:T(8,128)S(1)} %constant_dynamic-update-slice_fusion.refs_2_, ...), custom_call_target="tpu_custom_call", output_to_operand_aliasing={{0}: (7, {}), {1}: (8, {})} | custom-call | tf_op jit(solution)/shard_map/sums/pallas_call | solution.py:414
  76.7 4.2 %collective-permute-done.17.refs_5_ = bf16[128,2048]{1,0:T(8,128)(2,1)S(1)} collective-permute-done((bf16[128,2048]{1,0:T(8,128)(2,1)S(1)}, bf16[128,2048]{1,0:T(8,128)(2,1)S(1)}, u32[]{:S(2)}, u32[]{:S(2)}) %collective-permute-start.17) | collective-permute-done | bytes 524320 | tf_op jit(solution)/shard_map/ppermute | solution.py:293
  80.9 0.6 collective-permute-done.14.refs_4_
  81.5 2.5 %sums.9 = (f32[256,2048]{1,0:T(8,128)S(1)}, f32[256,128]{1,0:T(8,128)S(1)}, bf16[256,2176]{1,0:T(8,128)(2,1)S(1)}) custom-call(f32[512,128]{1,0:T(8,128)S(1)} %get-tuple-element.58.refs_0_, bf16[512,2048]{1,0:T(8,128)(2,1)S(1)} %get-tuple-element.59.refs_1_.proj_ref, f32[8,40,128]{2,1,0:T(8,128)S(1)} %constant_dynamic-update-slice_fusion.refs_2_, ...), custom_call_target="tpu_custom_call" | custom-call | tf_op jit(solution)/shard_map/sums/pallas_call | solution.py:414
  84.0 0.1 collective-permute-start.20
  84.1 2.7 %collective-permute-done.20.got_ref = bf16[256,2176]{1,0:T(8,128)(2,1)S(1)} collective-permute-done((bf16[256,2176]{1,0:T(8,128)(2,1)S(1)}, bf16[256,2176]{1,0:T(8,128)(2,1)S(1)}, u32[]{:S(2)}, u32[]{:S(2)}) %collective-permute-start.20) | collective-permute-done | bytes 1114144 | tf_op jit(solution)/shard_map/ppermute | solution.py:439
  86.8 2.0 %final.1 = f32[256,2048]{1,0:T(8,128)} custom-call(f32[256,2048]{1,0:T(8,128)S(1)} %get-tuple-element.85.kept_ref, f32[256,128]{1,0:T(8,128)S(1)} %get-tuple-element.86.kept_cnt_ref, bf16[256,2176]{1,0:T(8,128)(2,1)S(1)} %collective-permute-done.20.got_ref, bf16[512,2048]{1,0:T(8,128)(2,1)S(1)} %get-tuple-element.59.refs_1_.proj_ref), custom_call_target="tpu_custom_call" | custom-call | tf_op jit(solution)/shard_map/final/pallas_call | solution.py:442
  (4 shorter events, 0.0 us)
Async XLA Ops:
  1.9 16.8 %copy-start = (s32[2,32]{1,0:T(2,128)S(1)}, s32[2,32]{1,0:T(2,128)}, u32[]{:S(2)}) copy-start(s32[2,32]{1,0:T(2,128)} %mask_s.3) | copy-start | bytes 772
  1.9 16.8 %copy-start.1 = (f32[256]{0:T(256)S(1)}, f32[256]{0:T(256)}, u32[]{:S(2)}) copy-start(f32[256]{0:T(256)} %param.5) | copy-start | bytes 3076
  1.9 15.2 %collective-permute-start = (bf16[128,2048]{1,0:T(8,128)(2,1)S(1)}, bf16[128,2048]{1,0:T(8,128)(2,1)S(1)}, u32[]{:S(2)}, u32[]{:S(2)}) collective-permute-start(bf16[128,2048]{1,0:T(8,128)(2,1)S(1)} %convert_element_type.3.own_ref.refs_4_), channel_id=1, source_target_pairs={{0,1},{1,0},{2,6},{3,7},{4,5},{5,4},{6,2},{7,3},{8,9},{9,8},{10,14... | collective-permute-start | bytes 1572872 | tf_op jit(solution)/shard_map/ppermute | solution.py:293
  5.0 12.2 %collective-permute-start.1 = (bf16[128,2048]{1,0:T(8,128)(2,1)S(1)}, bf16[128,2048]{1,0:T(8,128)(2,1)S(1)}, u32[]{:S(2)}, u32[]{:S(2)}) collective-permute-start(bf16[128,2048]{1,0:T(8,128)(2,1)S(1)} %convert_element_type.3.own_ref.refs_4_), channel_id=1, source_target_pairs={{0,4},{1,5},{2,3},{3,2},{4,0},{5,1},{6,7},{7,6},{8,12},{9,13},{10,... | collective-permute-start | bytes 1572872 | tf_op jit(solution)/shard_map/ppermute | solution.py:293
  6.5 25.5 %collective-permute-start.6 = (bf16[128,2048]{1,0:T(8,128)(2,1)S(1)}, bf16[128,2048]{1,0:T(8,128)(2,1)S(1)}, u32[]{:S(2)}, u32[]{:S(2)}) collective-permute-start(bf16[128,2048]{1,0:T(8,128)(2,1)S(1)} %convert_element_type.3.own_ref.refs_4_), channel_id=1, source_target_pairs={{0,16},{1,17},{2,18},{3,19},{4,20},{5,21},{6,22},{7,23},{8,24},{9,... | collective-permute-start | bytes 1572872 | tf_op jit(solution)/shard_map/ppermute | solution.py:293
  9.1 23.4 %collective-permute-start.7 = (bf16[128,2048]{1,0:T(8,128)(2,1)S(1)}, bf16[128,2048]{1,0:T(8,128)(2,1)S(1)}, u32[]{:S(2)}, u32[]{:S(2)}) collective-permute-start(bf16[128,2048]{1,0:T(8,128)(2,1)S(1)} %convert_element_type.3.own_ref.refs_4_), channel_id=1, source_target_pairs={{0,8},{1,9},{2,10},{3,11},{4,12},{5,13},{6,14},{7,15},{8,0},{9,1},... | collective-permute-start | bytes 1572872 | tf_op jit(solution)/shard_map/ppermute | solution.py:293
  17.2 15.3 %collective-permute-start.8 = (bf16[128,2048]{1,0:T(8,128)(2,1)S(1)}, bf16[128,2048]{1,0:T(8,128)(2,1)S(1)}, u32[]{:S(2)}, u32[]{:S(2)}) collective-permute-start(bf16[128,2048]{1,0:T(8,128)(2,1)S(1)} %collective-permute-done.first_ref.refs_5_), channel_id=1, source_target_pairs={{0,4},{1,5},{2,3},{3,2},{4,0},{5,1},{6,7},{7,6},{8,12},{9,13},{10,... | collective-permute-start | bytes 1572872 | tf_op jit(solution)/shard_map/ppermute | solution.py:293
  24.6 3.7 %collective-permute-start.2 = (f32[8,256]{1,0:T(8,128)S(1)}, f32[8,256]{1,0:T(8,128)S(1)}, u32[]{:S(2)}, u32[]{:S(2)}) collective-permute-start(f32[8,256]{1,0:T(8,128)S(1)} %get-tuple-element.52.mine_ref), channel_id=1, source_target_pairs={{0,1},{1,0},{2,3},{3,2},{4,5},{5,4},{6,7},{7,6},{8,9},{9,8},{10,11... | collective-permute-start | bytes 24584 | tf_op jit(solution)/shard_map/ppermute | solution.py:293
  28.9 6.2 %collective-permute-start.3 = (f32[2,40,128]{2,1,0:T(8,128)S(1)}, f32[2,40,128]{2,1,0:T(8,128)S(1)}, u32[]{:S(2)}, u32[]{:S(2)}) collective-permute-start(f32[2,40,128]{2,1,0:T(8,128)S(1)} %meta.1), channel_id=1, source_target_pairs={{0,4},{1,5},{2,6},{3,7},{4,0},{5,1},{6,2},{7,3},{8,12},{9,13},{10,... | collective-permute-start | bytes 122888 | tf_op jit(solution)/shard_map/ppermute | solution.py:293
  29.9 5.2 %collective-permute-start.4 = (f32[2,40,128]{2,1,0:T(8,128)S(1)}, f32[2,40,128]{2,1,0:T(8,128)S(1)}, u32[]{:S(2)}, u32[]{:S(2)}) collective-permute-start(f32[2,40,128]{2,1,0:T(8,128)S(1)} %meta.1), channel_id=1, source_target_pairs={{0,8},{1,9},{2,10},{3,11},{4,12},{5,13},{6,14},{7,15},{8,0},{9,1},... | collective-permute-start | bytes 122888 | tf_op jit(solution)/shard_map/ppermute | solution.py:293
  32.0 4.9 %collective-permute-start.5 = (f32[2,40,128]{2,1,0:T(8,128)S(1)}, f32[2,40,128]{2,1,0:T(8,128)S(1)}, u32[]{:S(2)}, u32[]{:S(2)}) collective-permute-start(f32[2,40,128]{2,1,0:T(8,128)S(1)} %meta.1), channel_id=1, source_target_pairs={{0,12},{1,13},{2,14},{3,15},{4,8},{5,9},{6,10},{7,11},{8,4},{9,5},... | collective-permute-start | bytes 122888 | tf_op jit(solution)/shard_map/ppermute | solution.py:293
  36.9 14.9 %collective-permute-start.11 = (bf16[128,2048]{1,0:T(8,128)(2,1)S(1)}, bf16[128,2048]{1,0:T(8,128)(2,1)S(1)}, u32[]{:S(2)}, u32[]{:S(2)}) collective-permute-start(bf16[128,2048]{1,0:T(8,128)(2,1)S(1)} %collective-permute-done.6.refs_5_), channel_id=1, source_target_pairs={{0,4},{1,5},{2,3},{3,2},{4,0},{5,1},{6,7},{7,6},{8,12},{9,13},{10,... | collective-permute-start | bytes 1572872 | tf_op jit(solution)/shard_map/ppermute | solution.py:293
  37.6 14.1 %collective-permute-start.10 = (bf16[128,2048]{1,0:T(8,128)(2,1)S(1)}, bf16[128,2048]{1,0:T(8,128)(2,1)S(1)}, u32[]{:S(2)}, u32[]{:S(2)}) collective-permute-start(bf16[128,2048]{1,0:T(8,128)(2,1)S(1)} %collective-permute-done.6.refs_5_), channel_id=1, source_target_pairs={{0,1},{1,0},{2,6},{3,7},{4,5},{5,4},{6,2},{7,3},{8,9},{9,8},{10,14... | collective-permute-start | bytes 1572872 | tf_op jit(solution)/shard_map/ppermute | solution.py:293
  39.1 12.7 %collective-permute-start.12 = (bf16[128,2048]{1,0:T(8,128)(2,1)S(1)}, bf16[128,2048]{1,0:T(8,128)(2,1)S(1)}, u32[]{:S(2)}, u32[]{:S(2)}) collective-permute-start(bf16[128,2048]{1,0:T(8,128)(2,1)S(1)} %collective-permute-done.6.refs_5_), channel_id=1, source_target_pairs={{0,8},{1,9},{2,10},{3,11},{4,12},{5,13},{6,14},{7,15},{8,0},{9,1},... | collective-permute-start | bytes 1572872 | tf_op jit(solution)/shard_map/ppermute | solution.py:293
  39.6 29.3 %collective-permute-start.15 = (bf16[128,2048]{1,0:T(8,128)(2,1)S(1)}, bf16[128,2048]{1,0:T(8,128)(2,1)S(1)}, u32[]{:S(2)}, u32[]{:S(2)}) collective-permute-start(bf16[128,2048]{1,0:T(8,128)(2,1)S(1)} %collective-permute-done.7.refs_4_), channel_id=1, source_target_pairs={{0,1},{1,0},{2,6},{3,7},{4,5},{5,4},{6,2},{7,3},{8,9},{9,8},{10,14... | collective-permute-start | bytes 1572872 | tf_op jit(solution)/shard_map/ppermute | solution.py:293
  51.7 17.1 %collective-permute-start.13 = (bf16[128,2048]{1,0:T(8,128)(2,1)S(1)}, bf16[128,2048]{1,0:T(8,128)(2,1)S(1)}, u32[]{:S(2)}, u32[]{:S(2)}) collective-permute-start(bf16[128,2048]{1,0:T(8,128)(2,1)S(1)} %collective-permute-done.10.refs_6_), channel_id=1, source_target_pairs={{0,4},{1,5},{2,3},{3,2},{4,0},{5,1},{6,7},{7,6},{8,12},{9,13},{10,... | collective-permute-start | bytes 1572872 | tf_op jit(solution)/shard_map/ppermute | solution.py:293
  52.5 19.1 %collective-permute-start.16 = (bf16[128,2048]{1,0:T(8,128)(2,1)S(1)}, bf16[128,2048]{1,0:T(8,128)(2,1)S(1)}, u32[]{:S(2)}, u32[]{:S(2)}) collective-permute-start(bf16[128,2048]{1,0:T(8,128)(2,1)S(1)} %collective-permute-done.12.refs_6_), channel_id=1, source_target_pairs={{0,1},{1,0},{2,6},{3,7},{4,5},{5,4},{6,2},{7,3},{8,9},{9,8},{10,14... | collective-permute-start | bytes 1572872 | tf_op jit(solution)/shard_map/ppermute | solution.py:293
  54.0 8.0 %collective-permute-start.9 = (f32[8,40,128]{2,1,0:T(8,128)S(1)}, f32[8,40,128]{2,1,0:T(8,128)S(1)}, u32[]{:S(2)}, u32[]{:S(2)}) collective-permute-start(f32[8,40,128]{2,1,0:T(8,128)S(1)} %constant_dynamic-update-slice_fusion.refs_2_), channel_id=1, source_target_pairs={{0,16},{1,17},{2,18},{3,19},{4,20},{5,21},{6,22},{7,23},{8,24},{9,... | collective-permute-start | bytes 491528 | tf_op jit(solution)/shard_map/ppermute | solution.py:293
  56.6 16.3 %collective-permute-start.19 = (bf16[128,2048]{1,0:T(8,128)(2,1)S(1)}, bf16[128,2048]{1,0:T(8,128)(2,1)S(1)}, u32[]{:S(2)}, u32[]{:S(2)}) collective-permute-start(bf16[128,2048]{1,0:T(8,128)(2,1)S(1)} %collective-permute-done.1.second_ref.refs_6_), channel_id=1, source_target_pairs={{0,8},{1,9},{2,10},{3,11},{4,12},{5,13},{6,14},{7,15},{8,0},{9,1},... | collective-permute-start | bytes 1572872 | tf_op jit(solution)/shard_map/ppermute | solution.py:293
  64.7 9.2 %collective-permute-start.18 = (bf16[128,2048]{1,0:T(8,128)(2,1)S(1)}, bf16[128,2048]{1,0:T(8,128)(2,1)S(1)}, u32[]{:S(2)}, u32[]{:S(2)}) collective-permute-start(bf16[128,2048]{1,0:T(8,128)(2,1)S(1)} %collective-permute-done.12.refs_6_), channel_id=1, source_target_pairs={{0,4},{1,5},{2,3},{3,2},{4,0},{5,1},{6,7},{7,6},{8,12},{9,13},{10,... | collective-permute-start | bytes 1572872 | tf_op jit(solution)/shard_map/ppermute | solution.py:293
  71.6 9.2 %collective-permute-start.17 = (bf16[128,2048]{1,0:T(8,128)(2,1)S(1)}, bf16[128,2048]{1,0:T(8,128)(2,1)S(1)}, u32[]{:S(2)}, u32[]{:S(2)}) collective-permute-start(bf16[128,2048]{1,0:T(8,128)(2,1)S(1)} %collective-permute-done.16.refs_4_), channel_id=1, source_target_pairs={{0,4},{1,5},{2,3},{3,2},{4,0},{5,1},{6,7},{7,6},{8,12},{9,13},{10,... | collective-permute-start | bytes 1572872 | tf_op jit(solution)/shard_map/ppermute | solution.py:293
  72.3 9.2 %collective-permute-start.14 = (bf16[128,2048]{1,0:T(8,128)(2,1)S(1)}, bf16[128,2048]{1,0:T(8,128)(2,1)S(1)}, u32[]{:S(2)}, u32[]{:S(2)}) collective-permute-start(bf16[128,2048]{1,0:T(8,128)(2,1)S(1)} %collective-permute-done.8.refs_7_), channel_id=1, source_target_pairs={{0,8},{1,9},{2,10},{3,11},{4,12},{5,13},{6,14},{7,15},{8,0},{9,1},... | collective-permute-start | bytes 1572872 | tf_op jit(solution)/shard_map/ppermute | solution.py:293
  84.0 2.8 %collective-permute-start.20 = (bf16[256,2176]{1,0:T(8,128)(2,1)S(1)}, bf16[256,2176]{1,0:T(8,128)(2,1)S(1)}, u32[]{:S(2)}, u32[]{:S(2)}) collective-permute-start(bf16[256,2176]{1,0:T(8,128)(2,1)S(1)} %get-tuple-element.87), channel_id=1, source_target_pairs={{0,2},{1,3},{2,0},{3,1},{4,6},{5,7},{6,4},{7,5},{8,10},{9,11},{10,... | collective-permute-start | bytes 3342344 | tf_op jit(solution)/shard_map/ppermute | solution.py:439

commit v3 on v2

--- a/solution.py
+++ b/solution.py
@@ -171,14 +171,17 @@
     top, share = joined(mine_ref, theirs_ref)
     parts, _, shard = meta_ref.shape
     tiles = mask_s.shape[1]
+    at = lax.broadcasted_iota(jnp.int32, (1, shard), 1)
     for b in range(parts):
         columns = slice(b * shard, (b + 1) * shard)
-        floor = -top[:, columns]
+        meta_ref[b, 0:1, :] = top[:, columns]
+        meta_ref[b, 1:2, :] = share[:, columns]
+        meta_ref[b, 2:3, :] = prec_ref[:, columns]
+        may = jnp.zeros((1, shard), jnp.float32)
         for t in range(tiles):
-            meta_ref[b, t : t + 1, :] = jnp.where(mask_s[b, t] > 0, floor, very_low)
-        meta_ref[b, tiles : tiles + 1, :] = share[:, columns]
-        meta_ref[b, tiles + 1 : tiles + 2, :] = prec_ref[:, columns]
-        meta_ref[b, tiles + 2 : tiles + 8, :] = jnp.zeros((6, shard), jnp.float32)
+            may = jnp.where((at == t) & (mask_s[b, t] > 0), 1.0, may)
+        meta_ref[b, 3:4, :] = may
+        meta_ref[b, 4:8, :] = jnp.zeros((4, shard), jnp.float32)
 
 
 def posterior_kernel(scores_ref, mine_ref, theirs_ref, post_ref):
@@ -190,7 +193,7 @@
     ).astype(post_ref.dtype)
 
 
-def sums_kernel(n_metas, shapes, first, last, *refs):
+def sums_kernel(n_metas, tiles_here, shapes, first, last, *refs):
     half_ref, proj_ref = refs[:2]
     metas, refs = refs[2 : 2 + n_metas], refs[2 + n_metas :]
     pieces, refs = refs[: len(shapes)], refs[len(shapes) :]
@@ -203,11 +206,10 @@
     chip, core = img // cores, lax.rem(img, cores)
     width, columns = proj_ref.shape
     n_ori = lax.axis_size("ori")
-    per_meta, tiles, shard = metas[0].shape
-    tiles -= 8
-    tiles_here = tiles * cores // lax.axis_size("img")
+    per_meta, _, shard = metas[0].shape
     tile = width // tiles_here
     seen = jnp.zeros((width, shard), jnp.float32)
+    lane = lax.broadcasted_iota(jnp.int32, (1, shard), 1)
 
     def meta_row(at, row):
         def read(d):
@@ -228,11 +230,12 @@
     )
     for b, at in enumerate(sum(shapes, ())):
         here = slice(b * shard, (b + 1) * shard)
-        mine = meta_row(at, tiles + 1) * (products[:, here] - half_ref[...])
-        share = meta_row(at, tiles)
+        top, share, prec, may = (meta_row(at, row) for row in range(4))
+        mine = prec * (products[:, here] - half_ref[...])
         for t in range(tiles_here):
             down = slice(t * tile, (t + 1) * tile)
-            floor = meta_row(at, chip * tiles_here + t)
+            mark = jnp.where(lane == chip * tiles_here + t, may, 0.0)
+            floor = jnp.where(jnp.max(mark, axis=1, keepdims=True) > 0, -top, very_low)
             weights_buf[down, here] = (jnp.exp(mine[down, :] + floor) * share).astype(
                 jnp.bfloat16
             )
@@ -269,9 +272,10 @@
 def final_kernel(kept_ref, kept_cnt_ref, got_ref, proj_ref, out_ref):
     rows, columns = out_ref.shape
     core = lax.rem(lax.axis_index("img"), cores)
+    here = pl.ds(pl.multiple_of(pl.program_id(0) * rows, rows), rows)
     first_row = (core * pl.num_programs(0) + pl.program_id(0)) * rows
-    counts = kept_cnt_ref[:, 0:1] + got_ref[:, columns : columns + 1].astype(jnp.float32)
-    sums = kept_ref[...] + got_ref[:, :columns].astype(jnp.float32)
+    counts = kept_cnt_ref[here, 0:1] + got_ref[here, columns : columns + 1].astype(jnp.float32)
+    sums = kept_ref[here, :] + got_ref[here, :columns].astype(jnp.float32)
     prior = prior_weight * proj_ref[pl.ds(pl.multiple_of(first_row, rows), rows), :].astype(
         jnp.float32
     )
@@ -355,7 +359,7 @@
         meta_kernel,
         in_specs=[smem, vmem, vmem, vmem],
         out_specs=vmem,
-        out_shape=jax.ShapeDtypeStruct((n_ori, tiles + 8, shard), f32),
+        out_shape=jax.ShapeDtypeStruct((n_ori, 8, shard), f32),
         compiler_params=limit,
         cost_estimate=pl.CostEstimate(flops=0, bytes_accessed=0, transcendentals=0),
         name="meta",
@@ -386,13 +390,14 @@
         (close, posteriors, far_slab, near_slab)
     )
     far_b = sent(far_slab, *far)
-    near_a = sent(near_slab, *near)
     metas = jnp.concatenate([meta, *close], axis=0)
     metas = [metas, swap(metas, (4, 0))]
-    near_b = sent(own_b, (2, 0))
-    far_a, far_b, last_slab = together((far_a, far_b, last_slab))
+    far_a, far_b, last_slab, metas, own_b, own_c = together(
+        (far_a, far_b, last_slab, metas, own_b, own_c)
+    )
     far_c = sent(far_a, *far)
     last_a, last_b = sent(last_slab, *near), sent(last_slab, *far)
+    near_b, near_c = sent(own_b, (2, 0)), sent(own_c, (2, 0))
 
     def add(group, state, last):
         shapes = tuple(shards for shards, _ in group)
@@ -412,7 +417,7 @@
             ]
         n_ins = 2 + len(metas) + len(pieces) + (0 if first else 2)
         return pl.pallas_call(
-            functools.partial(sums_kernel, len(metas), shapes, first, last),
+            functools.partial(sums_kernel, len(metas), tiles * cores // n_img, shapes, first, last),
             in_specs=[vmem] * n_ins,
             out_specs=[vmem] * len(out_shape),
             out_shape=out_shape,
@@ -429,25 +434,20 @@
 
     state = add([own, own_a, own_b, own_c], None, False)
     state = add([near_slab, far_slab, far_a, far_b], state, False)
-    state, far_c, own_c = together((state, far_c, own_c))
-    near_c = sent(own_c, (2, 0))
-    state = add([near_a, far_c, last_slab], state, False)
-    state, last_a = together((state, last_a))
+    state, near_slab, far_c, last_a = together((state, near_slab, far_c, last_a))
     last_c = sent(last_a, *far)
-    state = add([last_a, last_b, near_b], state, False)
-    kept, kept_cnt, sent_away = add([near_c, last_c], state, True)
+    near_a = sent(near_slab, *near)
+    state = add([far_c, last_slab, last_a], state, False)
+    state, last_b, near_b = together((state, last_b, near_b))
+    state = add([last_b, near_b], state, False)
+    kept, kept_cnt, sent_away = add([near_a, near_c, last_c], state, True)
     got = lax.ppermute(sent_away, both, [(i, i ^ n_ori) for i in range(n)])
     out_rows = width // 2
     cut = 4
     refined = pl.pallas_call(
         final_kernel,
         grid=(cut,),
-        in_specs=[
-            pl.BlockSpec((out_rows // cut, columns), lambda i: (i, 0)),
-            pl.BlockSpec((out_rows // cut, lanes), lambda i: (i, 0)),
-            pl.BlockSpec((out_rows // cut, columns + lanes), lambda i: (i, 0)),
-            vmem,
-        ],
+        in_specs=[vmem] * 4,
         out_specs=pl.BlockSpec((out_rows // cut, columns), lambda i: (i, 0)),
         out_shape=jax.ShapeDtypeStruct((out_rows, columns), f32),
         compiler_params=limit,
@@ -472,6 +472,7 @@
             and shard % lanes == 0
             and tiles * cores % n_img == 0
             and orient % (tiles * lanes) == 0
+            and tiles <= shard
             and gathered_bytes <= 16 * 2**20
         )
         if fits:

time: 89 us -> 87.9 us (0.988)
  waiting for transfers between devices: 28.9 us -> 24.1 us
  starting transfers between devices: 26.9 us -> 30.3 us
    ppermute x20, waiting for transfers between devices: 26.2 us -> 21.4 us  [swap(): lax.ppermute(a, both, [(i, i ^ masks[i // n_ori % cores]) for i in range(...]
    ppermute x20, starting transfers between devices: 26.8 us -> 30.2 us  [swap(): lax.ppermute(a, both, [(i, i ^ masks[i // n_ori % cores]) for i in range(...]
  transfers between devices with their start and end apart: 21 -> 21, of which waited for: 8 -> 11; matrix products, arithmetic and copies ran while one was open for 0% -> 0% of each run, Pallas kernels for 30% -> 30%
where the time goes in v3:
time: 87.9 us; the launch traced here: 87.3 us
  Pallas kernels  30.8 us (35%)
  starting transfers between devices  30.3 us (34%)
  waiting for transfers between devices  24.1 us (27%)
  other arithmetic  1.29 us (1%)
    ppermute x20, starting transfers between devices, swap(): lax.ppermute(a, both, [(i, i ^ masks[i // n_ori % cores]) for i in range(...  30.2 us
    ppermute x20, waiting for transfers between devices, swap(): lax.ppermute(a, both, [(i, i ^ masks[i // n_ori % cores]) for i in range(...  21.4 us
    pallas_call x5, Pallas kernels, add(): pl.pallas_call(functools.partial(sums_kernel, len(metas), tiles * cores /...  13.2 us
    pallas_call x1, Pallas kernels, gathered_body(): pl.pallas_call(functools.partial(load_kernel, chips), in_specs=[pl.BlockS...  6.53 us
    pallas_call x1, Pallas kernels, gathered_body(): pl.pallas_call(functools.partial(scores_kernel, chips), in_specs=[smem] +...  5.83 us
    ppermute x1, waiting for transfers between devices, gathered_body(): got = lax.ppermute(sent_away, both, [(i, i ^ n_ori) for i in range(n)])  2.74 us
    pallas_call x1, Pallas kernels, gathered_body(): pl.pallas_call(posterior_kernel, grid=(cut,), in_specs=[vmem, pl.BlockSpe...  2.62 us
    pallas_call x1, Pallas kernels, gathered_body(): pl.pallas_call(final_kernel, grid=(cut,), in_specs=[vmem] * 4, out_specs=...  1.99 us
  transfers between devices with their start and end apart: 21, of which 11 were waited for; matrix products, arithmetic and copies ran while one was open for 0% of the time, Pallas kernels for 30%

profile of v3, /device:TPU:0, one launch (start us, length us, event | category | flops | bytes accessed | tf_op | source)
XLA Modules:
  0.0 87.3 jit_solution(10250914339272482767)
XLA Ops:
  0.6 1.3 %convert_element_type.3.own_ref.refs_4_ = bf16[128,2048]{1,0:T(8,128)(2,1)S(1)} convert(f32[128,2048]{1,0:T(8,128)} %param.4) | non-fusion elementwise | flops 262144 | bytes 1572864 | tf_op jit(solution)/shard_map/convert_element_type | solution.py:316
  1.9 0.0 copy-start
  1.9 0.0 copy-start.1
  1.9 3.0 %collective-permute-start = (bf16[128,2048]{1,0:T(8,128)(2,1)S(1)}, bf16[128,2048]{1,0:T(8,128)(2,1)S(1)}, u32[]{:S(2)}, u32[]{:S(2)}) collective-permute-start(bf16[128,2048]{1,0:T(8,128)(2,1)S(1)} %convert_element_type.3.own_ref.refs_4_), channel_id=1, source_target_pairs={{0,1},{1,0},{2,6},{3,7},{4,5},{5,4},{6,2},{7,3},{8,9},{9,8},{10,14... | collective-permute-start | bytes 1572872 | tf_op jit(solution)/shard_map/ppermute | solution.py:297
  5.0 1.5 %collective-permute-start.1 = (bf16[128,2048]{1,0:T(8,128)(2,1)S(1)}, bf16[128,2048]{1,0:T(8,128)(2,1)S(1)}, u32[]{:S(2)}, u32[]{:S(2)}) collective-permute-start(bf16[128,2048]{1,0:T(8,128)(2,1)S(1)} %convert_element_type.3.own_ref.refs_4_), channel_id=1, source_target_pairs={{0,4},{1,5},{2,3},{3,2},{4,0},{5,1},{6,7},{7,6},{8,12},{9,13},{10,... | collective-permute-start | bytes 1572872 | tf_op jit(solution)/shard_map/ppermute | solution.py:297
  6.5 2.6 %collective-permute-start.6 = (bf16[128,2048]{1,0:T(8,128)(2,1)S(1)}, bf16[128,2048]{1,0:T(8,128)(2,1)S(1)}, u32[]{:S(2)}, u32[]{:S(2)}) collective-permute-start(bf16[128,2048]{1,0:T(8,128)(2,1)S(1)} %convert_element_type.3.own_ref.refs_4_), channel_id=1, source_target_pairs={{0,16},{1,17},{2,18},{3,19},{4,20},{5,21},{6,22},{7,23},{8,24},{9,... | collective-permute-start | bytes 1572872 | tf_op jit(solution)/shard_map/ppermute | solution.py:297
  9.1 1.6 %collective-permute-start.7 = (bf16[128,2048]{1,0:T(8,128)(2,1)S(1)}, bf16[128,2048]{1,0:T(8,128)(2,1)S(1)}, u32[]{:S(2)}, u32[]{:S(2)}) collective-permute-start(bf16[128,2048]{1,0:T(8,128)(2,1)S(1)} %convert_element_type.3.own_ref.refs_4_), channel_id=1, source_target_pairs={{0,8},{1,9},{2,10},{3,11},{4,12},{5,13},{6,14},{7,15},{8,0},{9,1},... | collective-permute-start | bytes 1572872 | tf_op jit(solution)/shard_map/ppermute | solution.py:297
  10.6 6.5 %load.1 = (bf16[4096,2048]{1,0:T(8,128)(2,1)S(1)}, bf16[512,2048]{1,0:T(8,128)(2,1)S(1)}, f32[8,4096]{1,0:T(8,128)S(1)}, f32[512,128]{1,0:T(8,128)S(1)}) custom-call(bf16[4096,2048]{1,0:T(8,128)(2,1)} %away_ref.1), custom_call_target="tpu_custom_call" | custom-call | tf_op jit(solution)/shard_map/load/pallas_call | solution.py:323
  17.2 0.0 collective-permute-done.first_ref.refs_5_
  17.2 0.0 collective-permute-done.1.second_ref.refs_6_
  17.2 1.5 %collective-permute-start.8 = (bf16[128,2048]{1,0:T(8,128)(2,1)S(1)}, bf16[128,2048]{1,0:T(8,128)(2,1)S(1)}, u32[]{:S(2)}, u32[]{:S(2)}) collective-permute-start(bf16[128,2048]{1,0:T(8,128)(2,1)S(1)} %collective-permute-done.first_ref.refs_5_), channel_id=1, source_target_pairs={{0,4},{1,5},{2,3},{3,2},{4,0},{5,1},{6,7},{7,6},{8,12},{9,13},{10,... | collective-permute-start | bytes 1572872 | tf_op jit(solution)/shard_map/ppermute | solution.py:297
  18.7 0.0 copy-done
  18.7 0.0 copy-done.1
  18.7 5.8 %scores.1 = (f32[256,4096]{1,0:T(8,128)S(1)}, f32[8,256]{1,0:T(8,128)S(1)}) custom-call(s32[2,32]{1,0:T(2,128)S(1)} %copy-done, f32[1,256]{1,0:T(1,128)S(1)} %bitcast.1, f32[8,4096]{1,0:T(8,128)S(1)} %get-tuple-element.54.half_ref, bf16[128,2048]{1,0:T(8,128)(2,1)S(1)} %convert_element_type.3.own_ref.refs_4_, ...), custom_call_target="tpu_custom_call" | custom-call | tf_op jit(solution)/shard_map/scores/pallas_call | solution.py:344
  24.6 1.7 %collective-permute-start.2 = (f32[8,256]{1,0:T(8,128)S(1)}, f32[8,256]{1,0:T(8,128)S(1)}, u32[]{:S(2)}, u32[]{:S(2)}) collective-permute-start(f32[8,256]{1,0:T(8,128)S(1)} %get-tuple-element.58.mine_ref), channel_id=1, source_target_pairs={{0,1},{1,0},{2,3},{3,2},{4,5},{5,4},{6,7},{7,6},{8,9},{9,8},{10,11... | collective-permute-start | bytes 24584 | tf_op jit(solution)/shard_map/ppermute | solution.py:297
  26.2 2.0 %collective-permute-done.2.theirs_ref = f32[8,256]{1,0:T(8,128)S(1)} collective-permute-done((f32[8,256]{1,0:T(8,128)S(1)}, f32[8,256]{1,0:T(8,128)S(1)}, u32[]{:S(2)}, u32[]{:S(2)}) %collective-permute-start.2) | collective-permute-done | bytes 8224 | tf_op jit(solution)/shard_map/ppermute | solution.py:297
  28.3 0.6 meta.1
  28.9 1.0 %collective-permute-start.3 = (f32[2,8,128]{2,1,0:T(8,128)S(1)}, f32[2,8,128]{2,1,0:T(8,128)S(1)}, u32[]{:S(2)}, u32[]{:S(2)}) collective-permute-start(f32[2,8,128]{2,1,0:T(8,128)S(1)} %meta.1), channel_id=1, source_target_pairs={{0,4},{1,5},{2,6},{3,7},{4,0},{5,1},{6,2},{7,3},{8,12},{9,13},{10,... | collective-permute-start | bytes 24584 | tf_op jit(solution)/shard_map/ppermute | solution.py:297
  29.9 2.1 %collective-permute-start.4 = (f32[2,8,128]{2,1,0:T(8,128)S(1)}, f32[2,8,128]{2,1,0:T(8,128)S(1)}, u32[]{:S(2)}, u32[]{:S(2)}) collective-permute-start(f32[2,8,128]{2,1,0:T(8,128)S(1)} %meta.1), channel_id=1, source_target_pairs={{0,8},{1,9},{2,10},{3,11},{4,12},{5,13},{6,14},{7,15},{8,0},{9,1},... | collective-permute-start | bytes 24584 | tf_op jit(solution)/shard_map/ppermute | solution.py:297
  32.0 0.0 collective-permute-done.6.refs_5_
  32.0 0.5 collective-permute-start.5
  32.4 0.0 collective-permute-done.7.refs_4_
  32.5 0.0 collective-permute-done.8.refs_7_
  32.5 2.6 %posterior.1 = bf16[256,4096]{1,0:T(8,128)(2,1)} custom-call(f32[256,4096]{1,0:T(8,128)S(1)} %get-tuple-element.60.scores_ref, f32[8,256]{1,0:T(8,128)S(1)} %get-tuple-element.58.mine_ref, f32[8,256]{1,0:T(8,128)S(1)} %collective-permute-done.2.theirs_ref), custom_call_target="tpu_custom_call" | custom-call | tf_op jit(solution)/shard_map/posterior/pallas_call | solution.py:374
  35.1 0.0 collective-permute-done.3
  35.1 0.0 collective-permute-done.4
  35.1 1.4 %collective-permute-done.5 = f32[2,8,128]{2,1,0:T(8,128)S(1)} collective-permute-done((f32[2,8,128]{2,1,0:T(8,128)S(1)}, f32[2,8,128]{2,1,0:T(8,128)S(1)}, u32[]{:S(2)}, u32[]{:S(2)}) %collective-permute-start.5) | collective-permute-done | bytes 8224 | tf_op jit(solution)/shard_map/ppermute | solution.py:297
  36.5 0.7 collective-permute-start.10
  37.3 0.9 collective-permute-start.11
  38.1 1.5 %collective-permute-start.9 = (bf16[128,2048]{1,0:T(8,128)(2,1)S(1)}, bf16[128,2048]{1,0:T(8,128)(2,1)S(1)}, u32[]{:S(2)}, u32[]{:S(2)}) collective-permute-start(bf16[128,2048]{1,0:T(8,128)(2,1)S(1)} %collective-permute-done.6.refs_5_), channel_id=1, source_target_pairs={{0,1},{1,0},{2,6},{3,7},{4,5},{5,4},{6,2},{7,3},{8,9},{9,8},{10,14... | collective-permute-start | bytes 1572872 | tf_op jit(solution)/shard_map/ppermute | solution.py:297
  39.6 2.7 %collective-permute-start.12 = (f32[8,8,128]{2,1,0:T(8,128)S(1)}, f32[8,8,128]{2,1,0:T(8,128)S(1)}, u32[]{:S(2)}, u32[]{:S(2)}) collective-permute-start(f32[8,8,128]{2,1,0:T(8,128)S(1)} %constant_dynamic-update-slice_fusion.refs_2_), channel_id=1, source_target_pairs={{0,16},{1,17},{2,18},{3,19},{4,20},{5,21},{6,22},{7,23},{8,24},{9,... | collective-permute-start | bytes 98312 | tf_op jit(solution)/shard_map/ppermute | solution.py:297
  42.3 5.9 %collective-permute-done.12.refs_3_ = f32[8,8,128]{2,1,0:T(8,128)S(1)} collective-permute-done((f32[8,8,128]{2,1,0:T(8,128)S(1)}, f32[8,8,128]{2,1,0:T(8,128)S(1)}, u32[]{:S(2)}, u32[]{:S(2)}) %collective-permute-start.12) | collective-permute-done | bytes 32800 | tf_op jit(solution)/shard_map/ppermute | solution.py:297
  48.1 1.5 %collective-permute-done.10.refs_7_ = bf16[128,2048]{1,0:T(8,128)(2,1)S(1)} collective-permute-done((bf16[128,2048]{1,0:T(8,128)(2,1)S(1)}, bf16[128,2048]{1,0:T(8,128)(2,1)S(1)}, u32[]{:S(2)}, u32[]{:S(2)}) %collective-permute-start.10) | collective-permute-done | bytes 524320 | tf_op jit(solution)/shard_map/ppermute | solution.py:297
  49.6 0.0 collective-permute-done.11.refs_5_
  49.6 0.0 collective-permute-done.9.refs_6_
  49.6 1.4 %collective-permute-start.13 = (bf16[128,2048]{1,0:T(8,128)(2,1)S(1)}, bf16[128,2048]{1,0:T(8,128)(2,1)S(1)}, u32[]{:S(2)}, u32[]{:S(2)}) collective-permute-start(bf16[128,2048]{1,0:T(8,128)(2,1)S(1)} %collective-permute-done.9.refs_6_), channel_id=1, source_target_pairs={{0,4},{1,5},{2,3},{3,2},{4,0},{5,1},{6,7},{7,6},{8,12},{9,13},{10,... | collective-permute-start | bytes 1572872 | tf_op jit(solution)/shard_map/ppermute | solution.py:297
  51.0 1.5 %collective-permute-start.14 = (bf16[128,2048]{1,0:T(8,128)(2,1)S(1)}, bf16[128,2048]{1,0:T(8,128)(2,1)S(1)}, u32[]{:S(2)}, u32[]{:S(2)}) collective-permute-start(bf16[128,2048]{1,0:T(8,128)(2,1)S(1)} %collective-permute-done.11.refs_5_), channel_id=1, source_target_pairs={{0,1},{1,0},{2,6},{3,7},{4,5},{5,4},{6,2},{7,3},{8,9},{9,8},{10,14... | collective-permute-start | bytes 1572872 | tf_op jit(solution)/shard_map/ppermute | solution.py:297
  52.5 0.7 collective-permute-start.18
  53.2 3.3 %collective-permute-start.19 = (bf16[128,2048]{1,0:T(8,128)(2,1)S(1)}, bf16[128,2048]{1,0:T(8,128)(2,1)S(1)}, u32[]{:S(2)}, u32[]{:S(2)}) collective-permute-start(bf16[128,2048]{1,0:T(8,128)(2,1)S(1)} %collective-permute-done.1.second_ref.refs_6_), channel_id=1, source_target_pairs={{0,8},{1,9},{2,10},{3,11},{4,12},{5,13},{6,14},{7,15},{8,0},{9,1},... | collective-permute-start | bytes 1572872 | tf_op jit(solution)/shard_map/ppermute | solution.py:297
  56.5 0.0 collective-permute-start.16
  56.5 2.7 %sums.5 = (f32[512,2048]{1,0:T(8,128)S(1)}, f32[512,128]{1,0:T(8,128)S(1)}) custom-call(f32[512,128]{1,0:T(8,128)S(1)} %get-tuple-element.64.refs_0_, bf16[512,2048]{1,0:T(8,128)(2,1)S(1)} %get-tuple-element.65.refs_1_.proj_ref, f32[8,8,128]{2,1,0:T(8,128)S(1)} %constant_dynamic-update-slice_fusion.refs_2_, ...), custom_call_target="tpu_custom_call" | custom-call | tf_op jit(solution)/shard_map/sums/pallas_call | solution.py:419
  59.2 2.7 %sums.6 = (f32[512,2048]{1,0:T(8,128)S(1)}, f32[512,128]{1,0:T(8,128)S(1)}) custom-call(f32[512,128]{1,0:T(8,128)S(1)} %get-tuple-element.64.refs_0_, bf16[512,2048]{1,0:T(8,128)(2,1)S(1)} %get-tuple-element.65.refs_1_.proj_ref, f32[8,8,128]{2,1,0:T(8,128)S(1)} %constant_dynamic-update-slice_fusion.refs_2_, ...), custom_call_target="tpu_custom_call", output_to_operand_aliasing={{0}: (8, {}), {1}: (9, {})} | custom-call | tf_op jit(solution)/shard_map/sums/pallas_call | solution.py:419
  61.9 1.1 %collective-permute-done.13.refs_4_ = bf16[128,2048]{1,0:T(8,128)(2,1)S(1)} collective-permute-done((bf16[128,2048]{1,0:T(8,128)(2,1)S(1)}, bf16[128,2048]{1,0:T(8,128)(2,1)S(1)}, u32[]{:S(2)}, u32[]{:S(2)}) %collective-permute-start.13) | collective-permute-done | bytes 524320 | tf_op jit(solution)/shard_map/ppermute | solution.py:297
  63.1 2.8 %collective-permute-done.14.refs_6_ = bf16[128,2048]{1,0:T(8,128)(2,1)S(1)} collective-permute-done((bf16[128,2048]{1,0:T(8,128)(2,1)S(1)}, bf16[128,2048]{1,0:T(8,128)(2,1)S(1)}, u32[]{:S(2)}, u32[]{:S(2)}) %collective-permute-start.14) | collective-permute-done | bytes 524320 | tf_op jit(solution)/shard_map/ppermute | solution.py:297
  65.9 1.5 %collective-permute-start.15 = (bf16[128,2048]{1,0:T(8,128)(2,1)S(1)}, bf16[128,2048]{1,0:T(8,128)(2,1)S(1)}, u32[]{:S(2)}, u32[]{:S(2)}) collective-permute-start(bf16[128,2048]{1,0:T(8,128)(2,1)S(1)} %collective-permute-done.7.refs_4_), channel_id=1, source_target_pairs={{0,1},{1,0},{2,6},{3,7},{4,5},{5,4},{6,2},{7,3},{8,9},{9,8},{10,14... | collective-permute-start | bytes 1572872 | tf_op jit(solution)/shard_map/ppermute | solution.py:297
  67.4 0.7 collective-permute-start.17
  68.0 2.7 %sums.7 = (f32[512,2048]{1,0:T(8,128)S(1)}, f32[512,128]{1,0:T(8,128)S(1)}) custom-call(f32[512,128]{1,0:T(8,128)S(1)} %get-tuple-element.64.refs_0_, bf16[512,2048]{1,0:T(8,128)(2,1)S(1)} %get-tuple-element.65.refs_1_.proj_ref, f32[8,8,128]{2,1,0:T(8,128)S(1)} %constant_dynamic-update-slice_fusion.refs_2_, ...), custom_call_target="tpu_custom_call", output_to_operand_aliasing={{0}: (7, {}), {1}: (8, {})} | custom-call | tf_op jit(solution)/shard_map/sums/pallas_call | solution.py:419
  70.8 2.2 %collective-permute-done.18.refs_4_ = bf16[128,2048]{1,0:T(8,128)(2,1)S(1)} collective-permute-done((bf16[128,2048]{1,0:T(8,128)(2,1)S(1)}, bf16[128,2048]{1,0:T(8,128)(2,1)S(1)}, u32[]{:S(2)}, u32[]{:S(2)}) %collective-permute-start.18) | collective-permute-done | bytes 524320 | tf_op jit(solution)/shard_map/ppermute | solution.py:297
  73.0 0.0 collective-permute-done.19.refs_5_
  73.0 2.5 %sums.8 = (f32[512,2048]{1,0:T(8,128)S(1)}, f32[512,128]{1,0:T(8,128)S(1)}) custom-call(f32[512,128]{1,0:T(8,128)S(1)} %get-tuple-element.64.refs_0_, bf16[512,2048]{1,0:T(8,128)(2,1)S(1)} %get-tuple-element.65.refs_1_.proj_ref, f32[8,8,128]{2,1,0:T(8,128)S(1)} %constant_dynamic-update-slice_fusion.refs_2_, ...), custom_call_target="tpu_custom_call", output_to_operand_aliasing={{0}: (6, {}), {1}: (7, {})} | custom-call | tf_op jit(solution)/shard_map/sums/pallas_call | solution.py:419
  75.5 1.0 %collective-permute-done.16.refs_5_ = bf16[128,2048]{1,0:T(8,128)(2,1)S(1)} collective-permute-done((bf16[128,2048]{1,0:T(8,128)(2,1)S(1)}, bf16[128,2048]{1,0:T(8,128)(2,1)S(1)}, u32[]{:S(2)}, u32[]{:S(2)}) %collective-permute-start.16) | collective-permute-done | bytes 524320 | tf_op jit(solution)/shard_map/ppermute | solution.py:297
  76.5 2.2 %collective-permute-done.15.refs_4_ = bf16[128,2048]{1,0:T(8,128)(2,1)S(1)} collective-permute-done((bf16[128,2048]{1,0:T(8,128)(2,1)S(1)}, bf16[128,2048]{1,0:T(8,128)(2,1)S(1)}, u32[]{:S(2)}, u32[]{:S(2)}) %collective-permute-start.15) | collective-permute-done | bytes 524320 | tf_op jit(solution)/shard_map/ppermute | solution.py:297
  78.7 1.2 %collective-permute-done.17.refs_6_ = bf16[128,2048]{1,0:T(8,128)(2,1)S(1)} collective-permute-done((bf16[128,2048]{1,0:T(8,128)(2,1)S(1)}, bf16[128,2048]{1,0:T(8,128)(2,1)S(1)}, u32[]{:S(2)}, u32[]{:S(2)}) %collective-permute-start.17) | collective-permute-done | bytes 524320 | tf_op jit(solution)/shard_map/ppermute | solution.py:297
  79.9 2.6 %sums.9 = (f32[256,2048]{1,0:T(8,128)S(1)}, f32[256,128]{1,0:T(8,128)S(1)}, bf16[256,2176]{1,0:T(8,128)(2,1)S(1)}) custom-call(f32[512,128]{1,0:T(8,128)S(1)} %get-tuple-element.64.refs_0_, bf16[512,2048]{1,0:T(8,128)(2,1)S(1)} %get-tuple-element.65.refs_1_.proj_ref, f32[8,8,128]{2,1,0:T(8,128)S(1)} %constant_dynamic-update-slice_fusion.refs_2_, ...), custom_call_target="tpu_custom_call" | custom-call | tf_op jit(solution)/shard_map/sums/pallas_call | solution.py:419
  82.5 0.1 collective-permute-start.20
  82.6 2.7 %collective-permute-done.20.got_ref = bf16[256,2176]{1,0:T(8,128)(2,1)S(1)} collective-permute-done((bf16[256,2176]{1,0:T(8,128)(2,1)S(1)}, bf16[256,2176]{1,0:T(8,128)(2,1)S(1)}, u32[]{:S(2)}, u32[]{:S(2)}) %collective-permute-start.20) | collective-permute-done | bytes 1114144 | tf_op jit(solution)/shard_map/ppermute | solution.py:444
  85.3 2.0 %final.1 = f32[256,2048]{1,0:T(8,128)} custom-call(f32[256,2048]{1,0:T(8,128)S(1)} %get-tuple-element.97.kept_ref, f32[256,128]{1,0:T(8,128)S(1)} %get-tuple-element.98.kept_cnt_ref, bf16[256,2176]{1,0:T(8,128)(2,1)S(1)} %collective-permute-done.20.got_ref, bf16[512,2048]{1,0:T(8,128)(2,1)S(1)} %get-tuple-element.65.refs_1_.proj_ref), custom_call_target="tpu_custom_call" | custom-call | tf_op jit(solution)/shard_map/final/pallas_call | solution.py:447
  (4 shorter events, 0.0 us)
Async XLA Ops:
  1.9 16.8 %copy-start = (s32[2,32]{1,0:T(2,128)S(1)}, s32[2,32]{1,0:T(2,128)}, u32[]{:S(2)}) copy-start(s32[2,32]{1,0:T(2,128)} %mask_s.3) | copy-start | bytes 772
  1.9 16.8 %copy-start.1 = (f32[256]{0:T(256)S(1)}, f32[256]{0:T(256)}, u32[]{:S(2)}) copy-start(f32[256]{0:T(256)} %param.5) | copy-start | bytes 3076
  1.9 15.2 %collective-permute-start = (bf16[128,2048]{1,0:T(8,128)(2,1)S(1)}, bf16[128,2048]{1,0:T(8,128)(2,1)S(1)}, u32[]{:S(2)}, u32[]{:S(2)}) collective-permute-start(bf16[128,2048]{1,0:T(8,128)(2,1)S(1)} %convert_element_type.3.own_ref.refs_4_), channel_id=1, source_target_pairs={{0,1},{1,0},{2,6},{3,7},{4,5},{5,4},{6,2},{7,3},{8,9},{9,8},{10,14... | collective-permute-start | bytes 1572872 | tf_op jit(solution)/shard_map/ppermute | solution.py:297
  5.0 12.2 %collective-permute-start.1 = (bf16[128,2048]{1,0:T(8,128)(2,1)S(1)}, bf16[128,2048]{1,0:T(8,128)(2,1)S(1)}, u32[]{:S(2)}, u32[]{:S(2)}) collective-permute-start(bf16[128,2048]{1,0:T(8,128)(2,1)S(1)} %convert_element_type.3.own_ref.refs_4_), channel_id=1, source_target_pairs={{0,4},{1,5},{2,3},{3,2},{4,0},{5,1},{6,7},{7,6},{8,12},{9,13},{10,... | collective-permute-start | bytes 1572872 | tf_op jit(solution)/shard_map/ppermute | solution.py:297
  6.5 25.5 %collective-permute-start.6 = (bf16[128,2048]{1,0:T(8,128)(2,1)S(1)}, bf16[128,2048]{1,0:T(8,128)(2,1)S(1)}, u32[]{:S(2)}, u32[]{:S(2)}) collective-permute-start(bf16[128,2048]{1,0:T(8,128)(2,1)S(1)} %convert_element_type.3.own_ref.refs_4_), channel_id=1, source_target_pairs={{0,16},{1,17},{2,18},{3,19},{4,20},{5,21},{6,22},{7,23},{8,24},{9,... | collective-permute-start | bytes 1572872 | tf_op jit(solution)/shard_map/ppermute | solution.py:297
  9.1 23.4 %collective-permute-start.7 = (bf16[128,2048]{1,0:T(8,128)(2,1)S(1)}, bf16[128,2048]{1,0:T(8,128)(2,1)S(1)}, u32[]{:S(2)}, u32[]{:S(2)}) collective-permute-start(bf16[128,2048]{1,0:T(8,128)(2,1)S(1)} %convert_element_type.3.own_ref.refs_4_), channel_id=1, source_target_pairs={{0,8},{1,9},{2,10},{3,11},{4,12},{5,13},{6,14},{7,15},{8,0},{9,1},... | collective-permute-start | bytes 1572872 | tf_op jit(solution)/shard_map/ppermute | solution.py:297
  17.2 15.3 %collective-permute-start.8 = (bf16[128,2048]{1,0:T(8,128)(2,1)S(1)}, bf16[128,2048]{1,0:T(8,128)(2,1)S(1)}, u32[]{:S(2)}, u32[]{:S(2)}) collective-permute-start(bf16[128,2048]{1,0:T(8,128)(2,1)S(1)} %collective-permute-done.first_ref.refs_5_), channel_id=1, source_target_pairs={{0,4},{1,5},{2,3},{3,2},{4,0},{5,1},{6,7},{7,6},{8,12},{9,13},{10,... | collective-permute-start | bytes 1572872 | tf_op jit(solution)/shard_map/ppermute | solution.py:297
  24.6 3.7 %collective-permute-start.2 = (f32[8,256]{1,0:T(8,128)S(1)}, f32[8,256]{1,0:T(8,128)S(1)}, u32[]{:S(2)}, u32[]{:S(2)}) collective-permute-start(f32[8,256]{1,0:T(8,128)S(1)} %get-tuple-element.58.mine_ref), channel_id=1, source_target_pairs={{0,1},{1,0},{2,3},{3,2},{4,5},{5,4},{6,7},{7,6},{8,9},{9,8},{10,11... | collective-permute-start | bytes 24584 | tf_op jit(solution)/shard_map/ppermute | solution.py:297
  28.9 6.2 %collective-permute-start.3 = (f32[2,8,128]{2,1,0:T(8,128)S(1)}, f32[2,8,128]{2,1,0:T(8,128)S(1)}, u32[]{:S(2)}, u32[]{:S(2)}) collective-permute-start(f32[2,8,128]{2,1,0:T(8,128)S(1)} %meta.1), channel_id=1, source_target_pairs={{0,4},{1,5},{2,6},{3,7},{4,0},{5,1},{6,2},{7,3},{8,12},{9,13},{10,... | collective-permute-start | bytes 24584 | tf_op jit(solution)/shard_map/ppermute | solution.py:297
  29.9 5.2 %collective-permute-start.4 = (f32[2,8,128]{2,1,0:T(8,128)S(1)}, f32[2,8,128]{2,1,0:T(8,128)S(1)}, u32[]{:S(2)}, u32[]{:S(2)}) collective-permute-start(f32[2,8,128]{2,1,0:T(8,128)S(1)} %meta.1), channel_id=1, source_target_pairs={{0,8},{1,9},{2,10},{3,11},{4,12},{5,13},{6,14},{7,15},{8,0},{9,1},... | collective-permute-start | bytes 24584 | tf_op jit(solution)/shard_map/ppermute | solution.py:297
  32.0 4.6 %collective-permute-start.5 = (f32[2,8,128]{2,1,0:T(8,128)S(1)}, f32[2,8,128]{2,1,0:T(8,128)S(1)}, u32[]{:S(2)}, u32[]{:S(2)}) collective-permute-start(f32[2,8,128]{2,1,0:T(8,128)S(1)} %meta.1), channel_id=1, source_target_pairs={{0,12},{1,13},{2,14},{3,15},{4,8},{5,9},{6,10},{7,11},{8,4},{9,5},... | collective-permute-start | bytes 24584 | tf_op jit(solution)/shard_map/ppermute | solution.py:297
  36.5 13.1 %collective-permute-start.10 = (bf16[128,2048]{1,0:T(8,128)(2,1)S(1)}, bf16[128,2048]{1,0:T(8,128)(2,1)S(1)}, u32[]{:S(2)}, u32[]{:S(2)}) collective-permute-start(bf16[128,2048]{1,0:T(8,128)(2,1)S(1)} %collective-permute-done.6.refs_5_), channel_id=1, source_target_pairs={{0,4},{1,5},{2,3},{3,2},{4,0},{5,1},{6,7},{7,6},{8,12},{9,13},{10,... | collective-permute-start | bytes 1572872 | tf_op jit(solution)/shard_map/ppermute | solution.py:297
  37.3 12.4 %collective-permute-start.11 = (bf16[128,2048]{1,0:T(8,128)(2,1)S(1)}, bf16[128,2048]{1,0:T(8,128)(2,1)S(1)}, u32[]{:S(2)}, u32[]{:S(2)}) collective-permute-start(bf16[128,2048]{1,0:T(8,128)(2,1)S(1)} %collective-permute-done.6.refs_5_), channel_id=1, source_target_pairs={{0,8},{1,9},{2,10},{3,11},{4,12},{5,13},{6,14},{7,15},{8,0},{9,1},... | collective-permute-start | bytes 1572872 | tf_op jit(solution)/shard_map/ppermute | solution.py:297
  38.1 11.5 %collective-permute-start.9 = (bf16[128,2048]{1,0:T(8,128)(2,1)S(1)}, bf16[128,2048]{1,0:T(8,128)(2,1)S(1)}, u32[]{:S(2)}, u32[]{:S(2)}) collective-permute-start(bf16[128,2048]{1,0:T(8,128)(2,1)S(1)} %collective-permute-done.6.refs_5_), channel_id=1, source_target_pairs={{0,1},{1,0},{2,6},{3,7},{4,5},{5,4},{6,2},{7,3},{8,9},{9,8},{10,14... | collective-permute-start | bytes 1572872 | tf_op jit(solution)/shard_map/ppermute | solution.py:297
  39.6 8.5 %collective-permute-start.12 = (f32[8,8,128]{2,1,0:T(8,128)S(1)}, f32[8,8,128]{2,1,0:T(8,128)S(1)}, u32[]{:S(2)}, u32[]{:S(2)}) collective-permute-start(f32[8,8,128]{2,1,0:T(8,128)S(1)} %constant_dynamic-update-slice_fusion.refs_2_), channel_id=1, source_target_pairs={{0,16},{1,17},{2,18},{3,19},{4,20},{5,21},{6,22},{7,23},{8,24},{9,... | collective-permute-start | bytes 98312 | tf_op jit(solution)/shard_map/ppermute | solution.py:297
  49.6 13.4 %collective-permute-start.13 = (bf16[128,2048]{1,0:T(8,128)(2,1)S(1)}, bf16[128,2048]{1,0:T(8,128)(2,1)S(1)}, u32[]{:S(2)}, u32[]{:S(2)}) collective-permute-start(bf16[128,2048]{1,0:T(8,128)(2,1)S(1)} %collective-permute-done.9.refs_6_), channel_id=1, source_target_pairs={{0,4},{1,5},{2,3},{3,2},{4,0},{5,1},{6,7},{7,6},{8,12},{9,13},{10,... | collective-permute-start | bytes 1572872 | tf_op jit(solution)/shard_map/ppermute | solution.py:297
  51.0 14.9 %collective-permute-start.14 = (bf16[128,2048]{1,0:T(8,128)(2,1)S(1)}, bf16[128,2048]{1,0:T(8,128)(2,1)S(1)}, u32[]{:S(2)}, u32[]{:S(2)}) collective-permute-start(bf16[128,2048]{1,0:T(8,128)(2,1)S(1)} %collective-permute-done.11.refs_5_), channel_id=1, source_target_pairs={{0,1},{1,0},{2,6},{3,7},{4,5},{5,4},{6,2},{7,3},{8,9},{9,8},{10,14... | collective-permute-start | bytes 1572872 | tf_op jit(solution)/shard_map/ppermute | solution.py:297
  52.5 20.4 %collective-permute-start.18 = (bf16[128,2048]{1,0:T(8,128)(2,1)S(1)}, bf16[128,2048]{1,0:T(8,128)(2,1)S(1)}, u32[]{:S(2)}, u32[]{:S(2)}) collective-permute-start(bf16[128,2048]{1,0:T(8,128)(2,1)S(1)} %collective-permute-done.11.refs_5_), channel_id=1, source_target_pairs={{0,4},{1,5},{2,3},{3,2},{4,0},{5,1},{6,7},{7,6},{8,12},{9,13},{10,... | collective-permute-start | bytes 1572872 | tf_op jit(solution)/shard_map/ppermute | solution.py:297
  53.2 19.8 %collective-permute-start.19 = (bf16[128,2048]{1,0:T(8,128)(2,1)S(1)}, bf16[128,2048]{1,0:T(8,128)(2,1)S(1)}, u32[]{:S(2)}, u32[]{:S(2)}) collective-permute-start(bf16[128,2048]{1,0:T(8,128)(2,1)S(1)} %collective-permute-done.1.second_ref.refs_6_), channel_id=1, source_target_pairs={{0,8},{1,9},{2,10},{3,11},{4,12},{5,13},{6,14},{7,15},{8,0},{9,1},... | collective-permute-start | bytes 1572872 | tf_op jit(solution)/shard_map/ppermute | solution.py:297
  56.5 20.0 %collective-permute-start.16 = (bf16[128,2048]{1,0:T(8,128)(2,1)S(1)}, bf16[128,2048]{1,0:T(8,128)(2,1)S(1)}, u32[]{:S(2)}, u32[]{:S(2)}) collective-permute-start(bf16[128,2048]{1,0:T(8,128)(2,1)S(1)} %collective-permute-done.8.refs_7_), channel_id=1, source_target_pairs={{0,8},{1,9},{2,10},{3,11},{4,12},{5,13},{6,14},{7,15},{8,0},{9,1},... | collective-permute-start | bytes 1572872 | tf_op jit(solution)/shard_map/ppermute | solution.py:297
  65.9 12.8 %collective-permute-start.15 = (bf16[128,2048]{1,0:T(8,128)(2,1)S(1)}, bf16[128,2048]{1,0:T(8,128)(2,1)S(1)}, u32[]{:S(2)}, u32[]{:S(2)}) collective-permute-start(bf16[128,2048]{1,0:T(8,128)(2,1)S(1)} %collective-permute-done.7.refs_4_), channel_id=1, source_target_pairs={{0,1},{1,0},{2,6},{3,7},{4,5},{5,4},{6,2},{7,3},{8,9},{9,8},{10,14... | collective-permute-start | bytes 1572872 | tf_op jit(solution)/shard_map/ppermute | solution.py:297
  67.4 12.5 %collective-permute-start.17 = (bf16[128,2048]{1,0:T(8,128)(2,1)S(1)}, bf16[128,2048]{1,0:T(8,128)(2,1)S(1)}, u32[]{:S(2)}, u32[]{:S(2)}) collective-permute-start(bf16[128,2048]{1,0:T(8,128)(2,1)S(1)} %collective-permute-done.14.refs_6_), channel_id=1, source_target_pairs={{0,4},{1,5},{2,3},{3,2},{4,0},{5,1},{6,7},{7,6},{8,12},{9,13},{10,... | collective-permute-start | bytes 1572872 | tf_op jit(solution)/shard_map/ppermute | solution.py:297
  82.5 2.8 %collective-permute-start.20 = (bf16[256,2176]{1,0:T(8,128)(2,1)S(1)}, bf16[256,2176]{1,0:T(8,128)(2,1)S(1)}, u32[]{:S(2)}, u32[]{:S(2)}) collective-permute-start(bf16[256,2176]{1,0:T(8,128)(2,1)S(1)} %get-tuple-element.99), channel_id=1, source_target_pairs={{0,2},{1,3},{2,0},{3,1},{4,6},{5,7},{6,4},{7,5},{8,10},{9,11},{10,... | collective-permute-start | bytes 3342344 | tf_op jit(solution)/shard_map/ppermute | solution.py:444

commit v4 on v3

--- a/solution.py
+++ b/solution.py
@@ -364,12 +364,12 @@
         cost_estimate=pl.CostEstimate(flops=0, bytes_accessed=0, transcendentals=0),
         name="meta",
     )(tile_mask, prec_row, stats, theirs)
-    close = [swap(meta, (d, 0)) for d in (1, 2, 3)]
+    from_y = swap(meta, y)
     far_slab, near_slab, own_c, meta, scores = together(
         (far_slab, near_slab, own_c, meta, scores)
     )
     last_slab = sent(far_slab, (2, 0))
-    far_a = sent(far_slab, *near)
+    far_a, far_b = sent(far_slab, *near), sent(far_slab, *far)
     cut = 4
     posteriors = pl.pallas_call(
         posterior_kernel,
@@ -386,18 +386,18 @@
         name="posterior",
     )(scores, stats, theirs)
 
-    close, posteriors, far_slab, near_slab = together(
-        (close, posteriors, far_slab, near_slab)
-    )
-    far_b = sent(far_slab, *far)
-    metas = jnp.concatenate([meta, *close], axis=0)
-    metas = [metas, swap(metas, (4, 0))]
-    far_a, far_b, last_slab, metas, own_b, own_c = together(
-        (far_a, far_b, last_slab, metas, own_b, own_c)
+    far_a, far_b, last_slab, from_y, meta, posteriors = together(
+        (far_a, far_b, last_slab, from_y, meta, posteriors)
     )
     far_c = sent(far_a, *far)
     last_a, last_b = sent(last_slab, *near), sent(last_slab, *far)
-    near_b, near_c = sent(own_b, (2, 0)), sent(own_c, (2, 0))
+    metas = jnp.concatenate([meta, from_y], axis=0)
+    metas = jnp.concatenate([metas, swap(metas, (2, 0))], axis=0)
+    metas = [metas, swap(metas, (4, 0))]
+    metas, own_b, own_c = together((metas, own_b, own_c))
+    half_shard = shard // 2
+    near_b = moved(own_b[0], (2, 0)), swap(own_b[1][:half_shard], (2, 0))
+    near_c = sent(own_c, (2, 0))
 
     def add(group, state, last):
         shapes = tuple(shards for shards, _ in group)
@@ -437,10 +437,10 @@
     state, near_slab, far_c, last_a = together((state, near_slab, far_c, last_a))
     last_c = sent(last_a, *far)
     near_a = sent(near_slab, *near)
-    state = add([far_c, last_slab, last_a], state, False)
-    state, last_b, near_b = together((state, last_b, near_b))
-    state = add([last_b, near_b], state, False)
-    kept, kept_cnt, sent_away = add([near_a, near_c, last_c], state, True)
+    near_b_low = (), swap(near_slab[1][half_shard:], *far)
+    state, last_b = together((state, last_b))
+    state = add([far_c, last_slab, last_a, last_b], state, False)
+    kept, kept_cnt, sent_away = add([near_a, near_b, near_b_low, near_c, last_c], state, True)
     got = lax.ppermute(sent_away, both, [(i, i ^ n_ori) for i in range(n)])
     out_rows = width // 2
     cut = 4

time: 87.9 us -> 85.9 us (0.977)
  Pallas kernels: 30.8 us -> 28.3 us
  waiting for transfers between devices: 24.1 us -> 26 us
  starting transfers between devices: 30.3 us -> 29.3 us
    pallas_call x5 -> x4, Pallas kernels: 13.2 us -> 10.8 us  [add(): pl.pallas_call(functools.partial(sums_kernel, len(metas), tiles * cores /...]
    ppermute x20, waiting for transfers between devices: 21.4 us -> 23.3 us  [swap(): lax.ppermute(a, both, [(i, i ^ masks[i // n_ori % cores]) for i in range(...]
    ppermute x20, starting transfers between devices: 30.2 us -> 29.2 us  [swap(): lax.ppermute(a, both, [(i, i ^ masks[i // n_ori % cores]) for i in range(...]
  transfers between devices with their start and end apart: 21 -> 21, of which waited for: 11 -> 12; matrix products, arithmetic and copies ran while one was open for 0% -> 0% of each run, Pallas kernels for 30% -> 28%
where the time goes in v4:
time: 85.9 us; the launch traced here: 85.7 us
  starting transfers between devices  29.3 us (34%)
  Pallas kernels  28.3 us (33%)
  waiting for transfers between devices  26 us (30%)
  other arithmetic  1.29 us (2%)
    ppermute x20, starting transfers between devices, swap(): lax.ppermute(a, both, [(i, i ^ masks[i // n_ori % cores]) for i in range(...  29.2 us
    ppermute x20, waiting for transfers between devices, swap(): lax.ppermute(a, both, [(i, i ^ masks[i // n_ori % cores]) for i in range(...  23.3 us
    pallas_call x4, Pallas kernels, add(): pl.pallas_call(functools.partial(sums_kernel, len(metas), tiles * cores /...  10.8 us
    pallas_call x1, Pallas kernels, gathered_body(): pl.pallas_call(functools.partial(load_kernel, chips), in_specs=[pl.BlockS...  6.53 us
    pallas_call x1, Pallas kernels, gathered_body(): pl.pallas_call(functools.partial(scores_kernel, chips), in_specs=[smem] +...  5.83 us
    ppermute x1, waiting for transfers between devices, gathered_body(): got = lax.ppermute(sent_away, both, [(i, i ^ n_ori) for i in range(n)])  2.74 us
    pallas_call x1, Pallas kernels, gathered_body(): pl.pallas_call(posterior_kernel, grid=(cut,), in_specs=[vmem, pl.BlockSpe...  2.55 us
    pallas_call x1, Pallas kernels, gathered_body(): pl.pallas_call(final_kernel, grid=(cut,), in_specs=[vmem] * 4, out_specs=...  1.99 us
  transfers between devices with their start and end apart: 21, of which 12 were waited for; matrix products, arithmetic and copies ran while one was open for 0% of the time, Pallas kernels for 28%

profile of v4, /device:TPU:0, one launch (start us, length us, event | category | flops | bytes accessed | tf_op | source)
XLA Modules:
  0.0 85.7 jit_solution(2322638167376329146)
XLA Ops:
  0.6 1.3 %convert_element_type.3.own_ref.refs_4_ = bf16[128,2048]{1,0:T(8,128)(2,1)S(1)} convert(f32[128,2048]{1,0:T(8,128)} %param.4) | non-fusion elementwise | flops 262144 | bytes 1572864 | tf_op jit(solution)/shard_map/convert_element_type | solution.py:316
  1.9 0.0 copy-start
  1.9 0.0 copy-start.1
  1.9 3.0 %collective-permute-start.2 = (bf16[128,2048]{1,0:T(8,128)(2,1)S(1)}, bf16[128,2048]{1,0:T(8,128)(2,1)S(1)}, u32[]{:S(2)}, u32[]{:S(2)}) collective-permute-start(bf16[128,2048]{1,0:T(8,128)(2,1)S(1)} %convert_element_type.3.own_ref.refs_4_), channel_id=1, source_target_pairs={{0,1},{1,0},{2,6},{3,7},{4,5},{5,4},{6,2},{7,3},{8,9},{9,8},{10,14... | collective-permute-start | bytes 1572872 | tf_op jit(solution)/shard_map/ppermute | solution.py:297
  5.0 1.5 %collective-permute-start.3 = (bf16[128,2048]{1,0:T(8,128)(2,1)S(1)}, bf16[128,2048]{1,0:T(8,128)(2,1)S(1)}, u32[]{:S(2)}, u32[]{:S(2)}) collective-permute-start(bf16[128,2048]{1,0:T(8,128)(2,1)S(1)} %convert_element_type.3.own_ref.refs_4_), channel_id=1, source_target_pairs={{0,4},{1,5},{2,3},{3,2},{4,0},{5,1},{6,7},{7,6},{8,12},{9,13},{10,... | collective-permute-start | bytes 1572872 | tf_op jit(solution)/shard_map/ppermute | solution.py:297
  6.5 2.6 %collective-permute-start = (bf16[128,2048]{1,0:T(8,128)(2,1)S(1)}, bf16[128,2048]{1,0:T(8,128)(2,1)S(1)}, u32[]{:S(2)}, u32[]{:S(2)}) collective-permute-start(bf16[128,2048]{1,0:T(8,128)(2,1)S(1)} %convert_element_type.3.own_ref.refs_4_), channel_id=1, source_target_pairs={{0,16},{1,17},{2,18},{3,19},{4,20},{5,21},{6,22},{7,23},{8,24},{9,... | collective-permute-start | bytes 1572872 | tf_op jit(solution)/shard_map/ppermute | solution.py:297
  9.1 1.6 %collective-permute-start.1 = (bf16[128,2048]{1,0:T(8,128)(2,1)S(1)}, bf16[128,2048]{1,0:T(8,128)(2,1)S(1)}, u32[]{:S(2)}, u32[]{:S(2)}) collective-permute-start(bf16[128,2048]{1,0:T(8,128)(2,1)S(1)} %convert_element_type.3.own_ref.refs_4_), channel_id=1, source_target_pairs={{0,8},{1,9},{2,10},{3,11},{4,12},{5,13},{6,14},{7,15},{8,0},{9,1},... | collective-permute-start | bytes 1572872 | tf_op jit(solution)/shard_map/ppermute | solution.py:297
  10.6 6.5 %load.1 = (bf16[4096,2048]{1,0:T(8,128)(2,1)S(1)}, bf16[512,2048]{1,0:T(8,128)(2,1)S(1)}, f32[8,4096]{1,0:T(8,128)S(1)}, f32[512,128]{1,0:T(8,128)S(1)}) custom-call(bf16[4096,2048]{1,0:T(8,128)(2,1)} %away_ref.1), custom_call_target="tpu_custom_call" | custom-call | tf_op jit(solution)/shard_map/load/pallas_call | solution.py:323
  17.2 0.0 collective-permute-done.2.first_ref.refs_5_
  17.2 0.0 collective-permute-done.3.second_ref.refs_6_
  17.2 1.5 %collective-permute-start.4 = (bf16[128,2048]{1,0:T(8,128)(2,1)S(1)}, bf16[128,2048]{1,0:T(8,128)(2,1)S(1)}, u32[]{:S(2)}, u32[]{:S(2)}) collective-permute-start(bf16[128,2048]{1,0:T(8,128)(2,1)S(1)} %collective-permute-done.2.first_ref.refs_5_), channel_id=1, source_target_pairs={{0,4},{1,5},{2,3},{3,2},{4,0},{5,1},{6,7},{7,6},{8,12},{9,13},{10,... | collective-permute-start | bytes 1572872 | tf_op jit(solution)/shard_map/ppermute | solution.py:297
  18.7 0.0 copy-done
  18.7 0.0 copy-done.1
  18.7 5.8 %scores.1 = (f32[256,4096]{1,0:T(8,128)S(1)}, f32[8,256]{1,0:T(8,128)S(1)}) custom-call(s32[2,32]{1,0:T(2,128)S(1)} %copy-done, f32[1,256]{1,0:T(1,128)S(1)} %bitcast.1, f32[8,4096]{1,0:T(8,128)S(1)} %get-tuple-element.49.half_ref, bf16[128,2048]{1,0:T(8,128)(2,1)S(1)} %convert_element_type.3.own_ref.refs_4_, ...), custom_call_target="tpu_custom_call" | custom-call | tf_op jit(solution)/shard_map/scores/pallas_call | solution.py:344
  24.6 1.7 %collective-permute-start.5 = (f32[8,256]{1,0:T(8,128)S(1)}, f32[8,256]{1,0:T(8,128)S(1)}, u32[]{:S(2)}, u32[]{:S(2)}) collective-permute-start(f32[8,256]{1,0:T(8,128)S(1)} %get-tuple-element.52.mine_ref), channel_id=1, source_target_pairs={{0,1},{1,0},{2,3},{3,2},{4,5},{5,4},{6,7},{7,6},{8,9},{9,8},{10,11... | collective-permute-start | bytes 24584 | tf_op jit(solution)/shard_map/ppermute | solution.py:297
  26.2 2.0 %collective-permute-done.5.theirs_ref = f32[8,256]{1,0:T(8,128)S(1)} collective-permute-done((f32[8,256]{1,0:T(8,128)S(1)}, f32[8,256]{1,0:T(8,128)S(1)}, u32[]{:S(2)}, u32[]{:S(2)}) %collective-permute-start.5) | collective-permute-done | bytes 8224 | tf_op jit(solution)/shard_map/ppermute | solution.py:297
  28.3 0.6 meta.1
  28.9 2.9 %collective-permute-done.refs_5_ = bf16[128,2048]{1,0:T(8,128)(2,1)S(1)} collective-permute-done((bf16[128,2048]{1,0:T(8,128)(2,1)S(1)}, bf16[128,2048]{1,0:T(8,128)(2,1)S(1)}, u32[]{:S(2)}, u32[]{:S(2)}) %collective-permute-start) | collective-permute-done | bytes 524320 | tf_op jit(solution)/shard_map/ppermute | solution.py:297
  31.8 0.2 collective-permute-done.1.refs_4_
  32.0 0.0 collective-permute-done.4.refs_7_
  32.0 0.5 collective-permute-start.6
  32.5 0.5 collective-permute-start.7
  33.0 1.5 %collective-permute-start.8 = (bf16[128,2048]{1,0:T(8,128)(2,1)S(1)}, bf16[128,2048]{1,0:T(8,128)(2,1)S(1)}, u32[]{:S(2)}, u32[]{:S(2)}) collective-permute-start(bf16[128,2048]{1,0:T(8,128)(2,1)S(1)} %collective-permute-done.refs_5_), channel_id=1, source_target_pairs={{0,8},{1,9},{2,10},{3,11},{4,12},{5,13},{6,14},{7,15},{8,0},{9,1},... | collective-permute-start | bytes 1572872 | tf_op jit(solution)/shard_map/ppermute | solution.py:297
  34.5 1.5 %collective-permute-start.9 = (f32[2,8,128]{2,1,0:T(8,128)S(1)}, f32[2,8,128]{2,1,0:T(8,128)S(1)}, u32[]{:S(2)}, u32[]{:S(2)}) collective-permute-start(f32[2,8,128]{2,1,0:T(8,128)S(1)} %meta.1), channel_id=1, source_target_pairs={{0,4},{1,5},{2,6},{3,7},{4,0},{5,1},{6,2},{7,3},{8,12},{9,13},{10,... | collective-permute-start | bytes 24584 | tf_op jit(solution)/shard_map/ppermute | solution.py:297
  36.0 2.6 %posterior.1 = bf16[256,4096]{1,0:T(8,128)(2,1)} custom-call(f32[256,4096]{1,0:T(8,128)S(1)} %get-tuple-element.56.scores_ref, f32[8,256]{1,0:T(8,128)S(1)} %get-tuple-element.52.mine_ref, f32[8,256]{1,0:T(8,128)S(1)} %collective-permute-done.5.theirs_ref), custom_call_target="tpu_custom_call" | custom-call | tf_op jit(solution)/shard_map/posterior/pallas_call | solution.py:374
  38.6 6.1 %collective-permute-done.9 = f32[2,8,128]{2,1,0:T(8,128)S(1)} collective-permute-done((f32[2,8,128]{2,1,0:T(8,128)S(1)}, f32[2,8,128]{2,1,0:T(8,128)S(1)}, u32[]{:S(2)}, u32[]{:S(2)}) %collective-permute-start.9) | collective-permute-done | bytes 8224 | tf_op jit(solution)/shard_map/ppermute | solution.py:297
  44.7 0.1 collective-permute-done.6.refs_6_
  44.8 0.0 collective-permute-done.7.refs_7_
  44.8 0.2 collective-permute-done.8.refs_5_
  45.0 1.6 %collective-permute-start.12 = (bf16[128,2048]{1,0:T(8,128)(2,1)S(1)}, bf16[128,2048]{1,0:T(8,128)(2,1)S(1)}, u32[]{:S(2)}, u32[]{:S(2)}) collective-permute-start(bf16[128,2048]{1,0:T(8,128)(2,1)S(1)} %collective-permute-done.6.refs_6_), channel_id=1, source_target_pairs={{0,4},{1,5},{2,3},{3,2},{4,0},{5,1},{6,7},{7,6},{8,12},{9,13},{10,... | collective-permute-start | bytes 1572872 | tf_op jit(solution)/shard_map/ppermute | solution.py:297
  46.5 1.5 %collective-permute-start.13 = (bf16[128,2048]{1,0:T(8,128)(2,1)S(1)}, bf16[128,2048]{1,0:T(8,128)(2,1)S(1)}, u32[]{:S(2)}, u32[]{:S(2)}) collective-permute-start(bf16[128,2048]{1,0:T(8,128)(2,1)S(1)} %collective-permute-done.8.refs_5_), channel_id=1, source_target_pairs={{0,1},{1,0},{2,6},{3,7},{4,5},{5,4},{6,2},{7,3},{8,9},{9,8},{10,14... | collective-permute-start | bytes 1572872 | tf_op jit(solution)/shard_map/ppermute | solution.py:297
  48.0 0.5 collective-permute-start.19
  48.5 1.7 %collective-permute-start.10 = (f32[4,8,128]{2,1,0:T(8,128)S(1)}, f32[4,8,128]{2,1,0:T(8,128)S(1)}, u32[]{:S(2)}, u32[]{:S(2)}) collective-permute-start(f32[4,8,128]{2,1,0:T(8,128)S(1)} %pad_maximum_fusion), channel_id=1, source_target_pairs={{0,8},{1,9},{2,10},{3,11},{4,12},{5,13},{6,14},{7,15},{8,0},{9,1},... | collective-permute-start | bytes 49160 | tf_op jit(solution)/shard_map/ppermute | solution.py:297
  50.2 2.0 %collective-permute-done.10 = f32[4,8,128]{2,1,0:T(8,128)S(1)} collective-permute-done((f32[4,8,128]{2,1,0:T(8,128)S(1)}, f32[4,8,128]{2,1,0:T(8,128)S(1)}, u32[]{:S(2)}, u32[]{:S(2)}) %collective-permute-start.10) | collective-permute-done | bytes 16416 | tf_op jit(solution)/shard_map/ppermute | solution.py:297
  52.3 3.3 %collective-permute-start.11 = (f32[8,8,128]{2,1,0:T(8,128)S(1)}, f32[8,8,128]{2,1,0:T(8,128)S(1)}, u32[]{:S(2)}, u32[]{:S(2)}) collective-permute-start(f32[8,8,128]{2,1,0:T(8,128)S(1)} %constant_dynamic-update-slice_fusion.refs_2_), channel_id=1, source_target_pairs={{0,16},{1,17},{2,18},{3,19},{4,20},{5,21},{6,22},{7,23},{8,24},{9,... | collective-permute-start | bytes 98312 | tf_op jit(solution)/shard_map/ppermute | solution.py:297
  55.6 2.0 %collective-permute-done.11.refs_3_ = f32[8,8,128]{2,1,0:T(8,128)S(1)} collective-permute-done((f32[8,8,128]{2,1,0:T(8,128)S(1)}, f32[8,8,128]{2,1,0:T(8,128)S(1)}, u32[]{:S(2)}, u32[]{:S(2)}) %collective-permute-start.11) | collective-permute-done | bytes 32800 | tf_op jit(solution)/shard_map/ppermute | solution.py:297
  57.6 1.6 %collective-permute-start.17 = (bf16[128,2048]{1,0:T(8,128)(2,1)S(1)}, bf16[128,2048]{1,0:T(8,128)(2,1)S(1)}, u32[]{:S(2)}, u32[]{:S(2)}) collective-permute-start(bf16[128,2048]{1,0:T(8,128)(2,1)S(1)} %collective-permute-done.4.refs_7_), channel_id=1, source_target_pairs={{0,8},{1,9},{2,10},{3,11},{4,12},{5,13},{6,14},{7,15},{8,0},{9,1},... | collective-permute-start | bytes 1572872 | tf_op jit(solution)/shard_map/ppermute | solution.py:297
  59.3 2.7 %sums.4 = (f32[512,2048]{1,0:T(8,128)S(1)}, f32[512,128]{1,0:T(8,128)S(1)}) custom-call(f32[512,128]{1,0:T(8,128)S(1)} %get-tuple-element.58.refs_0_, bf16[512,2048]{1,0:T(8,128)(2,1)S(1)} %get-tuple-element.59.refs_1_.proj_ref, f32[8,8,128]{2,1,0:T(8,128)S(1)} %constant_dynamic-update-slice_fusion.refs_2_, ...), custom_call_target="tpu_custom_call" | custom-call | tf_op jit(solution)/shard_map/sums/pallas_call | solution.py:419
  61.9 2.7 %sums.5 = (f32[512,2048]{1,0:T(8,128)S(1)}, f32[512,128]{1,0:T(8,128)S(1)}) custom-call(f32[512,128]{1,0:T(8,128)S(1)} %get-tuple-element.58.refs_0_, bf16[512,2048]{1,0:T(8,128)(2,1)S(1)} %get-tuple-element.59.refs_1_.proj_ref, f32[8,8,128]{2,1,0:T(8,128)S(1)} %constant_dynamic-update-slice_fusion.refs_2_, ...), custom_call_target="tpu_custom_call", output_to_operand_aliasing={{0}: (8, {}), {1}: (9, {})} | custom-call | tf_op jit(solution)/shard_map/sums/pallas_call | solution.py:419
  64.7 0.0 collective-permute-done.12.refs_4_
  64.7 0.0 collective-permute-done.13.refs_6_
  64.7 0.6 collective-permute-start.14
  65.3 1.9 %collective-permute-start.18 = (bf16[128,2048]{1,0:T(8,128)(2,1)S(1)}, bf16[128,2048]{1,0:T(8,128)(2,1)S(1)}, u32[]{:S(2)}, u32[]{:S(2)}) collective-permute-start(bf16[128,2048]{1,0:T(8,128)(2,1)S(1)} %collective-permute-done.13.refs_6_), channel_id=1, source_target_pairs={{0,4},{1,5},{2,3},{3,2},{4,0},{5,1},{6,7},{7,6},{8,12},{9,13},{10,... | collective-permute-start | bytes 1572872 | tf_op jit(solution)/shard_map/ppermute | solution.py:297
  67.2 0.1 collective-permute-start.15
  67.3 0.0 collective-permute-done.19.refs_7_
  67.3 0.5 collective-permute-start.16
  67.8 2.7 %sums.6 = (f32[512,2048]{1,0:T(8,128)S(1)}, f32[512,128]{1,0:T(8,128)S(1)}) custom-call(f32[512,128]{1,0:T(8,128)S(1)} %get-tuple-element.58.refs_0_, bf16[512,2048]{1,0:T(8,128)(2,1)S(1)} %get-tuple-element.59.refs_1_.proj_ref, f32[8,8,128]{2,1,0:T(8,128)S(1)} %constant_dynamic-update-slice_fusion.refs_2_, ...), custom_call_target="tpu_custom_call", output_to_operand_aliasing={{0}: (8, {}), {1}: (9, {})} | custom-call | tf_op jit(solution)/shard_map/sums/pallas_call | solution.py:419
  70.6 3.8 %collective-permute-done.15.refs_5_ = bf16[64,2048]{1,0:T(8,128)(2,1)S(1)} collective-permute-done((bf16[64,2048]{1,0:T(8,128)(2,1)S(1)}, bf16[64,2048]{1,0:T(8,128)(2,1)S(1)}, u32[]{:S(2)}, u32[]{:S(2)}) %collective-permute-start.15) | collective-permute-done | bytes 262176 | tf_op jit(solution)/shard_map/ppermute | solution.py:297
  74.4 0.0 collective-permute-done.17.refs_7_
  74.4 3.8 %collective-permute-done.16.refs_6_ = bf16[64,2048]{1,0:T(8,128)(2,1)S(1)} collective-permute-done((bf16[64,2048]{1,0:T(8,128)(2,1)S(1)}, bf16[64,2048]{1,0:T(8,128)(2,1)S(1)}, u32[]{:S(2)}, u32[]{:S(2)}) %collective-permute-start.16) | collective-permute-done | bytes 262176 | tf_op jit(solution)/shard_map/ppermute | solution.py:297
  78.2 0.1 collective-permute-done.14.refs_4_
  78.2 0.0 collective-permute-done.18.refs_8_
  78.2 2.7 %sums.7 = (f32[256,2048]{1,0:T(8,128)S(1)}, f32[256,128]{1,0:T(8,128)S(1)}, bf16[256,2176]{1,0:T(8,128)(2,1)S(1)}) custom-call(f32[512,128]{1,0:T(8,128)S(1)} %get-tuple-element.58.refs_0_, bf16[512,2048]{1,0:T(8,128)(2,1)S(1)} %get-tuple-element.59.refs_1_.proj_ref, f32[8,8,128]{2,1,0:T(8,128)S(1)} %constant_dynamic-update-slice_fusion.refs_2_, ...), custom_call_target="tpu_custom_call" | custom-call | tf_op jit(solution)/shard_map/sums/pallas_call | solution.py:419
  80.9 0.1 collective-permute-start.20
  81.0 2.7 %collective-permute-done.20.got_ref = bf16[256,2176]{1,0:T(8,128)(2,1)S(1)} collective-permute-done((bf16[256,2176]{1,0:T(8,128)(2,1)S(1)}, bf16[256,2176]{1,0:T(8,128)(2,1)S(1)}, u32[]{:S(2)}, u32[]{:S(2)}) %collective-permute-start.20) | collective-permute-done | bytes 1114144 | tf_op jit(solution)/shard_map/ppermute | solution.py:444
  83.7 2.0 %final.1 = f32[256,2048]{1,0:T(8,128)} custom-call(f32[256,2048]{1,0:T(8,128)S(1)} %get-tuple-element.85.kept_ref, f32[256,128]{1,0:T(8,128)S(1)} %get-tuple-element.86.kept_cnt_ref, bf16[256,2176]{1,0:T(8,128)(2,1)S(1)} %collective-permute-done.20.got_ref, bf16[512,2048]{1,0:T(8,128)(2,1)S(1)} %get-tuple-element.59.refs_1_.proj_ref), custom_call_target="tpu_custom_call" | custom-call | tf_op jit(solution)/shard_map/final/pallas_call | solution.py:447
  (6 shorter events, 0.0 us)
Async XLA Ops:
  1.9 16.8 %copy-start = (s32[2,32]{1,0:T(2,128)S(1)}, s32[2,32]{1,0:T(2,128)}, u32[]{:S(2)}) copy-start(s32[2,32]{1,0:T(2,128)} %mask_s.3) | copy-start | bytes 772
  1.9 16.8 %copy-start.1 = (f32[256]{0:T(256)S(1)}, f32[256]{0:T(256)}, u32[]{:S(2)}) copy-start(f32[256]{0:T(256)} %param.5) | copy-start | bytes 3076
  1.9 15.2 %collective-permute-start.2 = (bf16[128,2048]{1,0:T(8,128)(2,1)S(1)}, bf16[128,2048]{1,0:T(8,128)(2,1)S(1)}, u32[]{:S(2)}, u32[]{:S(2)}) collective-permute-start(bf16[128,2048]{1,0:T(8,128)(2,1)S(1)} %convert_element_type.3.own_ref.refs_4_), channel_id=1, source_target_pairs={{0,1},{1,0},{2,6},{3,7},{4,5},{5,4},{6,2},{7,3},{8,9},{9,8},{10,14... | collective-permute-start | bytes 1572872 | tf_op jit(solution)/shard_map/ppermute | solution.py:297
  5.0 12.2 %collective-permute-start.3 = (bf16[128,2048]{1,0:T(8,128)(2,1)S(1)}, bf16[128,2048]{1,0:T(8,128)(2,1)S(1)}, u32[]{:S(2)}, u32[]{:S(2)}) collective-permute-start(bf16[128,2048]{1,0:T(8,128)(2,1)S(1)} %convert_element_type.3.own_ref.refs_4_), channel_id=1, source_target_pairs={{0,4},{1,5},{2,3},{3,2},{4,0},{5,1},{6,7},{7,6},{8,12},{9,13},{10,... | collective-permute-start | bytes 1572872 | tf_op jit(solution)/shard_map/ppermute | solution.py:297
  6.5 25.3 %collective-permute-start = (bf16[128,2048]{1,0:T(8,128)(2,1)S(1)}, bf16[128,2048]{1,0:T(8,128)(2,1)S(1)}, u32[]{:S(2)}, u32[]{:S(2)}) collective-permute-start(bf16[128,2048]{1,0:T(8,128)(2,1)S(1)} %convert_element_type.3.own_ref.refs_4_), channel_id=1, source_target_pairs={{0,16},{1,17},{2,18},{3,19},{4,20},{5,21},{6,22},{7,23},{8,24},{9,... | collective-permute-start | bytes 1572872 | tf_op jit(solution)/shard_map/ppermute | solution.py:297
  9.1 22.9 %collective-permute-start.1 = (bf16[128,2048]{1,0:T(8,128)(2,1)S(1)}, bf16[128,2048]{1,0:T(8,128)(2,1)S(1)}, u32[]{:S(2)}, u32[]{:S(2)}) collective-permute-start(bf16[128,2048]{1,0:T(8,128)(2,1)S(1)} %convert_element_type.3.own_ref.refs_4_), channel_id=1, source_target_pairs={{0,8},{1,9},{2,10},{3,11},{4,12},{5,13},{6,14},{7,15},{8,0},{9,1},... | collective-permute-start | bytes 1572872 | tf_op jit(solution)/shard_map/ppermute | solution.py:297
  17.2 14.8 %collective-permute-start.4 = (bf16[128,2048]{1,0:T(8,128)(2,1)S(1)}, bf16[128,2048]{1,0:T(8,128)(2,1)S(1)}, u32[]{:S(2)}, u32[]{:S(2)}) collective-permute-start(bf16[128,2048]{1,0:T(8,128)(2,1)S(1)} %collective-permute-done.2.first_ref.refs_5_), channel_id=1, source_target_pairs={{0,4},{1,5},{2,3},{3,2},{4,0},{5,1},{6,7},{7,6},{8,12},{9,13},{10,... | collective-permute-start | bytes 1572872 | tf_op jit(solution)/shard_map/ppermute | solution.py:297
  24.6 3.7 %collective-permute-start.5 = (f32[8,256]{1,0:T(8,128)S(1)}, f32[8,256]{1,0:T(8,128)S(1)}, u32[]{:S(2)}, u32[]{:S(2)}) collective-permute-start(f32[8,256]{1,0:T(8,128)S(1)} %get-tuple-element.52.mine_ref), channel_id=1, source_target_pairs={{0,1},{1,0},{2,3},{3,2},{4,5},{5,4},{6,7},{7,6},{8,9},{9,8},{10,11... | collective-permute-start | bytes 24584 | tf_op jit(solution)/shard_map/ppermute | solution.py:297
  32.0 12.7 %collective-permute-start.6 = (bf16[128,2048]{1,0:T(8,128)(2,1)S(1)}, bf16[128,2048]{1,0:T(8,128)(2,1)S(1)}, u32[]{:S(2)}, u32[]{:S(2)}) collective-permute-start(bf16[128,2048]{1,0:T(8,128)(2,1)S(1)} %collective-permute-done.refs_5_), channel_id=1, source_target_pairs={{0,1},{1,0},{2,6},{3,7},{4,5},{5,4},{6,2},{7,3},{8,9},{9,8},{10,14... | collective-permute-start | bytes 1572872 | tf_op jit(solution)/shard_map/ppermute | solution.py:297
  32.5 12.2 %collective-permute-start.7 = (bf16[128,2048]{1,0:T(8,128)(2,1)S(1)}, bf16[128,2048]{1,0:T(8,128)(2,1)S(1)}, u32[]{:S(2)}, u32[]{:S(2)}) collective-permute-start(bf16[128,2048]{1,0:T(8,128)(2,1)S(1)} %collective-permute-done.refs_5_), channel_id=1, source_target_pairs={{0,4},{1,5},{2,3},{3,2},{4,0},{5,1},{6,7},{7,6},{8,12},{9,13},{10,... | collective-permute-start | bytes 1572872 | tf_op jit(solution)/shard_map/ppermute | solution.py:297
  33.0 12.0 %collective-permute-start.8 = (bf16[128,2048]{1,0:T(8,128)(2,1)S(1)}, bf16[128,2048]{1,0:T(8,128)(2,1)S(1)}, u32[]{:S(2)}, u32[]{:S(2)}) collective-permute-start(bf16[128,2048]{1,0:T(8,128)(2,1)S(1)} %collective-permute-done.refs_5_), channel_id=1, source_target_pairs={{0,8},{1,9},{2,10},{3,11},{4,12},{5,13},{6,14},{7,15},{8,0},{9,1},... | collective-permute-start | bytes 1572872 | tf_op jit(solution)/shard_map/ppermute | solution.py:297
  34.5 10.2 %collective-permute-start.9 = (f32[2,8,128]{2,1,0:T(8,128)S(1)}, f32[2,8,128]{2,1,0:T(8,128)S(1)}, u32[]{:S(2)}, u32[]{:S(2)}) collective-permute-start(f32[2,8,128]{2,1,0:T(8,128)S(1)} %meta.1), channel_id=1, source_target_pairs={{0,4},{1,5},{2,6},{3,7},{4,0},{5,1},{6,2},{7,3},{8,12},{9,13},{10,... | collective-permute-start | bytes 24584 | tf_op jit(solution)/shard_map/ppermute | solution.py:297
  45.0 19.7 %collective-permute-start.12 = (bf16[128,2048]{1,0:T(8,128)(2,1)S(1)}, bf16[128,2048]{1,0:T(8,128)(2,1)S(1)}, u32[]{:S(2)}, u32[]{:S(2)}) collective-permute-start(bf16[128,2048]{1,0:T(8,128)(2,1)S(1)} %collective-permute-done.6.refs_6_), channel_id=1, source_target_pairs={{0,4},{1,5},{2,3},{3,2},{4,0},{5,1},{6,7},{7,6},{8,12},{9,13},{10,... | collective-permute-start | bytes 1572872 | tf_op jit(solution)/shard_map/ppermute | solution.py:297
  46.5 18.2 %collective-permute-start.13 = (bf16[128,2048]{1,0:T(8,128)(2,1)S(1)}, bf16[128,2048]{1,0:T(8,128)(2,1)S(1)}, u32[]{:S(2)}, u32[]{:S(2)}) collective-permute-start(bf16[128,2048]{1,0:T(8,128)(2,1)S(1)} %collective-permute-done.8.refs_5_), channel_id=1, source_target_pairs={{0,1},{1,0},{2,6},{3,7},{4,5},{5,4},{6,2},{7,3},{8,9},{9,8},{10,14... | collective-permute-start | bytes 1572872 | tf_op jit(solution)/shard_map/ppermute | solution.py:297
  48.0 19.3 %collective-permute-start.19 = (bf16[128,2048]{1,0:T(8,128)(2,1)S(1)}, bf16[128,2048]{1,0:T(8,128)(2,1)S(1)}, u32[]{:S(2)}, u32[]{:S(2)}) collective-permute-start(bf16[128,2048]{1,0:T(8,128)(2,1)S(1)} %collective-permute-done.8.refs_5_), channel_id=1, source_target_pairs={{0,4},{1,5},{2,3},{3,2},{4,0},{5,1},{6,7},{7,6},{8,12},{9,13},{10,... | collective-permute-start | bytes 1572872 | tf_op jit(solution)/shard_map/ppermute | solution.py:297
  48.5 3.7 %collective-permute-start.10 = (f32[4,8,128]{2,1,0:T(8,128)S(1)}, f32[4,8,128]{2,1,0:T(8,128)S(1)}, u32[]{:S(2)}, u32[]{:S(2)}) collective-permute-start(f32[4,8,128]{2,1,0:T(8,128)S(1)} %pad_maximum_fusion), channel_id=1, source_target_pairs={{0,8},{1,9},{2,10},{3,11},{4,12},{5,13},{6,14},{7,15},{8,0},{9,1},... | collective-permute-start | bytes 49160 | tf_op jit(solution)/shard_map/ppermute | solution.py:297
  52.3 5.3 %collective-permute-start.11 = (f32[8,8,128]{2,1,0:T(8,128)S(1)}, f32[8,8,128]{2,1,0:T(8,128)S(1)}, u32[]{:S(2)}, u32[]{:S(2)}) collective-permute-start(f32[8,8,128]{2,1,0:T(8,128)S(1)} %constant_dynamic-update-slice_fusion.refs_2_), channel_id=1, source_target_pairs={{0,16},{1,17},{2,18},{3,19},{4,20},{5,21},{6,22},{7,23},{8,24},{9,... | collective-permute-start | bytes 98312 | tf_op jit(solution)/shard_map/ppermute | solution.py:297
  57.6 16.7 %collective-permute-start.17 = (bf16[128,2048]{1,0:T(8,128)(2,1)S(1)}, bf16[128,2048]{1,0:T(8,128)(2,1)S(1)}, u32[]{:S(2)}, u32[]{:S(2)}) collective-permute-start(bf16[128,2048]{1,0:T(8,128)(2,1)S(1)} %collective-permute-done.4.refs_7_), channel_id=1, source_target_pairs={{0,8},{1,9},{2,10},{3,11},{4,12},{5,13},{6,14},{7,15},{8,0},{9,1},... | collective-permute-start | bytes 1572872 | tf_op jit(solution)/shard_map/ppermute | solution.py:297
  64.7 13.5 %collective-permute-start.14 = (bf16[128,2048]{1,0:T(8,128)(2,1)S(1)}, bf16[128,2048]{1,0:T(8,128)(2,1)S(1)}, u32[]{:S(2)}, u32[]{:S(2)}) collective-permute-start(bf16[128,2048]{1,0:T(8,128)(2,1)S(1)} %collective-permute-done.1.refs_4_), channel_id=1, source_target_pairs={{0,1},{1,0},{2,6},{3,7},{4,5},{5,4},{6,2},{7,3},{8,9},{9,8},{10,14... | collective-permute-start | bytes 1572872 | tf_op jit(solution)/shard_map/ppermute | solution.py:297
  65.3 12.9 %collective-permute-start.18 = (bf16[128,2048]{1,0:T(8,128)(2,1)S(1)}, bf16[128,2048]{1,0:T(8,128)(2,1)S(1)}, u32[]{:S(2)}, u32[]{:S(2)}) collective-permute-start(bf16[128,2048]{1,0:T(8,128)(2,1)S(1)} %collective-permute-done.13.refs_6_), channel_id=1, source_target_pairs={{0,4},{1,5},{2,3},{3,2},{4,0},{5,1},{6,7},{7,6},{8,12},{9,13},{10,... | collective-permute-start | bytes 1572872 | tf_op jit(solution)/shard_map/ppermute | solution.py:297
  67.2 7.2 %collective-permute-start.15 = (bf16[64,2048]{1,0:T(8,128)(2,1)S(1)}, bf16[64,2048]{1,0:T(8,128)(2,1)S(1)}, u32[]{:S(2)}, u32[]{:S(2)}) collective-permute-start(bf16[64,2048]{1,0:T(8,128)(2,1)S(1)} %slice.6), channel_id=1, source_target_pairs={{0,8},{1,9},{2,10},{3,11},{4,12},{5,13},{6,14},{7,15},{8,0},{9,1},... | collective-permute-start | bytes 786440 | tf_op jit(solution)/shard_map/ppermute | solution.py:297
  67.3 10.8 %collective-permute-start.16 = (bf16[64,2048]{1,0:T(8,128)(2,1)S(1)}, bf16[64,2048]{1,0:T(8,128)(2,1)S(1)}, u32[]{:S(2)}, u32[]{:S(2)}) collective-permute-start(bf16[64,2048]{1,0:T(8,128)(2,1)S(1)} %slice.7), channel_id=1, source_target_pairs={{0,4},{1,5},{2,3},{3,2},{4,0},{5,1},{6,7},{7,6},{8,12},{9,13},{10,... | collective-permute-start | bytes 786440 | tf_op jit(solution)/shard_map/ppermute | solution.py:297
  80.9 2.8 %collective-permute-start.20 = (bf16[256,2176]{1,0:T(8,128)(2,1)S(1)}, bf16[256,2176]{1,0:T(8,128)(2,1)S(1)}, u32[]{:S(2)}, u32[]{:S(2)}) collective-permute-start(bf16[256,2176]{1,0:T(8,128)(2,1)S(1)} %get-tuple-element.87), channel_id=1, source_target_pairs={{0,2},{1,3},{2,0},{3,1},{4,6},{5,7},{6,4},{7,5},{8,10},{9,11},{10,... | collective-permute-start | bytes 3342344 | tf_op jit(solution)/shard_map/ppermute | solution.py:444

commit v5 on v4

--- a/solution.py
+++ b/solution.py
@@ -243,14 +243,15 @@
     if not first:
         seen += cnt_ref[...]
     if last:
-        kept_ref, kept_cnt_ref, sent_ref = outs
+        kept_weights_ref, kept_cnt_ref, sent_ref = outs
         half_width = width // 2
         keep = pl.ds(pl.multiple_of(core * half_width, half_width), half_width)
         send = pl.ds(pl.multiple_of((1 - core) * half_width, half_width), half_width)
         seen_buf[...] = jnp.broadcast_to(jnp.sum(seen, axis=1, keepdims=True), seen.shape)
         kept_cnt_ref[...] = seen_buf[keep, :]
         sent_ref[:, columns:] = seen_buf[send, :].astype(jnp.bfloat16)
-        targets = ((send, sent_ref), (keep, kept_ref))
+        kept_weights_ref[...] = weights_buf[keep, :]
+        targets = ((send, sent_ref),)
     else:
         outs[1][...] = seen
         targets = ((pl.ds(0, width), outs[0]),)
@@ -269,6 +270,27 @@
             out[:, part] = sums.astype(out.dtype)
 
 
+def keep_kernel(acc_ref, weights_ref, *refs):
+    pieces, (kept_ref, rows_buf) = refs[:-2], refs[-2:]
+    done = 0
+    for piece in pieces:
+        n = piece.shape[0]
+        rows_buf[done : done + n, :] = piece[...]
+        done += n
+    rows, columns = kept_ref.shape
+    core = lax.rem(lax.axis_index("img"), cores)
+    keep = pl.ds(pl.multiple_of(core * rows, rows), rows)
+    chunk = min(columns, 512)
+    for c in range(0, columns, chunk):
+        part = slice(c, c + chunk)
+        kept_ref[:, part] = acc_ref[keep, part] + lax.dot_general(
+            weights_ref[...],
+            rows_buf[:, part],
+            (((1,), (0,)), ((), ())),
+            preferred_element_type=jnp.float32,
+        )
+
+
 def final_kernel(kept_ref, kept_cnt_ref, got_ref, proj_ref, out_ref):
     rows, columns = out_ref.shape
     core = lax.rem(lax.axis_index("img"), cores)
@@ -395,8 +417,8 @@
     metas = jnp.concatenate([metas, swap(metas, (2, 0))], axis=0)
     metas = [metas, swap(metas, (4, 0))]
     metas, own_b, own_c = together((metas, own_b, own_c))
-    half_shard = shard // 2
-    near_b = moved(own_b[0], (2, 0)), swap(own_b[1][:half_shard], (2, 0))
+    by_z = shard // 4 * 3
+    near_b = moved(own_b[0], (2, 0)), swap(own_b[1][:by_z], (2, 0))
     near_c = sent(own_c, (2, 0))
 
     def add(group, state, last):
@@ -406,7 +428,7 @@
         first = state is None
         if last:
             out_shape = [
-                jax.ShapeDtypeStruct((width // 2, columns), f32),
+                jax.ShapeDtypeStruct((width // 2, images_here), jnp.bfloat16),
                 jax.ShapeDtypeStruct((width // 2, lanes), f32),
                 jax.ShapeDtypeStruct((width // 2, columns + lanes), jnp.bfloat16),
             ]
@@ -437,11 +459,23 @@
     state, near_slab, far_c, last_a = together((state, near_slab, far_c, last_a))
     last_c = sent(last_a, *far)
     near_a = sent(near_slab, *near)
-    near_b_low = (), swap(near_slab[1][half_shard:], *far)
+    near_b_low = (), swap(near_slab[1][by_z:], *far)
     state, last_b = together((state, last_b))
     state = add([far_c, last_slab, last_a, last_b], state, False)
-    kept, kept_cnt, sent_away = add([near_a, near_b, near_b_low, near_c, last_c], state, True)
+    final_group = [near_a, near_b, near_b_low, near_c, last_c]
+    kept_weights, kept_cnt, sent_away = add(final_group, state, True)
     got = lax.ppermute(sent_away, both, [(i, i ^ n_ori) for i in range(n)])
+    last_pieces = [a for _, a in final_group]
+    kept = pl.pallas_call(
+        keep_kernel,
+        in_specs=[vmem] * (2 + len(last_pieces)),
+        out_specs=vmem,
+        out_shape=jax.ShapeDtypeStruct((width // 2, columns), f32),
+        scratch_shapes=[pltpu.VMEM((kept_weights.shape[1], columns), jnp.bfloat16)],
+        compiler_params=limit,
+        cost_estimate=pl.CostEstimate(flops=0, bytes_accessed=0, transcendentals=0),
+        name="keep",
+    )(state[0], kept_weights, *last_pieces)
     out_rows = width // 2
     cut = 4
     refined = pl.pallas_call(

time: 85.9 us -> 84.3 us (0.981)
  waiting for transfers between devices: 26 us -> 24.2 us
    ppermute x20, waiting for transfers between devices: 23.3 us -> 22.2 us  [swap(): lax.ppermute(a, both, [(i, i ^ masks[i // n_ori % cores]) for i in range(...]
  transfers between devices with their start and end apart: 21 -> 21, of which waited for: 12 -> 10; matrix products, arithmetic and copies ran while one was open for 0% -> 0% of each run, Pallas kernels for 28% -> 29%
where the time goes in v5:
time: 84.3 us; the launch traced here: 84.2 us
  starting transfers between devices  29.3 us (35%)
  Pallas kernels  28.6 us (34%)
  waiting for transfers between devices  24.2 us (29%)
  other arithmetic  1.29 us (2%)
    ppermute x20, starting transfers between devices, swap(): lax.ppermute(a, both, [(i, i ^ masks[i // n_ori % cores]) for i in range(...  29.2 us
    ppermute x20, waiting for transfers between devices, swap(): lax.ppermute(a, both, [(i, i ^ masks[i // n_ori % cores]) for i in range(...  22.2 us
    pallas_call x4, Pallas kernels, add(): pl.pallas_call(functools.partial(sums_kernel, len(metas), tiles * cores /...  10.3 us
    pallas_call x1, Pallas kernels, gathered_body(): pl.pallas_call(functools.partial(load_kernel, chips), in_specs=[pl.BlockS...  6.53 us
    pallas_call x1, Pallas kernels, gathered_body(): pl.pallas_call(functools.partial(scores_kernel, chips), in_specs=[smem] +...  5.83 us
    pallas_call x1, Pallas kernels, gathered_body(): pl.pallas_call(posterior_kernel, grid=(cut,), in_specs=[vmem, pl.BlockSpe...  2.55 us
    ppermute x1, waiting for transfers between devices, gathered_body(): got = lax.ppermute(sent_away, both, [(i, i ^ n_ori) for i in range(n)])  2.02 us
    pallas_call x1, Pallas kernels, gathered_body(): pl.pallas_call(final_kernel, grid=(cut,), in_specs=[vmem] * 4, out_specs=...  1.99 us
  transfers between devices with their start and end apart: 21, of which 10 were waited for; matrix products, arithmetic and copies ran while one was open for 0% of the time, Pallas kernels for 29%

profile of v5, /device:TPU:0, one launch (start us, length us, event | category | flops | bytes accessed | tf_op | source)
XLA Modules:
  0.0 84.2 jit_solution(14471490658428671064)
XLA Ops:
  0.6 1.3 %convert_element_type.3.own_ref.refs_4_ = bf16[128,2048]{1,0:T(8,128)(2,1)S(1)} convert(f32[128,2048]{1,0:T(8,128)} %param.4) | non-fusion elementwise | flops 262144 | bytes 1572864 | tf_op jit(solution)/shard_map/convert_element_type | solution.py:338
  1.9 0.0 copy-start
  1.9 0.0 copy-start.1
  1.9 3.0 %collective-permute-start.2 = (bf16[128,2048]{1,0:T(8,128)(2,1)S(1)}, bf16[128,2048]{1,0:T(8,128)(2,1)S(1)}, u32[]{:S(2)}, u32[]{:S(2)}) collective-permute-start(bf16[128,2048]{1,0:T(8,128)(2,1)S(1)} %convert_element_type.3.own_ref.refs_4_), channel_id=1, source_target_pairs={{0,1},{1,0},{2,6},{3,7},{4,5},{5,4},{6,2},{7,3},{8,9},{9,8},{10,14... | collective-permute-start | bytes 1572872 | tf_op jit(solution)/shard_map/ppermute | solution.py:319
  5.0 1.5 %collective-permute-start.3 = (bf16[128,2048]{1,0:T(8,128)(2,1)S(1)}, bf16[128,2048]{1,0:T(8,128)(2,1)S(1)}, u32[]{:S(2)}, u32[]{:S(2)}) collective-permute-start(bf16[128,2048]{1,0:T(8,128)(2,1)S(1)} %convert_element_type.3.own_ref.refs_4_), channel_id=1, source_target_pairs={{0,4},{1,5},{2,3},{3,2},{4,0},{5,1},{6,7},{7,6},{8,12},{9,13},{10,... | collective-permute-start | bytes 1572872 | tf_op jit(solution)/shard_map/ppermute | solution.py:319
  6.5 2.6 %collective-permute-start = (bf16[128,2048]{1,0:T(8,128)(2,1)S(1)}, bf16[128,2048]{1,0:T(8,128)(2,1)S(1)}, u32[]{:S(2)}, u32[]{:S(2)}) collective-permute-start(bf16[128,2048]{1,0:T(8,128)(2,1)S(1)} %convert_element_type.3.own_ref.refs_4_), channel_id=1, source_target_pairs={{0,16},{1,17},{2,18},{3,19},{4,20},{5,21},{6,22},{7,23},{8,24},{9,... | collective-permute-start | bytes 1572872 | tf_op jit(solution)/shard_map/ppermute | solution.py:319
  9.1 1.6 %collective-permute-start.1 = (bf16[128,2048]{1,0:T(8,128)(2,1)S(1)}, bf16[128,2048]{1,0:T(8,128)(2,1)S(1)}, u32[]{:S(2)}, u32[]{:S(2)}) collective-permute-start(bf16[128,2048]{1,0:T(8,128)(2,1)S(1)} %convert_element_type.3.own_ref.refs_4_), channel_id=1, source_target_pairs={{0,8},{1,9},{2,10},{3,11},{4,12},{5,13},{6,14},{7,15},{8,0},{9,1},... | collective-permute-start | bytes 1572872 | tf_op jit(solution)/shard_map/ppermute | solution.py:319
  10.6 6.5 %load.1 = (bf16[4096,2048]{1,0:T(8,128)(2,1)S(1)}, bf16[512,2048]{1,0:T(8,128)(2,1)S(1)}, f32[8,4096]{1,0:T(8,128)S(1)}, f32[512,128]{1,0:T(8,128)S(1)}) custom-call(bf16[4096,2048]{1,0:T(8,128)(2,1)} %away_ref.1), custom_call_target="tpu_custom_call" | custom-call | tf_op jit(solution)/shard_map/load/pallas_call | solution.py:345
  17.2 0.0 collective-permute-done.2.first_ref.refs_5_
  17.2 0.0 collective-permute-done.3.second_ref.refs_6_
  17.2 1.5 %collective-permute-start.4 = (bf16[128,2048]{1,0:T(8,128)(2,1)S(1)}, bf16[128,2048]{1,0:T(8,128)(2,1)S(1)}, u32[]{:S(2)}, u32[]{:S(2)}) collective-permute-start(bf16[128,2048]{1,0:T(8,128)(2,1)S(1)} %collective-permute-done.2.first_ref.refs_5_), channel_id=1, source_target_pairs={{0,4},{1,5},{2,3},{3,2},{4,0},{5,1},{6,7},{7,6},{8,12},{9,13},{10,... | collective-permute-start | bytes 1572872 | tf_op jit(solution)/shard_map/ppermute | solution.py:319
  18.7 0.0 copy-done
  18.7 0.0 copy-done.1
  18.7 5.8 %scores.1 = (f32[256,4096]{1,0:T(8,128)S(1)}, f32[8,256]{1,0:T(8,128)S(1)}) custom-call(s32[2,32]{1,0:T(2,128)S(1)} %copy-done, f32[1,256]{1,0:T(1,128)S(1)} %bitcast.1, f32[8,4096]{1,0:T(8,128)S(1)} %get-tuple-element.49.half_ref, bf16[128,2048]{1,0:T(8,128)(2,1)S(1)} %convert_element_type.3.own_ref.refs_4_, ...), custom_call_target="tpu_custom_call" | custom-call | tf_op jit(solution)/shard_map/scores/pallas_call | solution.py:366
  24.6 1.7 %collective-permute-start.5 = (f32[8,256]{1,0:T(8,128)S(1)}, f32[8,256]{1,0:T(8,128)S(1)}, u32[]{:S(2)}, u32[]{:S(2)}) collective-permute-start(f32[8,256]{1,0:T(8,128)S(1)} %get-tuple-element.52.mine_ref), channel_id=1, source_target_pairs={{0,1},{1,0},{2,3},{3,2},{4,5},{5,4},{6,7},{7,6},{8,9},{9,8},{10,11... | collective-permute-start | bytes 24584 | tf_op jit(solution)/shard_map/ppermute | solution.py:319
  26.2 2.0 %collective-permute-done.5.theirs_ref = f32[8,256]{1,0:T(8,128)S(1)} collective-permute-done((f32[8,256]{1,0:T(8,128)S(1)}, f32[8,256]{1,0:T(8,128)S(1)}, u32[]{:S(2)}, u32[]{:S(2)}) %collective-permute-start.5) | collective-permute-done | bytes 8224 | tf_op jit(solution)/shard_map/ppermute | solution.py:319
  28.3 0.6 meta.1
  28.9 2.9 %collective-permute-done.refs_5_ = bf16[128,2048]{1,0:T(8,128)(2,1)S(1)} collective-permute-done((bf16[128,2048]{1,0:T(8,128)(2,1)S(1)}, bf16[128,2048]{1,0:T(8,128)(2,1)S(1)}, u32[]{:S(2)}, u32[]{:S(2)}) %collective-permute-start) | collective-permute-done | bytes 524320 | tf_op jit(solution)/shard_map/ppermute | solution.py:319
  31.8 0.2 collective-permute-done.1.refs_4_
  32.0 0.0 collective-permute-done.4.refs_7_
  32.0 0.5 collective-permute-start.6
  32.5 0.5 collective-permute-start.7
  33.0 1.5 %collective-permute-start.8 = (bf16[128,2048]{1,0:T(8,128)(2,1)S(1)}, bf16[128,2048]{1,0:T(8,128)(2,1)S(1)}, u32[]{:S(2)}, u32[]{:S(2)}) collective-permute-start(bf16[128,2048]{1,0:T(8,128)(2,1)S(1)} %collective-permute-done.refs_5_), channel_id=1, source_target_pairs={{0,8},{1,9},{2,10},{3,11},{4,12},{5,13},{6,14},{7,15},{8,0},{9,1},... | collective-permute-start | bytes 1572872 | tf_op jit(solution)/shard_map/ppermute | solution.py:319
  34.5 1.5 %collective-permute-start.9 = (f32[2,8,128]{2,1,0:T(8,128)S(1)}, f32[2,8,128]{2,1,0:T(8,128)S(1)}, u32[]{:S(2)}, u32[]{:S(2)}) collective-permute-start(f32[2,8,128]{2,1,0:T(8,128)S(1)} %meta.1), channel_id=1, source_target_pairs={{0,4},{1,5},{2,6},{3,7},{4,0},{5,1},{6,2},{7,3},{8,12},{9,13},{10,... | collective-permute-start | bytes 24584 | tf_op jit(solution)/shard_map/ppermute | solution.py:319
  36.0 2.6 %posterior.1 = bf16[256,4096]{1,0:T(8,128)(2,1)} custom-call(f32[256,4096]{1,0:T(8,128)S(1)} %get-tuple-element.56.scores_ref, f32[8,256]{1,0:T(8,128)S(1)} %get-tuple-element.52.mine_ref, f32[8,256]{1,0:T(8,128)S(1)} %collective-permute-done.5.theirs_ref), custom_call_target="tpu_custom_call" | custom-call | tf_op jit(solution)/shard_map/posterior/pallas_call | solution.py:396
  38.6 6.1 %collective-permute-done.9 = f32[2,8,128]{2,1,0:T(8,128)S(1)} collective-permute-done((f32[2,8,128]{2,1,0:T(8,128)S(1)}, f32[2,8,128]{2,1,0:T(8,128)S(1)}, u32[]{:S(2)}, u32[]{:S(2)}) %collective-permute-start.9) | collective-permute-done | bytes 8224 | tf_op jit(solution)/shard_map/ppermute | solution.py:319
  44.7 0.1 collective-permute-done.6.refs_6_
  44.8 0.0 collective-permute-done.7.refs_7_
  44.8 0.2 collective-permute-done.8.refs_5_
  45.0 1.6 %collective-permute-start.12 = (bf16[128,2048]{1,0:T(8,128)(2,1)S(1)}, bf16[128,2048]{1,0:T(8,128)(2,1)S(1)}, u32[]{:S(2)}, u32[]{:S(2)}) collective-permute-start(bf16[128,2048]{1,0:T(8,128)(2,1)S(1)} %collective-permute-done.6.refs_6_), channel_id=1, source_target_pairs={{0,4},{1,5},{2,3},{3,2},{4,0},{5,1},{6,7},{7,6},{8,12},{9,13},{10,... | collective-permute-start | bytes 1572872 | tf_op jit(solution)/shard_map/ppermute | solution.py:319
  46.5 1.5 %collective-permute-start.13 = (bf16[128,2048]{1,0:T(8,128)(2,1)S(1)}, bf16[128,2048]{1,0:T(8,128)(2,1)S(1)}, u32[]{:S(2)}, u32[]{:S(2)}) collective-permute-start(bf16[128,2048]{1,0:T(8,128)(2,1)S(1)} %collective-permute-done.8.refs_5_), channel_id=1, source_target_pairs={{0,1},{1,0},{2,6},{3,7},{4,5},{5,4},{6,2},{7,3},{8,9},{9,8},{10,14... | collective-permute-start | bytes 1572872 | tf_op jit(solution)/shard_map/ppermute | solution.py:319
  48.0 0.5 collective-permute-start.14
  48.5 1.7 %collective-permute-start.10 = (f32[4,8,128]{2,1,0:T(8,128)S(1)}, f32[4,8,128]{2,1,0:T(8,128)S(1)}, u32[]{:S(2)}, u32[]{:S(2)}) collective-permute-start(f32[4,8,128]{2,1,0:T(8,128)S(1)} %pad_maximum_fusion), channel_id=1, source_target_pairs={{0,8},{1,9},{2,10},{3,11},{4,12},{5,13},{6,14},{7,15},{8,0},{9,1},... | collective-permute-start | bytes 49160 | tf_op jit(solution)/shard_map/ppermute | solution.py:319
  50.2 2.0 %collective-permute-done.10 = f32[4,8,128]{2,1,0:T(8,128)S(1)} collective-permute-done((f32[4,8,128]{2,1,0:T(8,128)S(1)}, f32[4,8,128]{2,1,0:T(8,128)S(1)}, u32[]{:S(2)}, u32[]{:S(2)}) %collective-permute-start.10) | collective-permute-done | bytes 16416 | tf_op jit(solution)/shard_map/ppermute | solution.py:319
  52.3 3.3 %collective-permute-start.11 = (f32[8,8,128]{2,1,0:T(8,128)S(1)}, f32[8,8,128]{2,1,0:T(8,128)S(1)}, u32[]{:S(2)}, u32[]{:S(2)}) collective-permute-start(f32[8,8,128]{2,1,0:T(8,128)S(1)} %constant_dynamic-update-slice_fusion.refs_2_), channel_id=1, source_target_pairs={{0,16},{1,17},{2,18},{3,19},{4,20},{5,21},{6,22},{7,23},{8,24},{9,... | collective-permute-start | bytes 98312 | tf_op jit(solution)/shard_map/ppermute | solution.py:319
  55.6 2.0 %collective-permute-done.11.refs_3_ = f32[8,8,128]{2,1,0:T(8,128)S(1)} collective-permute-done((f32[8,8,128]{2,1,0:T(8,128)S(1)}, f32[8,8,128]{2,1,0:T(8,128)S(1)}, u32[]{:S(2)}, u32[]{:S(2)}) %collective-permute-start.11) | collective-permute-done | bytes 32800 | tf_op jit(solution)/shard_map/ppermute | solution.py:319
  57.6 1.6 %collective-permute-start.18 = (bf16[128,2048]{1,0:T(8,128)(2,1)S(1)}, bf16[128,2048]{1,0:T(8,128)(2,1)S(1)}, u32[]{:S(2)}, u32[]{:S(2)}) collective-permute-start(bf16[128,2048]{1,0:T(8,128)(2,1)S(1)} %collective-permute-done.4.refs_7_), channel_id=1, source_target_pairs={{0,8},{1,9},{2,10},{3,11},{4,12},{5,13},{6,14},{7,15},{8,0},{9,1},... | collective-permute-start | bytes 1572872 | tf_op jit(solution)/shard_map/ppermute | solution.py:319
  59.3 2.7 %sums.4 = (f32[512,2048]{1,0:T(8,128)S(1)}, f32[512,128]{1,0:T(8,128)S(1)}) custom-call(f32[512,128]{1,0:T(8,128)S(1)} %get-tuple-element.58.refs_0_, bf16[512,2048]{1,0:T(8,128)(2,1)S(1)} %get-tuple-element.59.refs_1_.proj_ref, f32[8,8,128]{2,1,0:T(8,128)S(1)} %constant_dynamic-update-slice_fusion.refs_2_, ...), custom_call_target="tpu_custom_call" | custom-call | tf_op jit(solution)/shard_map/sums/pallas_call | solution.py:441
  61.9 2.7 %sums.5 = (f32[512,2048]{1,0:T(8,128)S(1)}, f32[512,128]{1,0:T(8,128)S(1)}) custom-call(f32[512,128]{1,0:T(8,128)S(1)} %get-tuple-element.58.refs_0_, bf16[512,2048]{1,0:T(8,128)(2,1)S(1)} %get-tuple-element.59.refs_1_.proj_ref, f32[8,8,128]{2,1,0:T(8,128)S(1)} %constant_dynamic-update-slice_fusion.refs_2_, ...), custom_call_target="tpu_custom_call", output_to_operand_aliasing={{0}: (8, {}), {1}: (9, {})} | custom-call | tf_op jit(solution)/shard_map/sums/pallas_call | solution.py:441
  64.7 0.0 collective-permute-done.12.refs_4_
  64.7 0.0 collective-permute-done.13.refs_6_
  64.7 0.6 collective-permute-start.15
  65.3 1.9 %collective-permute-start.19 = (bf16[128,2048]{1,0:T(8,128)(2,1)S(1)}, bf16[128,2048]{1,0:T(8,128)(2,1)S(1)}, u32[]{:S(2)}, u32[]{:S(2)}) collective-permute-start(bf16[128,2048]{1,0:T(8,128)(2,1)S(1)} %collective-permute-done.13.refs_6_), channel_id=1, source_target_pairs={{0,4},{1,5},{2,3},{3,2},{4,0},{5,1},{6,7},{7,6},{8,12},{9,13},{10,... | collective-permute-start | bytes 1572872 | tf_op jit(solution)/shard_map/ppermute | solution.py:319
  67.2 0.1 collective-permute-start.16
  67.3 0.0 collective-permute-done.14.refs_7_
  67.3 0.5 collective-permute-start.17
  67.8 2.7 %sums.6 = (f32[512,2048]{1,0:T(8,128)S(1)}, f32[512,128]{1,0:T(8,128)S(1)}) custom-call(f32[512,128]{1,0:T(8,128)S(1)} %get-tuple-element.58.refs_0_, bf16[512,2048]{1,0:T(8,128)(2,1)S(1)} %get-tuple-element.59.refs_1_.proj_ref, f32[8,8,128]{2,1,0:T(8,128)S(1)} %constant_dynamic-update-slice_fusion.refs_2_, ...), custom_call_target="tpu_custom_call", output_to_operand_aliasing={{0}: (8, {}), {1}: (9, {})} | custom-call | tf_op jit(solution)/shard_map/sums/pallas_call | solution.py:441
  70.6 6.6 %collective-permute-done.16.refs_5_.refs_1_ = bf16[96,2048]{1,0:T(8,128)(2,1)S(1)} collective-permute-done((bf16[96,2048]{1,0:T(8,128)(2,1)S(1)}, bf16[96,2048]{1,0:T(8,128)(2,1)S(1)}, u32[]{:S(2)}, u32[]{:S(2)}) %collective-permute-start.16) | collective-permute-done | bytes 393248 | tf_op jit(solution)/shard_map/ppermute | solution.py:319
  77.2 0.0 collective-permute-done.18.refs_7_.refs_3_
  77.2 0.0 collective-permute-done.17.refs_6_.refs_2_
  77.2 0.0 collective-permute-done.15.refs_4_.refs_0_
  77.2 0.0 collective-permute-done.19.refs_8_.refs_4_
  77.2 2.2 %sums.7 = (bf16[256,512]{1,0:T(8,128)(2,1)S(1)}, f32[256,128]{1,0:T(8,128)S(1)}, bf16[256,2176]{1,0:T(8,128)(2,1)S(1)}) custom-call(f32[512,128]{1,0:T(8,128)S(1)} %get-tuple-element.58.refs_0_, bf16[512,2048]{1,0:T(8,128)(2,1)S(1)} %get-tuple-element.59.refs_1_.proj_ref, f32[8,8,128]{2,1,0:T(8,128)S(1)} %constant_dynamic-update-slice_fusion.refs_2_, ...), custom_call_target="tpu_custom_call" | custom-call | tf_op jit(solution)/shard_map/sums/pallas_call | solution.py:441
  79.4 0.1 collective-permute-start.20
  79.5 0.7 keep.1.kept_ref
  80.2 2.0 %collective-permute-done.20.got_ref = bf16[256,2176]{1,0:T(8,128)(2,1)S(1)} collective-permute-done((bf16[256,2176]{1,0:T(8,128)(2,1)S(1)}, bf16[256,2176]{1,0:T(8,128)(2,1)S(1)}, u32[]{:S(2)}, u32[]{:S(2)}) %collective-permute-start.20) | collective-permute-done | bytes 1114144 | tf_op jit(solution)/shard_map/ppermute | solution.py:467
  82.2 2.0 %final.1 = f32[256,2048]{1,0:T(8,128)} custom-call(f32[256,2048]{1,0:T(8,128)S(1)} %keep.1.kept_ref, f32[256,128]{1,0:T(8,128)S(1)} %get-tuple-element.86.kept_cnt_ref, bf16[256,2176]{1,0:T(8,128)(2,1)S(1)} %collective-permute-done.20.got_ref, bf16[512,2048]{1,0:T(8,128)(2,1)S(1)} %get-tuple-element.59.refs_1_.proj_ref), custom_call_target="tpu_custom_call" | custom-call | tf_op jit(solution)/shard_map/final/pallas_call | solution.py:481
  (6 shorter events, 0.0 us)
Async XLA Ops:
  1.9 16.8 %copy-start = (s32[2,32]{1,0:T(2,128)S(1)}, s32[2,32]{1,0:T(2,128)}, u32[]{:S(2)}) copy-start(s32[2,32]{1,0:T(2,128)} %mask_s.3) | copy-start | bytes 772
  1.9 16.8 %copy-start.1 = (f32[256]{0:T(256)S(1)}, f32[256]{0:T(256)}, u32[]{:S(2)}) copy-start(f32[256]{0:T(256)} %param.5) | copy-start | bytes 3076
  1.9 15.2 %collective-permute-start.2 = (bf16[128,2048]{1,0:T(8,128)(2,1)S(1)}, bf16[128,2048]{1,0:T(8,128)(2,1)S(1)}, u32[]{:S(2)}, u32[]{:S(2)}) collective-permute-start(bf16[128,2048]{1,0:T(8,128)(2,1)S(1)} %convert_element_type.3.own_ref.refs_4_), channel_id=1, source_target_pairs={{0,1},{1,0},{2,6},{3,7},{4,5},{5,4},{6,2},{7,3},{8,9},{9,8},{10,14... | collective-permute-start | bytes 1572872 | tf_op jit(solution)/shard_map/ppermute | solution.py:319
  5.0 12.2 %collective-permute-start.3 = (bf16[128,2048]{1,0:T(8,128)(2,1)S(1)}, bf16[128,2048]{1,0:T(8,128)(2,1)S(1)}, u32[]{:S(2)}, u32[]{:S(2)}) collective-permute-start(bf16[128,2048]{1,0:T(8,128)(2,1)S(1)} %convert_element_type.3.own_ref.refs_4_), channel_id=1, source_target_pairs={{0,4},{1,5},{2,3},{3,2},{4,0},{5,1},{6,7},{7,6},{8,12},{9,13},{10,... | collective-permute-start | bytes 1572872 | tf_op jit(solution)/shard_map/ppermute | solution.py:319
  6.5 25.3 %collective-permute-start = (bf16[128,2048]{1,0:T(8,128)(2,1)S(1)}, bf16[128,2048]{1,0:T(8,128)(2,1)S(1)}, u32[]{:S(2)}, u32[]{:S(2)}) collective-permute-start(bf16[128,2048]{1,0:T(8,128)(2,1)S(1)} %convert_element_type.3.own_ref.refs_4_), channel_id=1, source_target_pairs={{0,16},{1,17},{2,18},{3,19},{4,20},{5,21},{6,22},{7,23},{8,24},{9,... | collective-permute-start | bytes 1572872 | tf_op jit(solution)/shard_map/ppermute | solution.py:319
  9.1 22.9 %collective-permute-start.1 = (bf16[128,2048]{1,0:T(8,128)(2,1)S(1)}, bf16[128,2048]{1,0:T(8,128)(2,1)S(1)}, u32[]{:S(2)}, u32[]{:S(2)}) collective-permute-start(bf16[128,2048]{1,0:T(8,128)(2,1)S(1)} %convert_element_type.3.own_ref.refs_4_), channel_id=1, source_target_pairs={{0,8},{1,9},{2,10},{3,11},{4,12},{5,13},{6,14},{7,15},{8,0},{9,1},... | collective-permute-start | bytes 1572872 | tf_op jit(solution)/shard_map/ppermute | solution.py:319
  17.2 14.8 %collective-permute-start.4 = (bf16[128,2048]{1,0:T(8,128)(2,1)S(1)}, bf16[128,2048]{1,0:T(8,128)(2,1)S(1)}, u32[]{:S(2)}, u32[]{:S(2)}) collective-permute-start(bf16[128,2048]{1,0:T(8,128)(2,1)S(1)} %collective-permute-done.2.first_ref.refs_5_), channel_id=1, source_target_pairs={{0,4},{1,5},{2,3},{3,2},{4,0},{5,1},{6,7},{7,6},{8,12},{9,13},{10,... | collective-permute-start | bytes 1572872 | tf_op jit(solution)/shard_map/ppermute | solution.py:319
  24.6 3.7 %collective-permute-start.5 = (f32[8,256]{1,0:T(8,128)S(1)}, f32[8,256]{1,0:T(8,128)S(1)}, u32[]{:S(2)}, u32[]{:S(2)}) collective-permute-start(f32[8,256]{1,0:T(8,128)S(1)} %get-tuple-element.52.mine_ref), channel_id=1, source_target_pairs={{0,1},{1,0},{2,3},{3,2},{4,5},{5,4},{6,7},{7,6},{8,9},{9,8},{10,11... | collective-permute-start | bytes 24584 | tf_op jit(solution)/shard_map/ppermute | solution.py:319
  32.0 12.7 %collective-permute-start.6 = (bf16[128,2048]{1,0:T(8,128)(2,1)S(1)}, bf16[128,2048]{1,0:T(8,128)(2,1)S(1)}, u32[]{:S(2)}, u32[]{:S(2)}) collective-permute-start(bf16[128,2048]{1,0:T(8,128)(2,1)S(1)} %collective-permute-done.refs_5_), channel_id=1, source_target_pairs={{0,1},{1,0},{2,6},{3,7},{4,5},{5,4},{6,2},{7,3},{8,9},{9,8},{10,14... | collective-permute-start | bytes 1572872 | tf_op jit(solution)/shard_map/ppermute | solution.py:319
  32.5 12.2 %collective-permute-start.7 = (bf16[128,2048]{1,0:T(8,128)(2,1)S(1)}, bf16[128,2048]{1,0:T(8,128)(2,1)S(1)}, u32[]{:S(2)}, u32[]{:S(2)}) collective-permute-start(bf16[128,2048]{1,0:T(8,128)(2,1)S(1)} %collective-permute-done.refs_5_), channel_id=1, source_target_pairs={{0,4},{1,5},{2,3},{3,2},{4,0},{5,1},{6,7},{7,6},{8,12},{9,13},{10,... | collective-permute-start | bytes 1572872 | tf_op jit(solution)/shard_map/ppermute | solution.py:319
  33.0 12.0 %collective-permute-start.8 = (bf16[128,2048]{1,0:T(8,128)(2,1)S(1)}, bf16[128,2048]{1,0:T(8,128)(2,1)S(1)}, u32[]{:S(2)}, u32[]{:S(2)}) collective-permute-start(bf16[128,2048]{1,0:T(8,128)(2,1)S(1)} %collective-permute-done.refs_5_), channel_id=1, source_target_pairs={{0,8},{1,9},{2,10},{3,11},{4,12},{5,13},{6,14},{7,15},{8,0},{9,1},... | collective-permute-start | bytes 1572872 | tf_op jit(solution)/shard_map/ppermute | solution.py:319
  34.5 10.2 %collective-permute-start.9 = (f32[2,8,128]{2,1,0:T(8,128)S(1)}, f32[2,8,128]{2,1,0:T(8,128)S(1)}, u32[]{:S(2)}, u32[]{:S(2)}) collective-permute-start(f32[2,8,128]{2,1,0:T(8,128)S(1)} %meta.1), channel_id=1, source_target_pairs={{0,4},{1,5},{2,6},{3,7},{4,0},{5,1},{6,2},{7,3},{8,12},{9,13},{10,... | collective-permute-start | bytes 24584 | tf_op jit(solution)/shard_map/ppermute | solution.py:319
  45.0 19.7 %collective-permute-start.12 = (bf16[128,2048]{1,0:T(8,128)(2,1)S(1)}, bf16[128,2048]{1,0:T(8,128)(2,1)S(1)}, u32[]{:S(2)}, u32[]{:S(2)}) collective-permute-start(bf16[128,2048]{1,0:T(8,128)(2,1)S(1)} %collective-permute-done.6.refs_6_), channel_id=1, source_target_pairs={{0,4},{1,5},{2,3},{3,2},{4,0},{5,1},{6,7},{7,6},{8,12},{9,13},{10,... | collective-permute-start | bytes 1572872 | tf_op jit(solution)/shard_map/ppermute | solution.py:319
  46.5 18.1 %collective-permute-start.13 = (bf16[128,2048]{1,0:T(8,128)(2,1)S(1)}, bf16[128,2048]{1,0:T(8,128)(2,1)S(1)}, u32[]{:S(2)}, u32[]{:S(2)}) collective-permute-start(bf16[128,2048]{1,0:T(8,128)(2,1)S(1)} %collective-permute-done.8.refs_5_), channel_id=1, source_target_pairs={{0,1},{1,0},{2,6},{3,7},{4,5},{5,4},{6,2},{7,3},{8,9},{9,8},{10,14... | collective-permute-start | bytes 1572872 | tf_op jit(solution)/shard_map/ppermute | solution.py:319
  48.0 19.3 %collective-permute-start.14 = (bf16[128,2048]{1,0:T(8,128)(2,1)S(1)}, bf16[128,2048]{1,0:T(8,128)(2,1)S(1)}, u32[]{:S(2)}, u32[]{:S(2)}) collective-permute-start(bf16[128,2048]{1,0:T(8,128)(2,1)S(1)} %collective-permute-done.8.refs_5_), channel_id=1, source_target_pairs={{0,4},{1,5},{2,3},{3,2},{4,0},{5,1},{6,7},{7,6},{8,12},{9,13},{10,... | collective-permute-start | bytes 1572872 | tf_op jit(solution)/shard_map/ppermute | solution.py:319
  48.5 3.7 %collective-permute-start.10 = (f32[4,8,128]{2,1,0:T(8,128)S(1)}, f32[4,8,128]{2,1,0:T(8,128)S(1)}, u32[]{:S(2)}, u32[]{:S(2)}) collective-permute-start(f32[4,8,128]{2,1,0:T(8,128)S(1)} %pad_maximum_fusion), channel_id=1, source_target_pairs={{0,8},{1,9},{2,10},{3,11},{4,12},{5,13},{6,14},{7,15},{8,0},{9,1},... | collective-permute-start | bytes 49160 | tf_op jit(solution)/shard_map/ppermute | solution.py:319
  52.3 5.3 %collective-permute-start.11 = (f32[8,8,128]{2,1,0:T(8,128)S(1)}, f32[8,8,128]{2,1,0:T(8,128)S(1)}, u32[]{:S(2)}, u32[]{:S(2)}) collective-permute-start(f32[8,8,128]{2,1,0:T(8,128)S(1)} %constant_dynamic-update-slice_fusion.refs_2_), channel_id=1, source_target_pairs={{0,16},{1,17},{2,18},{3,19},{4,20},{5,21},{6,22},{7,23},{8,24},{9,... | collective-permute-start | bytes 98312 | tf_op jit(solution)/shard_map/ppermute | solution.py:319
  57.6 19.5 %collective-permute-start.18 = (bf16[128,2048]{1,0:T(8,128)(2,1)S(1)}, bf16[128,2048]{1,0:T(8,128)(2,1)S(1)}, u32[]{:S(2)}, u32[]{:S(2)}) collective-permute-start(bf16[128,2048]{1,0:T(8,128)(2,1)S(1)} %collective-permute-done.4.refs_7_), channel_id=1, source_target_pairs={{0,8},{1,9},{2,10},{3,11},{4,12},{5,13},{6,14},{7,15},{8,0},{9,1},... | collective-permute-start | bytes 1572872 | tf_op jit(solution)/shard_map/ppermute | solution.py:319
  64.7 12.5 %collective-permute-start.15 = (bf16[128,2048]{1,0:T(8,128)(2,1)S(1)}, bf16[128,2048]{1,0:T(8,128)(2,1)S(1)}, u32[]{:S(2)}, u32[]{:S(2)}) collective-permute-start(bf16[128,2048]{1,0:T(8,128)(2,1)S(1)} %collective-permute-done.1.refs_4_), channel_id=1, source_target_pairs={{0,1},{1,0},{2,6},{3,7},{4,5},{5,4},{6,2},{7,3},{8,9},{9,8},{10,14... | collective-permute-start | bytes 1572872 | tf_op jit(solution)/shard_map/ppermute | solution.py:319
  65.3 11.9 %collective-permute-start.19 = (bf16[128,2048]{1,0:T(8,128)(2,1)S(1)}, bf16[128,2048]{1,0:T(8,128)(2,1)S(1)}, u32[]{:S(2)}, u32[]{:S(2)}) collective-permute-start(bf16[128,2048]{1,0:T(8,128)(2,1)S(1)} %collective-permute-done.13.refs_6_), channel_id=1, source_target_pairs={{0,4},{1,5},{2,3},{3,2},{4,0},{5,1},{6,7},{7,6},{8,12},{9,13},{10,... | collective-permute-start | bytes 1572872 | tf_op jit(solution)/shard_map/ppermute | solution.py:319
  67.2 10.0 %collective-permute-start.16 = (bf16[96,2048]{1,0:T(8,128)(2,1)S(1)}, bf16[96,2048]{1,0:T(8,128)(2,1)S(1)}, u32[]{:S(2)}, u32[]{:S(2)}) collective-permute-start(bf16[96,2048]{1,0:T(8,128)(2,1)S(1)} %slice.6), channel_id=1, source_target_pairs={{0,8},{1,9},{2,10},{3,11},{4,12},{5,13},{6,14},{7,15},{8,0},{9,1},... | collective-permute-start | bytes 1179656 | tf_op jit(solution)/shard_map/ppermute | solution.py:319
  67.3 9.8 %collective-permute-start.17 = (bf16[32,2048]{1,0:T(8,128)(2,1)S(1)}, bf16[32,2048]{1,0:T(8,128)(2,1)S(1)}, u32[]{:S(2)}, u32[]{:S(2)}) collective-permute-start(bf16[32,2048]{1,0:T(8,128)(2,1)S(1)} %slice.7), channel_id=1, source_target_pairs={{0,4},{1,5},{2,3},{3,2},{4,0},{5,1},{6,7},{7,6},{8,12},{9,13},{10,... | collective-permute-start | bytes 393224 | tf_op jit(solution)/shard_map/ppermute | solution.py:319
  79.4 2.8 %collective-permute-start.20 = (bf16[256,2176]{1,0:T(8,128)(2,1)S(1)}, bf16[256,2176]{1,0:T(8,128)(2,1)S(1)}, u32[]{:S(2)}, u32[]{:S(2)}) collective-permute-start(bf16[256,2176]{1,0:T(8,128)(2,1)S(1)} %get-tuple-element.87), channel_id=1, source_target_pairs={{0,2},{1,3},{2,0},{3,1},{4,6},{5,7},{6,4},{7,5},{8,10},{9,11},{10,... | collective-permute-start | bytes 3342344 | tf_op jit(solution)/shard_map/ppermute | solution.py:467

commit v6 on v5

--- a/solution.py
+++ b/solution.py
@@ -477,7 +477,7 @@
         name="keep",
     )(state[0], kept_weights, *last_pieces)
     out_rows = width // 2
-    cut = 4
+    cut = 2
     refined = pl.pallas_call(
         final_kernel,
         grid=(cut,),

time: 84.3 us -> 83.9 us (level)
  no operation moved by 1% of the time
where the time goes in v6:
time: 83.9 us; the launch traced here: 83.7 us
  starting transfers between devices  29.3 us (35%)
  Pallas kernels  28.1 us (33%)
  waiting for transfers between devices  24.2 us (29%)
  other arithmetic  1.29 us (2%)
    ppermute x20, starting transfers between devices, swap(): lax.ppermute(a, both, [(i, i ^ masks[i // n_ori % cores]) for i in range(...  29.2 us
    ppermute x20, waiting for transfers between devices, swap(): lax.ppermute(a, both, [(i, i ^ masks[i // n_ori % cores]) for i in range(...  22.2 us
    pallas_call x4, Pallas kernels, add(): pl.pallas_call(functools.partial(sums_kernel, len(metas), tiles * cores /...  10.3 us
    pallas_call x1, Pallas kernels, gathered_body(): pl.pallas_call(functools.partial(load_kernel, chips), in_specs=[pl.BlockS...  6.53 us
    pallas_call x1, Pallas kernels, gathered_body(): pl.pallas_call(functools.partial(scores_kernel, chips), in_specs=[smem] +...  5.83 us
    pallas_call x1, Pallas kernels, gathered_body(): pl.pallas_call(posterior_kernel, grid=(cut,), in_specs=[vmem, pl.BlockSpe...  2.55 us
    ppermute x1, waiting for transfers between devices, gathered_body(): got = lax.ppermute(sent_away, both, [(i, i ^ n_ori) for i in range(n)])  2.02 us
  transfers between devices with their start and end apart: 21, of which 10 were waited for; matrix products, arithmetic and copies ran while one was open for 0% of the time, Pallas kernels for 29%

profile of v6, /device:TPU:0, one launch (start us, length us, event | category | flops | bytes accessed | tf_op | source)
XLA Modules:
  0.0 83.7 jit_solution(18261848869057273689)
XLA Ops:
  0.6 1.3 %convert_element_type.3.own_ref.refs_4_ = bf16[128,2048]{1,0:T(8,128)(2,1)S(1)} convert(f32[128,2048]{1,0:T(8,128)} %param.4) | non-fusion elementwise | flops 262144 | bytes 1572864 | tf_op jit(solution)/shard_map/convert_element_type | solution.py:338
  1.9 0.0 copy-start
  1.9 0.0 copy-start.1
  1.9 3.0 %collective-permute-start.2 = (bf16[128,2048]{1,0:T(8,128)(2,1)S(1)}, bf16[128,2048]{1,0:T(8,128)(2,1)S(1)}, u32[]{:S(2)}, u32[]{:S(2)}) collective-permute-start(bf16[128,2048]{1,0:T(8,128)(2,1)S(1)} %convert_element_type.3.own_ref.refs_4_), channel_id=1, source_target_pairs={{0,1},{1,0},{2,6},{3,7},{4,5},{5,4},{6,2},{7,3},{8,9},{9,8},{10,14... | collective-permute-start | bytes 1572872 | tf_op jit(solution)/shard_map/ppermute | solution.py:319
  5.0 1.5 %collective-permute-start.3 = (bf16[128,2048]{1,0:T(8,128)(2,1)S(1)}, bf16[128,2048]{1,0:T(8,128)(2,1)S(1)}, u32[]{:S(2)}, u32[]{:S(2)}) collective-permute-start(bf16[128,2048]{1,0:T(8,128)(2,1)S(1)} %convert_element_type.3.own_ref.refs_4_), channel_id=1, source_target_pairs={{0,4},{1,5},{2,3},{3,2},{4,0},{5,1},{6,7},{7,6},{8,12},{9,13},{10,... | collective-permute-start | bytes 1572872 | tf_op jit(solution)/shard_map/ppermute | solution.py:319
  6.5 2.6 %collective-permute-start = (bf16[128,2048]{1,0:T(8,128)(2,1)S(1)}, bf16[128,2048]{1,0:T(8,128)(2,1)S(1)}, u32[]{:S(2)}, u32[]{:S(2)}) collective-permute-start(bf16[128,2048]{1,0:T(8,128)(2,1)S(1)} %convert_element_type.3.own_ref.refs_4_), channel_id=1, source_target_pairs={{0,16},{1,17},{2,18},{3,19},{4,20},{5,21},{6,22},{7,23},{8,24},{9,... | collective-permute-start | bytes 1572872 | tf_op jit(solution)/shard_map/ppermute | solution.py:319
  9.1 1.6 %collective-permute-start.1 = (bf16[128,2048]{1,0:T(8,128)(2,1)S(1)}, bf16[128,2048]{1,0:T(8,128)(2,1)S(1)}, u32[]{:S(2)}, u32[]{:S(2)}) collective-permute-start(bf16[128,2048]{1,0:T(8,128)(2,1)S(1)} %convert_element_type.3.own_ref.refs_4_), channel_id=1, source_target_pairs={{0,8},{1,9},{2,10},{3,11},{4,12},{5,13},{6,14},{7,15},{8,0},{9,1},... | collective-permute-start | bytes 1572872 | tf_op jit(solution)/shard_map/ppermute | solution.py:319
  10.6 6.5 %load.1 = (bf16[4096,2048]{1,0:T(8,128)(2,1)S(1)}, bf16[512,2048]{1,0:T(8,128)(2,1)S(1)}, f32[8,4096]{1,0:T(8,128)S(1)}, f32[512,128]{1,0:T(8,128)S(1)}) custom-call(bf16[4096,2048]{1,0:T(8,128)(2,1)} %away_ref.1), custom_call_target="tpu_custom_call" | custom-call | tf_op jit(solution)/shard_map/load/pallas_call | solution.py:345
  17.2 0.0 collective-permute-done.2.first_ref.refs_5_
  17.2 0.0 collective-permute-done.3.second_ref.refs_6_
  17.2 1.5 %collective-permute-start.4 = (bf16[128,2048]{1,0:T(8,128)(2,1)S(1)}, bf16[128,2048]{1,0:T(8,128)(2,1)S(1)}, u32[]{:S(2)}, u32[]{:S(2)}) collective-permute-start(bf16[128,2048]{1,0:T(8,128)(2,1)S(1)} %collective-permute-done.2.first_ref.refs_5_), channel_id=1, source_target_pairs={{0,4},{1,5},{2,3},{3,2},{4,0},{5,1},{6,7},{7,6},{8,12},{9,13},{10,... | collective-permute-start | bytes 1572872 | tf_op jit(solution)/shard_map/ppermute | solution.py:319
  18.7 0.0 copy-done
  18.7 0.0 copy-done.1
  18.7 5.8 %scores.1 = (f32[256,4096]{1,0:T(8,128)S(1)}, f32[8,256]{1,0:T(8,128)S(1)}) custom-call(s32[2,32]{1,0:T(2,128)S(1)} %copy-done, f32[1,256]{1,0:T(1,128)S(1)} %bitcast.1, f32[8,4096]{1,0:T(8,128)S(1)} %get-tuple-element.49.half_ref, bf16[128,2048]{1,0:T(8,128)(2,1)S(1)} %convert_element_type.3.own_ref.refs_4_, ...), custom_call_target="tpu_custom_call" | custom-call | tf_op jit(solution)/shard_map/scores/pallas_call | solution.py:366
  24.6 1.7 %collective-permute-start.5 = (f32[8,256]{1,0:T(8,128)S(1)}, f32[8,256]{1,0:T(8,128)S(1)}, u32[]{:S(2)}, u32[]{:S(2)}) collective-permute-start(f32[8,256]{1,0:T(8,128)S(1)} %get-tuple-element.52.mine_ref), channel_id=1, source_target_pairs={{0,1},{1,0},{2,3},{3,2},{4,5},{5,4},{6,7},{7,6},{8,9},{9,8},{10,11... | collective-permute-start | bytes 24584 | tf_op jit(solution)/shard_map/ppermute | solution.py:319
  26.2 2.0 %collective-permute-done.5.theirs_ref = f32[8,256]{1,0:T(8,128)S(1)} collective-permute-done((f32[8,256]{1,0:T(8,128)S(1)}, f32[8,256]{1,0:T(8,128)S(1)}, u32[]{:S(2)}, u32[]{:S(2)}) %collective-permute-start.5) | collective-permute-done | bytes 8224 | tf_op jit(solution)/shard_map/ppermute | solution.py:319
  28.3 0.6 meta.1
  28.9 2.9 %collective-permute-done.refs_5_ = bf16[128,2048]{1,0:T(8,128)(2,1)S(1)} collective-permute-done((bf16[128,2048]{1,0:T(8,128)(2,1)S(1)}, bf16[128,2048]{1,0:T(8,128)(2,1)S(1)}, u32[]{:S(2)}, u32[]{:S(2)}) %collective-permute-start) | collective-permute-done | bytes 524320 | tf_op jit(solution)/shard_map/ppermute | solution.py:319
  31.8 0.2 collective-permute-done.1.refs_4_
  32.0 0.0 collective-permute-done.4.refs_7_
  32.0 0.5 collective-permute-start.6
  32.5 0.5 collective-permute-start.7
  33.0 1.5 %collective-permute-start.8 = (bf16[128,2048]{1,0:T(8,128)(2,1)S(1)}, bf16[128,2048]{1,0:T(8,128)(2,1)S(1)}, u32[]{:S(2)}, u32[]{:S(2)}) collective-permute-start(bf16[128,2048]{1,0:T(8,128)(2,1)S(1)} %collective-permute-done.refs_5_), channel_id=1, source_target_pairs={{0,8},{1,9},{2,10},{3,11},{4,12},{5,13},{6,14},{7,15},{8,0},{9,1},... | collective-permute-start | bytes 1572872 | tf_op jit(solution)/shard_map/ppermute | solution.py:319
  34.5 1.5 %collective-permute-start.9 = (f32[2,8,128]{2,1,0:T(8,128)S(1)}, f32[2,8,128]{2,1,0:T(8,128)S(1)}, u32[]{:S(2)}, u32[]{:S(2)}) collective-permute-start(f32[2,8,128]{2,1,0:T(8,128)S(1)} %meta.1), channel_id=1, source_target_pairs={{0,4},{1,5},{2,6},{3,7},{4,0},{5,1},{6,2},{7,3},{8,12},{9,13},{10,... | collective-permute-start | bytes 24584 | tf_op jit(solution)/shard_map/ppermute | solution.py:319
  36.0 2.6 %posterior.1 = bf16[256,4096]{1,0:T(8,128)(2,1)} custom-call(f32[256,4096]{1,0:T(8,128)S(1)} %get-tuple-element.56.scores_ref, f32[8,256]{1,0:T(8,128)S(1)} %get-tuple-element.52.mine_ref, f32[8,256]{1,0:T(8,128)S(1)} %collective-permute-done.5.theirs_ref), custom_call_target="tpu_custom_call" | custom-call | tf_op jit(solution)/shard_map/posterior/pallas_call | solution.py:396
  38.6 6.1 %collective-permute-done.9 = f32[2,8,128]{2,1,0:T(8,128)S(1)} collective-permute-done((f32[2,8,128]{2,1,0:T(8,128)S(1)}, f32[2,8,128]{2,1,0:T(8,128)S(1)}, u32[]{:S(2)}, u32[]{:S(2)}) %collective-permute-start.9) | collective-permute-done | bytes 8224 | tf_op jit(solution)/shard_map/ppermute | solution.py:319
  44.7 0.1 collective-permute-done.6.refs_6_
  44.8 0.0 collective-permute-done.7.refs_7_
  44.8 0.2 collective-permute-done.8.refs_5_
  45.0 1.6 %collective-permute-start.12 = (bf16[128,2048]{1,0:T(8,128)(2,1)S(1)}, bf16[128,2048]{1,0:T(8,128)(2,1)S(1)}, u32[]{:S(2)}, u32[]{:S(2)}) collective-permute-start(bf16[128,2048]{1,0:T(8,128)(2,1)S(1)} %collective-permute-done.6.refs_6_), channel_id=1, source_target_pairs={{0,4},{1,5},{2,3},{3,2},{4,0},{5,1},{6,7},{7,6},{8,12},{9,13},{10,... | collective-permute-start | bytes 1572872 | tf_op jit(solution)/shard_map/ppermute | solution.py:319
  46.5 1.5 %collective-permute-start.13 = (bf16[128,2048]{1,0:T(8,128)(2,1)S(1)}, bf16[128,2048]{1,0:T(8,128)(2,1)S(1)}, u32[]{:S(2)}, u32[]{:S(2)}) collective-permute-start(bf16[128,2048]{1,0:T(8,128)(2,1)S(1)} %collective-permute-done.8.refs_5_), channel_id=1, source_target_pairs={{0,1},{1,0},{2,6},{3,7},{4,5},{5,4},{6,2},{7,3},{8,9},{9,8},{10,14... | collective-permute-start | bytes 1572872 | tf_op jit(solution)/shard_map/ppermute | solution.py:319
  48.0 0.5 collective-permute-start.14
  48.5 1.7 %collective-permute-start.10 = (f32[4,8,128]{2,1,0:T(8,128)S(1)}, f32[4,8,128]{2,1,0:T(8,128)S(1)}, u32[]{:S(2)}, u32[]{:S(2)}) collective-permute-start(f32[4,8,128]{2,1,0:T(8,128)S(1)} %pad_maximum_fusion), channel_id=1, source_target_pairs={{0,8},{1,9},{2,10},{3,11},{4,12},{5,13},{6,14},{7,15},{8,0},{9,1},... | collective-permute-start | bytes 49160 | tf_op jit(solution)/shard_map/ppermute | solution.py:319
  50.2 2.0 %collective-permute-done.10 = f32[4,8,128]{2,1,0:T(8,128)S(1)} collective-permute-done((f32[4,8,128]{2,1,0:T(8,128)S(1)}, f32[4,8,128]{2,1,0:T(8,128)S(1)}, u32[]{:S(2)}, u32[]{:S(2)}) %collective-permute-start.10) | collective-permute-done | bytes 16416 | tf_op jit(solution)/shard_map/ppermute | solution.py:319
  52.3 3.3 %collective-permute-start.11 = (f32[8,8,128]{2,1,0:T(8,128)S(1)}, f32[8,8,128]{2,1,0:T(8,128)S(1)}, u32[]{:S(2)}, u32[]{:S(2)}) collective-permute-start(f32[8,8,128]{2,1,0:T(8,128)S(1)} %constant_dynamic-update-slice_fusion.refs_2_), channel_id=1, source_target_pairs={{0,16},{1,17},{2,18},{3,19},{4,20},{5,21},{6,22},{7,23},{8,24},{9,... | collective-permute-start | bytes 98312 | tf_op jit(solution)/shard_map/ppermute | solution.py:319
  55.6 2.0 %collective-permute-done.11.refs_3_ = f32[8,8,128]{2,1,0:T(8,128)S(1)} collective-permute-done((f32[8,8,128]{2,1,0:T(8,128)S(1)}, f32[8,8,128]{2,1,0:T(8,128)S(1)}, u32[]{:S(2)}, u32[]{:S(2)}) %collective-permute-start.11) | collective-permute-done | bytes 32800 | tf_op jit(solution)/shard_map/ppermute | solution.py:319
  57.6 1.6 %collective-permute-start.18 = (bf16[128,2048]{1,0:T(8,128)(2,1)S(1)}, bf16[128,2048]{1,0:T(8,128)(2,1)S(1)}, u32[]{:S(2)}, u32[]{:S(2)}) collective-permute-start(bf16[128,2048]{1,0:T(8,128)(2,1)S(1)} %collective-permute-done.4.refs_7_), channel_id=1, source_target_pairs={{0,8},{1,9},{2,10},{3,11},{4,12},{5,13},{6,14},{7,15},{8,0},{9,1},... | collective-permute-start | bytes 1572872 | tf_op jit(solution)/shard_map/ppermute | solution.py:319
  59.3 2.7 %sums.4 = (f32[512,2048]{1,0:T(8,128)S(1)}, f32[512,128]{1,0:T(8,128)S(1)}) custom-call(f32[512,128]{1,0:T(8,128)S(1)} %get-tuple-element.58.refs_0_, bf16[512,2048]{1,0:T(8,128)(2,1)S(1)} %get-tuple-element.59.refs_1_.proj_ref, f32[8,8,128]{2,1,0:T(8,128)S(1)} %constant_dynamic-update-slice_fusion.refs_2_, ...), custom_call_target="tpu_custom_call" | custom-call | tf_op jit(solution)/shard_map/sums/pallas_call | solution.py:441
  61.9 2.7 %sums.5 = (f32[512,2048]{1,0:T(8,128)S(1)}, f32[512,128]{1,0:T(8,128)S(1)}) custom-call(f32[512,128]{1,0:T(8,128)S(1)} %get-tuple-element.58.refs_0_, bf16[512,2048]{1,0:T(8,128)(2,1)S(1)} %get-tuple-element.59.refs_1_.proj_ref, f32[8,8,128]{2,1,0:T(8,128)S(1)} %constant_dynamic-update-slice_fusion.refs_2_, ...), custom_call_target="tpu_custom_call", output_to_operand_aliasing={{0}: (8, {}), {1}: (9, {})} | custom-call | tf_op jit(solution)/shard_map/sums/pallas_call | solution.py:441
  64.7 0.0 collective-permute-done.12.refs_4_
  64.7 0.0 collective-permute-done.13.refs_6_
  64.7 0.6 collective-permute-start.15
  65.3 1.9 %collective-permute-start.19 = (bf16[128,2048]{1,0:T(8,128)(2,1)S(1)}, bf16[128,2048]{1,0:T(8,128)(2,1)S(1)}, u32[]{:S(2)}, u32[]{:S(2)}) collective-permute-start(bf16[128,2048]{1,0:T(8,128)(2,1)S(1)} %collective-permute-done.13.refs_6_), channel_id=1, source_target_pairs={{0,4},{1,5},{2,3},{3,2},{4,0},{5,1},{6,7},{7,6},{8,12},{9,13},{10,... | collective-permute-start | bytes 1572872 | tf_op jit(solution)/shard_map/ppermute | solution.py:319
  67.2 0.1 collective-permute-start.16
  67.3 0.0 collective-permute-done.14.refs_7_
  67.3 0.5 collective-permute-start.17
  67.8 2.7 %sums.6 = (f32[512,2048]{1,0:T(8,128)S(1)}, f32[512,128]{1,0:T(8,128)S(1)}) custom-call(f32[512,128]{1,0:T(8,128)S(1)} %get-tuple-element.58.refs_0_, bf16[512,2048]{1,0:T(8,128)(2,1)S(1)} %get-tuple-element.59.refs_1_.proj_ref, f32[8,8,128]{2,1,0:T(8,128)S(1)} %constant_dynamic-update-slice_fusion.refs_2_, ...), custom_call_target="tpu_custom_call", output_to_operand_aliasing={{0}: (8, {}), {1}: (9, {})} | custom-call | tf_op jit(solution)/shard_map/sums/pallas_call | solution.py:441
  70.6 6.6 %collective-permute-done.16.refs_5_.refs_1_ = bf16[96,2048]{1,0:T(8,128)(2,1)S(1)} collective-permute-done((bf16[96,2048]{1,0:T(8,128)(2,1)S(1)}, bf16[96,2048]{1,0:T(8,128)(2,1)S(1)}, u32[]{:S(2)}, u32[]{:S(2)}) %collective-permute-start.16) | collective-permute-done | bytes 393248 | tf_op jit(solution)/shard_map/ppermute | solution.py:319
  77.2 0.0 collective-permute-done.18.refs_7_.refs_3_
  77.2 0.0 collective-permute-done.17.refs_6_.refs_2_
  77.2 0.0 collective-permute-done.15.refs_4_.refs_0_
  77.2 0.0 collective-permute-done.19.refs_8_.refs_4_
  77.2 2.2 %sums.7 = (bf16[256,512]{1,0:T(8,128)(2,1)S(1)}, f32[256,128]{1,0:T(8,128)S(1)}, bf16[256,2176]{1,0:T(8,128)(2,1)S(1)}) custom-call(f32[512,128]{1,0:T(8,128)S(1)} %get-tuple-element.58.refs_0_, bf16[512,2048]{1,0:T(8,128)(2,1)S(1)} %get-tuple-element.59.refs_1_.proj_ref, f32[8,8,128]{2,1,0:T(8,128)S(1)} %constant_dynamic-update-slice_fusion.refs_2_, ...), custom_call_target="tpu_custom_call" | custom-call | tf_op jit(solution)/shard_map/sums/pallas_call | solution.py:441
  79.4 0.1 collective-permute-start.20
  79.5 0.7 keep.1.kept_ref
  80.2 2.0 %collective-permute-done.20.got_ref = bf16[256,2176]{1,0:T(8,128)(2,1)S(1)} collective-permute-done((bf16[256,2176]{1,0:T(8,128)(2,1)S(1)}, bf16[256,2176]{1,0:T(8,128)(2,1)S(1)}, u32[]{:S(2)}, u32[]{:S(2)}) %collective-permute-start.20) | collective-permute-done | bytes 1114144 | tf_op jit(solution)/shard_map/ppermute | solution.py:467
  82.2 1.5 %final.1 = f32[256,2048]{1,0:T(8,128)} custom-call(f32[256,2048]{1,0:T(8,128)S(1)} %keep.1.kept_ref, f32[256,128]{1,0:T(8,128)S(1)} %get-tuple-element.86.kept_cnt_ref, bf16[256,2176]{1,0:T(8,128)(2,1)S(1)} %collective-permute-done.20.got_ref, bf16[512,2048]{1,0:T(8,128)(2,1)S(1)} %get-tuple-element.59.refs_1_.proj_ref), custom_call_target="tpu_custom_call" | custom-call | tf_op jit(solution)/shard_map/final/pallas_call | solution.py:481
  (6 shorter events, 0.0 us)
Async XLA Ops:
  1.9 16.8 %copy-start = (s32[2,32]{1,0:T(2,128)S(1)}, s32[2,32]{1,0:T(2,128)}, u32[]{:S(2)}) copy-start(s32[2,32]{1,0:T(2,128)} %mask_s.3) | copy-start | bytes 772
  1.9 16.8 %copy-start.1 = (f32[256]{0:T(256)S(1)}, f32[256]{0:T(256)}, u32[]{:S(2)}) copy-start(f32[256]{0:T(256)} %param.5) | copy-start | bytes 3076
  1.9 15.2 %collective-permute-start.2 = (bf16[128,2048]{1,0:T(8,128)(2,1)S(1)}, bf16[128,2048]{1,0:T(8,128)(2,1)S(1)}, u32[]{:S(2)}, u32[]{:S(2)}) collective-permute-start(bf16[128,2048]{1,0:T(8,128)(2,1)S(1)} %convert_element_type.3.own_ref.refs_4_), channel_id=1, source_target_pairs={{0,1},{1,0},{2,6},{3,7},{4,5},{5,4},{6,2},{7,3},{8,9},{9,8},{10,14... | collective-permute-start | bytes 1572872 | tf_op jit(solution)/shard_map/ppermute | solution.py:319
  5.0 12.2 %collective-permute-start.3 = (bf16[128,2048]{1,0:T(8,128)(2,1)S(1)}, bf16[128,2048]{1,0:T(8,128)(2,1)S(1)}, u32[]{:S(2)}, u32[]{:S(2)}) collective-permute-start(bf16[128,2048]{1,0:T(8,128)(2,1)S(1)} %convert_element_type.3.own_ref.refs_4_), channel_id=1, source_target_pairs={{0,4},{1,5},{2,3},{3,2},{4,0},{5,1},{6,7},{7,6},{8,12},{9,13},{10,... | collective-permute-start | bytes 1572872 | tf_op jit(solution)/shard_map/ppermute | solution.py:319
  6.5 25.3 %collective-permute-start = (bf16[128,2048]{1,0:T(8,128)(2,1)S(1)}, bf16[128,2048]{1,0:T(8,128)(2,1)S(1)}, u32[]{:S(2)}, u32[]{:S(2)}) collective-permute-start(bf16[128,2048]{1,0:T(8,128)(2,1)S(1)} %convert_element_type.3.own_ref.refs_4_), channel_id=1, source_target_pairs={{0,16},{1,17},{2,18},{3,19},{4,20},{5,21},{6,22},{7,23},{8,24},{9,... | collective-permute-start | bytes 1572872 | tf_op jit(solution)/shard_map/ppermute | solution.py:319
  9.1 22.9 %collective-permute-start.1 = (bf16[128,2048]{1,0:T(8,128)(2,1)S(1)}, bf16[128,2048]{1,0:T(8,128)(2,1)S(1)}, u32[]{:S(2)}, u32[]{:S(2)}) collective-permute-start(bf16[128,2048]{1,0:T(8,128)(2,1)S(1)} %convert_element_type.3.own_ref.refs_4_), channel_id=1, source_target_pairs={{0,8},{1,9},{2,10},{3,11},{4,12},{5,13},{6,14},{7,15},{8,0},{9,1},... | collective-permute-start | bytes 1572872 | tf_op jit(solution)/shard_map/ppermute | solution.py:319
  17.2 14.8 %collective-permute-start.4 = (bf16[128,2048]{1,0:T(8,128)(2,1)S(1)}, bf16[128,2048]{1,0:T(8,128)(2,1)S(1)}, u32[]{:S(2)}, u32[]{:S(2)}) collective-permute-start(bf16[128,2048]{1,0:T(8,128)(2,1)S(1)} %collective-permute-done.2.first_ref.refs_5_), channel_id=1, source_target_pairs={{0,4},{1,5},{2,3},{3,2},{4,0},{5,1},{6,7},{7,6},{8,12},{9,13},{10,... | collective-permute-start | bytes 1572872 | tf_op jit(solution)/shard_map/ppermute | solution.py:319
  24.6 3.7 %collective-permute-start.5 = (f32[8,256]{1,0:T(8,128)S(1)}, f32[8,256]{1,0:T(8,128)S(1)}, u32[]{:S(2)}, u32[]{:S(2)}) collective-permute-start(f32[8,256]{1,0:T(8,128)S(1)} %get-tuple-element.52.mine_ref), channel_id=1, source_target_pairs={{0,1},{1,0},{2,3},{3,2},{4,5},{5,4},{6,7},{7,6},{8,9},{9,8},{10,11... | collective-permute-start | bytes 24584 | tf_op jit(solution)/shard_map/ppermute | solution.py:319
  32.0 12.7 %collective-permute-start.6 = (bf16[128,2048]{1,0:T(8,128)(2,1)S(1)}, bf16[128,2048]{1,0:T(8,128)(2,1)S(1)}, u32[]{:S(2)}, u32[]{:S(2)}) collective-permute-start(bf16[128,2048]{1,0:T(8,128)(2,1)S(1)} %collective-permute-done.refs_5_), channel_id=1, source_target_pairs={{0,1},{1,0},{2,6},{3,7},{4,5},{5,4},{6,2},{7,3},{8,9},{9,8},{10,14... | collective-permute-start | bytes 1572872 | tf_op jit(solution)/shard_map/ppermute | solution.py:319
  32.5 12.2 %collective-permute-start.7 = (bf16[128,2048]{1,0:T(8,128)(2,1)S(1)}, bf16[128,2048]{1,0:T(8,128)(2,1)S(1)}, u32[]{:S(2)}, u32[]{:S(2)}) collective-permute-start(bf16[128,2048]{1,0:T(8,128)(2,1)S(1)} %collective-permute-done.refs_5_), channel_id=1, source_target_pairs={{0,4},{1,5},{2,3},{3,2},{4,0},{5,1},{6,7},{7,6},{8,12},{9,13},{10,... | collective-permute-start | bytes 1572872 | tf_op jit(solution)/shard_map/ppermute | solution.py:319
  33.0 12.0 %collective-permute-start.8 = (bf16[128,2048]{1,0:T(8,128)(2,1)S(1)}, bf16[128,2048]{1,0:T(8,128)(2,1)S(1)}, u32[]{:S(2)}, u32[]{:S(2)}) collective-permute-start(bf16[128,2048]{1,0:T(8,128)(2,1)S(1)} %collective-permute-done.refs_5_), channel_id=1, source_target_pairs={{0,8},{1,9},{2,10},{3,11},{4,12},{5,13},{6,14},{7,15},{8,0},{9,1},... | collective-permute-start | bytes 1572872 | tf_op jit(solution)/shard_map/ppermute | solution.py:319
  34.5 10.2 %collective-permute-start.9 = (f32[2,8,128]{2,1,0:T(8,128)S(1)}, f32[2,8,128]{2,1,0:T(8,128)S(1)}, u32[]{:S(2)}, u32[]{:S(2)}) collective-permute-start(f32[2,8,128]{2,1,0:T(8,128)S(1)} %meta.1), channel_id=1, source_target_pairs={{0,4},{1,5},{2,6},{3,7},{4,0},{5,1},{6,2},{7,3},{8,12},{9,13},{10,... | collective-permute-start | bytes 24584 | tf_op jit(solution)/shard_map/ppermute | solution.py:319
  45.0 19.7 %collective-permute-start.12 = (bf16[128,2048]{1,0:T(8,128)(2,1)S(1)}, bf16[128,2048]{1,0:T(8,128)(2,1)S(1)}, u32[]{:S(2)}, u32[]{:S(2)}) collective-permute-start(bf16[128,2048]{1,0:T(8,128)(2,1)S(1)} %collective-permute-done.6.refs_6_), channel_id=1, source_target_pairs={{0,4},{1,5},{2,3},{3,2},{4,0},{5,1},{6,7},{7,6},{8,12},{9,13},{10,... | collective-permute-start | bytes 1572872 | tf_op jit(solution)/shard_map/ppermute | solution.py:319
  46.5 18.1 %collective-permute-start.13 = (bf16[128,2048]{1,0:T(8,128)(2,1)S(1)}, bf16[128,2048]{1,0:T(8,128)(2,1)S(1)}, u32[]{:S(2)}, u32[]{:S(2)}) collective-permute-start(bf16[128,2048]{1,0:T(8,128)(2,1)S(1)} %collective-permute-done.8.refs_5_), channel_id=1, source_target_pairs={{0,1},{1,0},{2,6},{3,7},{4,5},{5,4},{6,2},{7,3},{8,9},{9,8},{10,14... | collective-permute-start | bytes 1572872 | tf_op jit(solution)/shard_map/ppermute | solution.py:319
  48.0 19.3 %collective-permute-start.14 = (bf16[128,2048]{1,0:T(8,128)(2,1)S(1)}, bf16[128,2048]{1,0:T(8,128)(2,1)S(1)}, u32[]{:S(2)}, u32[]{:S(2)}) collective-permute-start(bf16[128,2048]{1,0:T(8,128)(2,1)S(1)} %collective-permute-done.8.refs_5_), channel_id=1, source_target_pairs={{0,4},{1,5},{2,3},{3,2},{4,0},{5,1},{6,7},{7,6},{8,12},{9,13},{10,... | collective-permute-start | bytes 1572872 | tf_op jit(solution)/shard_map/ppermute | solution.py:319
  48.5 3.7 %collective-permute-start.10 = (f32[4,8,128]{2,1,0:T(8,128)S(1)}, f32[4,8,128]{2,1,0:T(8,128)S(1)}, u32[]{:S(2)}, u32[]{:S(2)}) collective-permute-start(f32[4,8,128]{2,1,0:T(8,128)S(1)} %pad_maximum_fusion), channel_id=1, source_target_pairs={{0,8},{1,9},{2,10},{3,11},{4,12},{5,13},{6,14},{7,15},{8,0},{9,1},... | collective-permute-start | bytes 49160 | tf_op jit(solution)/shard_map/ppermute | solution.py:319
  52.3 5.3 %collective-permute-start.11 = (f32[8,8,128]{2,1,0:T(8,128)S(1)}, f32[8,8,128]{2,1,0:T(8,128)S(1)}, u32[]{:S(2)}, u32[]{:S(2)}) collective-permute-start(f32[8,8,128]{2,1,0:T(8,128)S(1)} %constant_dynamic-update-slice_fusion.refs_2_), channel_id=1, source_target_pairs={{0,16},{1,17},{2,18},{3,19},{4,20},{5,21},{6,22},{7,23},{8,24},{9,... | collective-permute-start | bytes 98312 | tf_op jit(solution)/shard_map/ppermute | solution.py:319
  57.6 19.5 %collective-permute-start.18 = (bf16[128,2048]{1,0:T(8,128)(2,1)S(1)}, bf16[128,2048]{1,0:T(8,128)(2,1)S(1)}, u32[]{:S(2)}, u32[]{:S(2)}) collective-permute-start(bf16[128,2048]{1,0:T(8,128)(2,1)S(1)} %collective-permute-done.4.refs_7_), channel_id=1, source_target_pairs={{0,8},{1,9},{2,10},{3,11},{4,12},{5,13},{6,14},{7,15},{8,0},{9,1},... | collective-permute-start | bytes 1572872 | tf_op jit(solution)/shard_map/ppermute | solution.py:319
  64.7 12.5 %collective-permute-start.15 = (bf16[128,2048]{1,0:T(8,128)(2,1)S(1)}, bf16[128,2048]{1,0:T(8,128)(2,1)S(1)}, u32[]{:S(2)}, u32[]{:S(2)}) collective-permute-start(bf16[128,2048]{1,0:T(8,128)(2,1)S(1)} %collective-permute-done.1.refs_4_), channel_id=1, source_target_pairs={{0,1},{1,0},{2,6},{3,7},{4,5},{5,4},{6,2},{7,3},{8,9},{9,8},{10,14... | collective-permute-start | bytes 1572872 | tf_op jit(solution)/shard_map/ppermute | solution.py:319
  65.3 11.9 %collective-permute-start.19 = (bf16[128,2048]{1,0:T(8,128)(2,1)S(1)}, bf16[128,2048]{1,0:T(8,128)(2,1)S(1)}, u32[]{:S(2)}, u32[]{:S(2)}) collective-permute-start(bf16[128,2048]{1,0:T(8,128)(2,1)S(1)} %collective-permute-done.13.refs_6_), channel_id=1, source_target_pairs={{0,4},{1,5},{2,3},{3,2},{4,0},{5,1},{6,7},{7,6},{8,12},{9,13},{10,... | collective-permute-start | bytes 1572872 | tf_op jit(solution)/shard_map/ppermute | solution.py:319
  67.2 10.0 %collective-permute-start.16 = (bf16[96,2048]{1,0:T(8,128)(2,1)S(1)}, bf16[96,2048]{1,0:T(8,128)(2,1)S(1)}, u32[]{:S(2)}, u32[]{:S(2)}) collective-permute-start(bf16[96,2048]{1,0:T(8,128)(2,1)S(1)} %slice.6), channel_id=1, source_target_pairs={{0,8},{1,9},{2,10},{3,11},{4,12},{5,13},{6,14},{7,15},{8,0},{9,1},... | collective-permute-start | bytes 1179656 | tf_op jit(solution)/shard_map/ppermute | solution.py:319
  67.3 9.8 %collective-permute-start.17 = (bf16[32,2048]{1,0:T(8,128)(2,1)S(1)}, bf16[32,2048]{1,0:T(8,128)(2,1)S(1)}, u32[]{:S(2)}, u32[]{:S(2)}) collective-permute-start(bf16[32,2048]{1,0:T(8,128)(2,1)S(1)} %slice.7), channel_id=1, source_target_pairs={{0,4},{1,5},{2,3},{3,2},{4,0},{5,1},{6,7},{7,6},{8,12},{9,13},{10,... | collective-permute-start | bytes 393224 | tf_op jit(solution)/shard_map/ppermute | solution.py:319
  79.4 2.8 %collective-permute-start.20 = (bf16[256,2176]{1,0:T(8,128)(2,1)S(1)}, bf16[256,2176]{1,0:T(8,128)(2,1)S(1)}, u32[]{:S(2)}, u32[]{:S(2)}) collective-permute-start(bf16[256,2176]{1,0:T(8,128)(2,1)S(1)} %get-tuple-element.87), channel_id=1, source_target_pairs={{0,2},{1,3},{2,0},{3,1},{4,6},{5,7},{6,4},{7,5},{8,10},{9,11},{10,... | collective-permute-start | bytes 3342344 | tf_op jit(solution)/shard_map/ppermute | solution.py:467
